TPU v7x, 32 devices: a whole 2x2x4 slice. The times are simulated.
32 devices in a mesh: items: 32 (over z, y, x, core).
Axes of the slice: x: 2, y: 2, z: 4, core: 2. Of those that a mesh axis runs over, the one named last changes fastest.
Arguments:
- frames_in: float32 [32, 1024, 512], P('items'), may hold values from -6 to 6
- conditioning: float32 [32, 1024, 512], P('items'), may hold values from -6 to 6
- prompt: float32 [32, 896, 512], P(None, 'items'), may hold values from -6 to 6
- item_lengths: int32 [32], P('items'), may hold values from 128 to 1024, as said below
- prompt_lengths: int32 [32], replicated, may hold values from 89 to 896, as said below
- key_mask: int32 [32, 896], P(None, 'items'), may hold values 0 or 1
- diffusion_steps: int32 [32], P('items'), may hold values from 0 to 999
- step_proj: float32 [2, 512, 512], P(None, 'items'), may hold values from -0.25 to 0.25
- conv_weight: float32 [2, 1536, 1024], P(None, 'items'), may hold values from -0.15625 to 0.15625
- cond_proj: float32 [2, 512, 1024], P(None, 'items'), may hold values from -0.25 to 0.25
- out_proj: float32 [2, 512, 1024], P(None, 'items'), may hold values from -0.25 to 0.25
- query_seeds: float32 [2, 512, 32], P(None, 'items'), may hold values from -6 to 6
- query_proj: float32 [2, 512, 512], P(None, 'items'), may hold values from -0.25 to 0.25
- key_proj: float32 [2, 512, 512], P(None, 'items'), may hold values from -0.25 to 0.25
- value_proj: float32 [2, 512, 512], P(None, 'items'), may hold values from -0.25 to 0.25
- mixing_proj: float32 [2, 512, 512], P(None, 'items'), may hold values from -1 to 1
- film_proj: float32 [2, 512, 1024], P(None, 'items'), may hold values from -2 to 2
- cot_frames: float32 [32, 1024, 512], P('items'), may hold values from -6 to 6
- cot_skip: float32 [32, 1024, 512], P('items'), may hold values from -6 to 6
Outputs:
- frames_out: float32 [32, 1024, 512], P('items')
- skip_out: float32 [32, 1024, 512], P('items')
- grad_frames: float32 [32, 1024, 512], P('items')
- grad_step_proj: float32 [2, 512, 512], P(None, 'items')
- grad_conv_weight: float32 [2, 1536, 1024], P(None, 'items')
- grad_cond_proj: float32 [2, 512, 1024], P(None, 'items')
- grad_out_proj: float32 [2, 512, 1024], P(None, 'items')
- grad_query_seeds: float32 [2, 512, 32], P(None, 'items')
- grad_query_proj: float32 [2, 512, 512], P(None, 'items')
- grad_key_proj: float32 [2, 512, 512], P(None, 'items')
- grad_value_proj: float32 [2, 512, 512], P(None, 'items')
- grad_mixing_proj: float32 [2, 512, 512], P(None, 'items')
- grad_film_proj: float32 [2, 512, 1024], P(None, 'items')
Inputs may be any that keep to these rules, and one draw needn't show every extreme that they name: `item_lengths`: some item has exactly 1024 live frames and another exactly 128. `prompt_lengths`: some item has exactly 896 prompt frames and another exactly 89.
All inputs are finite; a program needn't handle non-finite values. No bound on the sum of `key_mask` on one device may be relied on, other than what follows from the above.
Results may differ from a plain program's by a relative error of at most 0.0003.
Values sent between devices are 32-bit elements; how exact they have to be, the bound alone decides.
No kernel may reach another device: no remote copies, remote signals or barrier semaphores. Data moves between devices by JAX's collectives and lax.ppermute only.
A program may use at most 256 MiB of HBM per device.

v0:
```python
from functools import partial
import math

import jax
import jax.numpy as jnp
from jax import lax
from jax.sharding import PartitionSpec as P

WIDTH = 512
HEADS = 8
LAYERS = 2


CLIP_NORM = 1.0
HIGH = lax.Precision.HIGHEST


def matmul(left, right):
    return jnp.dot(left, right, precision=HIGH)


def step_embedding(diffusion_step):
    half_width = WIDTH // 2
    ramp = jnp.arange(half_width, dtype=jnp.int32).astype(jnp.float32) / (half_width - 1)
    angles = diffusion_step.astype(jnp.float32) / 1000.0 * jnp.exp(ramp * math.log(100.0))
    return jnp.concatenate([jnp.sin(angles), jnp.cos(angles)])


def frame_layer(
    frames, skip_sum, conditioning, frame_live, step_embed, film_params, weights, dilation
):
    step_proj, conv_weight, cond_proj, out_proj = weights
    frame_count = frames.shape[0]
    hidden_in = (frames + matmul(step_embed[None, :], step_proj)) * frame_live[:, None]
    zero_rim = jnp.zeros((dilation, WIDTH), hidden_in.dtype)
    padded = jnp.concatenate([zero_rim, hidden_in, zero_rim], axis=0)
    conv_taps = jnp.concatenate([padded[:frame_count], hidden_in, padded[2 * dilation :]], axis=1)
    pre_gate = matmul(conv_taps, conv_weight) + matmul(conditioning, cond_proj)
    gate_act = jnp.tanh(pre_gate[:, :WIDTH]) * jax.nn.sigmoid(pre_gate[:, WIDTH:])
    modulated = gate_act * (1.0 + film_params[:WIDTH]) + film_params[WIDTH:]
    post_gate = matmul(modulated, out_proj)
    frames_next = (frames + post_gate[:, :WIDTH]) * frame_live[:, None] * math.sqrt(0.5)
    skip_next = skip_sum + post_gate[:, WIDTH:] * frame_live[:, None]
    return (frames_next, skip_next)


def film_of(attended, mixing_proj, film_proj):
    mixed_rows = jnp.einsum("bqw,wx->bqx", attended, mixing_proj, precision=HIGH)
    return jnp.einsum("bw,wx->bx", jnp.mean(mixed_rows, axis=1), film_proj, precision=HIGH)


def project_rows(query_seeds, query_proj, key_proj, value_proj, prompt_local):
    head_dim = WIDTH // HEADS
    item_count, key_count = (prompt_local.shape[0], prompt_local.shape[1])
    query_rows = matmul(query_seeds.T, query_proj).reshape(-1, HEADS, head_dim)
    key_rows = jnp.einsum("bkw,wx->bkx", prompt_local, key_proj, precision=HIGH).reshape(
        item_count, key_count, HEADS, head_dim
    )
    value_rows = jnp.einsum("bkw,wx->bkx", prompt_local, value_proj, precision=HIGH).reshape(
        item_count, key_count, HEADS, head_dim
    )
    return (query_rows, key_rows, value_rows)


def masked_scores(query_rows, key_rows, key_live):
    head_dim = WIDTH // HEADS
    scores = jnp.einsum("qhe,bkhe->bhqk", query_rows, key_rows, precision=HIGH) / math.sqrt(
        head_dim
    )
    return jnp.where(key_live[:, None, None, :], scores, -1e30)


def on_device(
    frames_in,
    conditioning,
    prompt,
    item_lengths,
    prompt_lengths,
    key_mask,
    diffusion_steps,
    step_proj,
    conv_weight,
    cond_proj,
    out_proj,
    query_seeds,
    query_proj,
    key_proj,
    value_proj,
    mixing_proj,
    film_proj,
    cot_frames,
    cot_skip,
):
    gathered = (
        lax.all_gather(step_proj, "items", axis=1, tiled=True),
        lax.all_gather(conv_weight, "items", axis=1, tiled=True),
        lax.all_gather(cond_proj, "items", axis=1, tiled=True),
        lax.all_gather(out_proj, "items", axis=1, tiled=True),
        lax.all_gather(query_seeds, "items", axis=1, tiled=True),
        lax.all_gather(query_proj, "items", axis=1, tiled=True),
        lax.all_gather(key_proj, "items", axis=1, tiled=True),
        lax.all_gather(value_proj, "items", axis=1, tiled=True),
        lax.all_gather(mixing_proj, "items", axis=1, tiled=True),
        lax.all_gather(film_proj, "items", axis=1, tiled=True),
    )
    own_count = frames_in.shape[0]
    own_start = lax.axis_index("items") * own_count
    key_count = prompt.shape[1]
    head_dim = WIDTH // HEADS
    frame_live = (
        jnp.arange(frames_in.shape[1], dtype=jnp.int32)[None, :] < item_lengths[:, None]
    ).astype(jnp.float32)
    key_place = (
        lax.axis_index("items") * key_count + jnp.arange(key_count, dtype=jnp.int32)[None, :]
    )
    key_live = (key_place < prompt_lengths[:, None]) & ((key_mask == 1) | (key_place == 0))
    embeds = jax.vmap(step_embedding)(diffusion_steps)
    member_count = len(gathered)
    frames = frames_in
    skip_sum = jnp.zeros_like(frames_in)
    kept = []
    for layer_index in range(LAYERS):
        layer_params = tuple((member[layer_index] for member in gathered))
        query_rows, key_rows, value_rows = project_rows(
            layer_params[4], layer_params[5], layer_params[6], layer_params[7], prompt
        )
        scores = masked_scores(query_rows, key_rows, key_live)
        top_score = lax.pmax(jnp.max(scores, axis=3), "items")
        exp_scores = jnp.exp(scores - top_score[..., None])
        part_sum = jnp.sum(exp_scores, axis=3)
        part_acc = jnp.einsum("bhqk,bkhe->bqhe", exp_scores, value_rows, precision=HIGH).reshape(
            exp_scores.shape[0], -1, WIDTH
        )
        acc_own, sum_own = (
            lax.psum_scatter(part_acc, "items", scatter_dimension=0, tiled=True),
            lax.psum_scatter(part_sum, "items", scatter_dimension=0, tiled=True),
        )
        sum_rows = jnp.transpose(sum_own, (0, 2, 1))[..., None]
        attended = (acc_own.reshape(own_count, -1, HEADS, head_dim) / sum_rows).reshape(
            own_count, -1, WIDTH
        )
        top_own = lax.dynamic_slice_in_dim(top_score, own_start, own_count, 0)
        log_total = top_own + jnp.log(sum_own)
        film_params, film_pull = jax.vjp(film_of, attended, layer_params[8], layer_params[9])
        mapped = jax.vmap(
            partial(frame_layer, dilation=2**layer_index), in_axes=(0, 0, 0, 0, 0, 0, None)
        )

        def local_layer(frames_now, skip_now, film_now, weights_now, mapped=mapped):
            return mapped(
                frames_now, skip_now, conditioning, frame_live, embeds, film_now, weights_now
            )

        (frames, skip_sum), frame_pull = jax.vjp(
            local_layer, frames, skip_sum, film_params, layer_params[:4]
        )
        kept.append((frame_pull, film_pull, attended, log_total))
    grad_frames = cot_frames
    grad_skip = cot_skip
    layer_grads = [None] * LAYERS
    for layer_index in reversed(range(LAYERS)):
        frame_pull, film_pull, attended, log_total = kept[layer_index]
        layer_params = tuple((member[layer_index] for member in gathered))
        grad_frames, grad_skip, grad_film, grad_four = frame_pull((grad_frames, grad_skip))
        grad_att, grad_mixing, grad_filmw = film_pull(grad_film)
        row_terms = jnp.sum((grad_att * attended).reshape(own_count, -1, HEADS, head_dim), axis=3)
        row_terms = jnp.transpose(row_terms, (0, 2, 1))
        all_att, all_terms, all_log = (
            lax.all_gather(grad_att, "items", axis=0, tiled=True),
            lax.all_gather(row_terms, "items", axis=0, tiled=True),
            lax.all_gather(log_total, "items", axis=0, tiled=True),
        )
        query_rows, key_rows, value_rows = project_rows(
            layer_params[4], layer_params[5], layer_params[6], layer_params[7], prompt
        )
        scores = masked_scores(query_rows, key_rows, key_live)
        attn_probs = jnp.exp(scores - all_log[..., None])
        att_heads = all_att.reshape(all_att.shape[0], -1, HEADS, head_dim)
        grad_probs = jnp.einsum("bqhe,bkhe->bhqk", att_heads, value_rows, precision=HIGH)
        grad_values = jnp.einsum("bhqk,bqhe->bkhe", attn_probs, att_heads, precision=HIGH).reshape(
            prompt.shape[0], key_count, WIDTH
        )
        grad_scores = attn_probs * (grad_probs - all_terms[..., None]) / math.sqrt(head_dim)
        grad_queries = jnp.einsum("bhqk,bkhe->qhe", grad_scores, key_rows, precision=HIGH).reshape(
            -1, WIDTH
        )
        grad_keys = jnp.einsum("bhqk,qhe->bkhe", grad_scores, query_rows, precision=HIGH).reshape(
            prompt.shape[0], key_count, WIDTH
        )
        grad_keyw = jnp.einsum("bkw,bkx->wx", prompt, grad_keys, precision=HIGH)
        grad_valuew = jnp.einsum("bkw,bkx->wx", prompt, grad_values, precision=HIGH)
        grad_queryw = matmul(layer_params[4], grad_queries)
        grad_seeds = matmul(layer_params[5], grad_queries.T)
        grad_params = (
            grad_four[0],
            grad_four[1],
            grad_four[2],
            grad_four[3],
            grad_seeds,
            grad_queryw,
            grad_keyw,
            grad_valuew,
            grad_mixing,
            grad_filmw,
        )
        layer_grads[layer_index] = grad_params
    stacked = tuple(
        (
            jnp.stack([layer_grads[layer_index][member] for layer_index in range(LAYERS)])
            for member in range(member_count)
        )
    )
    shards = lax.psum_scatter(stacked, "items", scatter_dimension=1, tiled=True)
    local_square = sum((jnp.sum(member * member) for member in shards))
    norm_square = lax.psum(local_square, "items")
    clip_factor = jnp.minimum(1.0, CLIP_NORM / jnp.sqrt(norm_square))
    return (
        frames,
        skip_sum,
        grad_frames,
        shards[0] * clip_factor,
        shards[1] * clip_factor,
        shards[2] * clip_factor,
        shards[3] * clip_factor,
        shards[4] * clip_factor,
        shards[5] * clip_factor,
        shards[6] * clip_factor,
        shards[7] * clip_factor,
        shards[8] * clip_factor,
        shards[9] * clip_factor,
    )


def solution(mesh):
    return jax.shard_map(
        on_device,
        mesh=mesh,
        in_specs=(
            P("items", None, None),
            P("items", None, None),
            P(None, "items", None),
            P("items"),
            P(),
            P(None, "items"),
            P("items"),
            P(None, "items", None),
            P(None, "items", None),
            P(None, "items", None),
            P(None, "items", None),
            P(None, "items", None),
            P(None, "items", None),
            P(None, "items", None),
            P(None, "items", None),
            P(None, "items", None),
            P(None, "items", None),
            P("items", None, None),
            P("items", None, None),
        ),
        out_specs=(
            P("items", None, None),
            P("items", None, None),
            P("items", None, None),
            P(None, "items", None),
            P(None, "items", None),
            P(None, "items", None),
            P(None, "items", None),
            P(None, "items", None),
            P(None, "items", None),
            P(None, "items", None),
            P(None, "items", None),
            P(None, "items", None),
            P(None, "items", None),
        ),
        check_vma=False,
    )
```

profile of v0, /device:TPU:0, one launch (start us, length us, event | category | flops | bytes accessed | tf_op | source)
XLA Modules:
  0.0 2333.7 jit_solution(4513425705704990657)
XLA Ops:
  10.4 44.8 %all_gather.53 = f32[2,512,32]{2,0,1:T(2,128)S(1)} all-gather(f32[2,16,32]{2,0,1:T(2,128)S(1)} %copy.259), channel_id=1, replica_groups=mesh['items'=32] {'items'}, dimensions={1}, use_global_device_ids=true | all-gather | bytes 135168 | tf_op jit(solution)/shard_map/all_gather | solution.py:99
  56.3 14.2 all-gather.24.cloned.1.call-done
  74.5 54.4 %all-gather.22.cloned.1.call-done = f32[2,512,512]{2,1,0:T(8,128)} async-done(((f32[2,16,512]{2,1,0:T(8,128)}), f32[2,512,512]{2,1,0:T(8,128)}) %all-gather.22.cloned.1.call-update) | async-done | bytes 2097168 | tf_op jit(solution)/shard_map/all_gather | solution.py:101
  138.6 7.8 fusion.107
  146.4 6.6 fusion.109
  160.5 6.4 bitcast_reduce_fusion.1
  169.6 123.3 %all-reduce.41.cloned.1.call-done = (f32[32,8,32]{2,1,0:T(8,128)}, f32[32,8,32]{2,1,0:T(8,128)}) async-done(((f32[32,8,32]{2,1,0:T(8,128)}, f32[32,8,32]{2,1,0:T(8,128)}), (f32[32,8,32]{2,1,0:T(8,128)}, f32[32,8,32]{2,1,0:T(8,128)})) %all-reduce.41.cloned.1.call-update) | async-done | bytes 65552 | tf_op jit(solution)/shard_map/pmax | solution.py:128
  294.8 6.1 fusion.205
  303.2 48.0 %all-gather.20.cloned.1.call-done = f32[2,512,512]{2,1,0:T(8,128)} async-done(((f32[2,16,512]{2,1,0:T(8,128)}), f32[2,512,512]{2,1,0:T(8,128)}) %all-gather.20.cloned.1.call-update) | async-done | bytes 2097168 | tf_op jit(solution)/shard_map/all_gather | solution.py:102
  355.8 9.2 fusion.72
  365.0 10.0 fusion.54
  375.1 5.8 copy.267
  387.5 9.2 fusion.70
  396.7 10.0 fusion.57
  406.8 5.8 copy.279
  432.0 108.3 %all-reduce.37.cloned.1.call-done = (f32[32,8,32]{2,1,0:T(8,128)}, f32[32,8,32]{2,1,0:T(8,128)}) async-done(((f32[32,8,32]{2,1,0:T(8,128)}, f32[32,8,32]{2,1,0:T(8,128)}), (f32[32,8,32]{2,1,0:T(8,128)}, f32[32,8,32]{2,1,0:T(8,128)})) %all-reduce.37.cloned.1.call-update) | async-done | bytes 65552
  542.3 56.4 %all-gather.26.cloned.1.call-done = f32[2,512,512]{2,1,0:T(8,128)} async-done(((f32[2,16,512]{2,1,0:T(8,128)}), f32[2,512,512]{2,1,0:T(8,128)}) %all-gather.26.cloned.1.call-update) | async-done | bytes 2097168 | tf_op jit(solution)/shard_map/all_gather | solution.py:103
  598.7 138.1 %reduce-scatter.4.cloned.1.call-done = f32[1,32,512]{2,1,0:T(8,128)} async-done(((f32[32,32,512]{2,1,0:T(8,128)}), f32[1,32,512]{2,1,0:T(8,128)}) %reduce-scatter.4.cloned.1.call-update) | async-done | bytes 65552 | tf_op jit(solution)/shard_map/reduce_scatter | solution.py:135
  738.8 133.3 %reduce-scatter.6.cloned.1.call-done = f32[1,32,512]{2,1,0:T(8,128)} async-done(((f32[32,32,512]{2,1,0:T(8,128)}), f32[1,32,512]{2,1,0:T(8,128)}) %reduce-scatter.6.cloned.1.call-update) | async-done | bytes 65552 | tf_op jit(solution)/shard_map/reduce_scatter | solution.py:135
  874.1 58.7 %all-gather.28.cloned.1.call-done = f32[2,512,1024]{2,1,0:T(8,128)} async-done(((f32[2,16,1024]{2,1,0:T(8,128)}), f32[2,512,1024]{2,1,0:T(8,128)}) %all-gather.28.cloned.1.call-update) | async-done | bytes 4194320 | tf_op jit(solution)/shard_map/all_gather | solution.py:104
  938.3 92.0 %all-gather.16.cloned.1.call-done = f32[2,1536,1024]{2,1,0:T(8,128)} async-done(((f32[2,48,1024]{2,1,0:T(8,128)}), f32[2,1536,1024]{2,1,0:T(8,128)}) %all-gather.16.cloned.1.call-update) | async-done | bytes 12582928 | tf_op jit(solution)/shard_map/all_gather | solution.py:96
  1030.3 26.2 %fusion.1 = f32[1024,1024]{1,0:T(8,128)} fusion(f32[2,1536,1024]{2,1,0:T(8,128)} %all-gather.16.cloned.1.call-done, f32[1,1024,512]{2,1,0:T(8,128)} %get-tuple-element.120, f32[1,1024,512]{2,1,0:T(8,128)} %copy-done.20, f32[1,1024,512]{2,1,0:T(8,128)} %get-tuple-element.119), kind=kOutput, calls=%fused_computation.6 | convolution fusion | flops 19330498560 | bytes 16777216 | tf_op jit(solution)/shard_map/jvp(vmap())/dot_general | solution.py:19
  1056.5 36.7 %all-gather.18.cloned.1.call-done = f32[2,512,1024]{2,1,0:T(8,128)} async-done(((f32[2,16,1024]{2,1,0:T(8,128)}), f32[2,512,1024]{2,1,0:T(8,128)}) %all-gather.18.cloned.1.call-update) | async-done | bytes 4194320 | tf_op jit(solution)/shard_map/all_gather | solution.py:97
  1093.3 10.2 add_bitcast_fusion.1
  1103.4 53.2 %all-gather.30.cloned.1.call-done = f32[2,512,1024]{2,1,0:T(8,128)} async-done(((f32[2,16,1024]{2,1,0:T(8,128)}), f32[2,512,1024]{2,1,0:T(8,128)}) %all-gather.30.cloned.1.call-update) | async-done | bytes 4194320 | tf_op jit(solution)/shard_map/all_gather | solution.py:98
  1156.7 10.3 convolution_bitcast_fusion.1
  1172.3 20.7 fusion.3
  1193.0 7.3 add_bitcast_fusion
  1200.3 12.7 fusion.74
  1213.1 20.2 fusion.8
  1238.0 10.0 fusion.75
  1255.3 39.5 %all_gather.58 = f32[32,8,32]{2,1,0:T(8,128)S(1)} all-gather(f32[1,8,32]{2,1,0:T(8,128)S(1)} %get-tuple-element.129), channel_id=1, replica_groups=mesh['items'=32] {'items'}, dimensions={0}, use_global_device_ids=true | all-gather | bytes 33792 | tf_op jit(solution)/shard_map/all_gather | solution.py:171
  1294.8 37.0 %all_gather.61 = f32[32,8,32]{2,1,0:T(8,128)S(1)} all-gather(f32[1,8,32]{2,1,0:T(8,128)S(1)} %get-tuple-element.131), channel_id=1, replica_groups=mesh['items'=32] {'items'}, dimensions={0}, use_global_device_ids=true | all-gather | bytes 33792 | tf_op jit(solution)/shard_map/all_gather | solution.py:171
  1339.6 35.4 %fusion.9 = f32[1,1024,1536]{2,1,0:T(8,128)S(1)} fusion(f32[2,1536,1024]{2,1,0:T(8,128)} %all-gather.16.cloned.1.call-done, f32[1,1024,512]{2,1,0:T(8,128)} %get-tuple-element.108, f32[1,1024,512]{2,1,0:T(8,128)} %get-tuple-element.107), kind=kOutput, calls=%fused_computation.16 | convolution fusion | flops 19328401408 | bytes 16777216 | tf_op jit(solution)/shard_map/transpose(jvp(vmap()))/dot_general | solution.py:19
  1380.3 8.0 fusion.121
  1388.3 8.3 fusion.126
  1396.7 9.9 convolution_bitcast_fusion
  1416.8 7.4 copy.283
  1424.2 10.1 fusion.111
  1434.3 7.1 fusion.116
  1441.8 5.2 copy.284
  1447.3 38.3 %all_gather.60 = f32[32,8,32]{2,1,0:T(8,128)S(1)} all-gather(f32[1,8,32]{2,1,0:T(8,128)S(1)} %copy.288), channel_id=1, replica_groups=mesh['items'=32] {'items'}, dimensions={0}, use_global_device_ids=true | all-gather | bytes 33792 | tf_op jit(solution)/shard_map/all_gather | solution.py:170
  1486.5 37.4 %all_gather.63 = f32[32,8,32]{2,1,0:T(8,128)S(1)} all-gather(f32[1,8,32]{2,1,0:T(8,128)S(1)} %copy.296), channel_id=1, replica_groups=mesh['items'=32] {'items'}, dimensions={0}, use_global_device_ids=true | all-gather | bytes 33792 | tf_op jit(solution)/shard_map/all_gather | solution.py:170
  1536.4 5.9 pad_maximum_fusion.3
  1546.7 12.6 fusion.32
  1559.3 6.2 copy.290
  1570.0 12.6 fusion.29
  1582.6 6.2 copy.298
  1588.9 9.2 multiply_multiply_fusion.1
  1598.1 6.0 fusion.136
  1604.1 5.1 convolution_bitcast_fusion.2
  1609.2 6.1 fusion.133
  1628.8 7.1 copy.304
  1640.4 5.1 convolution_bitcast_fusion.8
  1645.5 5.1 copy.303
  1666.0 9.2 fusion.65
  1683.7 5.1 convolution_bitcast_fusion.6
  1688.9 8.1 fusion.60
  1713.4 24.9 %fusion.7 = f32[1,1536,1024]{2,1,0:T(8,128)} fusion(f32[1,1024,512]{2,1,0:T(8,128)} %copy-done.47, f32[1,1024,512]{2,1,0:T(8,128)} %copy-done.28, f32[1,1024,512]{2,1,0:T(8,128)} %copy-done.46, f32[1,1024,512]{2,1,0:T(8,128)} %copy-done.86, f32[1,1024,512]{2,1,0:T(8,128)} %copy-done.84), kind=kOutput, calls=%fused_computation.14 | convolution fusion | flops 19331547136 | bytes 16777216 | tf_op jit(solution)/shard_map/transpose(jvp(vmap()))/dot_general | solution.py:19
  1738.3 23.1 fusion.6
  1761.4 12.1 pad_maximum_fusion
  1773.6 324.8 %all-reduce.39.cloned.1.call-done = (f32[2,512,512]{2,0,1:T(2,128)}, f32[2,512,1024]{2,0,1:T(2,128)}, f32[2,512,1024]{2,0,1:T(2,128)}, f32[2,512,32]{2,0,1:T(2,1...) async-done(((f32[2,512,512]{2,0,1:T(2,128)}, ...) | async-done | bytes 23199760
  2112.3 147.3 %reduce-scatter.8.cloned.1.call-done = f32[2,48,1024]{2,1,0:T(8,128)} async-done(((f32[2,1536,1024]{2,1,0:T(8,128)}), f32[2,48,1024]{2,1,0:T(8,128)}) %reduce-scatter.8.cloned.1.call-update) | async-done | bytes 393232 | tf_op jit(solution)/shard_map/reduce_scatter | solution.py:213
  2272.0 39.7 %psum.7 = f32[]{:T(128)} all-reduce(f32[]{:T(128)S(6)} %add.230), channel_id=1, replica_groups=mesh['items'=32] {'items'}, use_global_device_ids=true, to_apply=%region_40.41 | all-reduce | flops 1 | bytes 8 | tf_op jit(solution)/shard_map/psum | solution.py:215
  (379 shorter events, 228.3 us)
Async XLA Ops:
  7.2 1086.1 %copy-start = (f32[1,1024,512]{2,1,0:T(8,128)S(1)}, f32[1,1024,512]{2,1,0:T(8,128)}, u32[]{:S(2)}) copy-start(f32[1,1024,512]{2,1,0:T(8,128)} %param.20) | copy-start | bytes 6291460
  7.2 63.3 %all-gather.24.cloned.1.call-start = ((), (), s32[]{:S(2)}) async-start(), calls=%async_computation.8 | async-start | bytes 2162688 | tf_op jit(solution)/shard_map/all_gather | solution.py:100
  7.9 121.0 %all-gather.22.cloned.1.call-start = ((), (), s32[]{:S(2)}) async-start(), calls=%async_computation.7 | async-start | bytes 2162688 | tf_op jit(solution)/shard_map/all_gather | solution.py:101
  8.7 284.2 %all-reduce.41.cloned.1.call-start = ((), (), s32[]{:S(2)}) async-start(), calls=%async_computation.19 | async-start | bytes 524288 | tf_op jit(solution)/shard_map/pmax | solution.py:128
  9.7 285.1 %copy-start.67 = (pred[32,28]{0,1:T(8,128)(4,1)}, pred[32,28]{0,1:T(8,128)(4,1)S(1)}, u32[]{:S(2)}) copy-start(pred[32,28]{0,1:T(8,128)(4,1)S(1)} %copy.257) | copy-start | bytes 2692
  56.3 102.4 %copy-start.40 = (f32[1,512,32]{2,0,1:T(1,128)}, f32[1,512,32]{2,0,1:T(1,128)S(1)}, u32[]{:S(2)}) copy-start(f32[1,512,32]{2,0,1:T(1,128)S(1)} %get-tuple-element.128) | copy-start | bytes 196612
  138.6 7.8 copy-start.6
  138.6 7.8 copy-start.35
  146.4 8.6 copy-start.8
  158.7 8.3 copy-start.2
  168.4 182.8 %all-gather.20.cloned.1.call-start = ((), (), s32[]{:S(2)}) async-start(), calls=%async_computation.6 | async-start | bytes 2162688 | tf_op jit(solution)/shard_map/all_gather | solution.py:102
  169.0 255.6 %all-gather.14.cloned.1.call-start = ((), (), s32[]{:S(2)}) async-start(), calls=%async_computation.3 | async-start | bytes 2162688 | tf_op jit(solution)/shard_map/all_gather | solution.py:95
  169.6 370.7 %all-reduce.37.cloned.1.call-start = ((), (), s32[]{:S(2)}) async-start(), calls=%async_computation.17 | async-start | bytes 524288
  302.4 296.3 %all-gather.26.cloned.1.call-start = ((), (), s32[]{:S(2)}) async-start(), calls=%async_computation.10 | async-start | bytes 2162688 | tf_op jit(solution)/shard_map/all_gather | solution.py:103
  303.1 433.7 %reduce-scatter.4.cloned.1.call-start = ((), (), s32[]{:S(2)}) async-start(), calls=%async_computation.9 | async-start | bytes 2162688 | tf_op jit(solution)/shard_map/reduce_scatter | solution.py:135
  355.8 9.3 copy-start.15
  365.0 10.0 copy-start.3
  385.7 486.5 %reduce-scatter.6.cloned.1.call-start = ((), (), s32[]{:S(2)}) async-start(), calls=%async_computation.13 | async-start | bytes 2162688 | tf_op jit(solution)/shard_map/reduce_scatter | solution.py:135
  387.5 9.3 copy-start.14
  396.7 10.0 copy-start.4
  417.4 515.5 %all-gather.28.cloned.1.call-start = ((), (), s32[]{:S(2)}) async-start(), calls=%async_computation.11 | async-start | bytes 4325376 | tf_op jit(solution)/shard_map/all_gather | solution.py:104
  417.9 612.4 %all-gather.16.cloned.1.call-start = ((), (), s32[]{:S(2)}) async-start(), calls=%async_computation.4 | async-start | bytes 12976128 | tf_op jit(solution)/shard_map/all_gather | solution.py:96
  418.7 674.6 %all-gather.18.cloned.1.call-start = ((), (), s32[]{:S(2)}) async-start(), calls=%async_computation.5 | async-start | bytes 4325376 | tf_op jit(solution)/shard_map/all_gather | solution.py:97
  419.3 737.4 %all-gather.30.cloned.1.call-start = ((), (), s32[]{:S(2)}) async-start(), calls=%async_computation.12 | async-start | bytes 4325376 | tf_op jit(solution)/shard_map/all_gather | solution.py:98
  420.0 1122.3 %all-gather.32.cloned.1.call-start = ((), (), s32[]{:S(2)}) async-start(), calls=%async_computation.15 | async-start | bytes 2162688 | tf_op jit(solution)/shard_map/all_gather | solution.py:169
  935.6 221.1 %copy-start.79 = (f32[1,512]{1,0:T(1,128)}, f32[1,512]{1,0:T(1,128)S(1)}, u32[]{:S(2)}) copy-start(f32[1,512]{1,0:T(1,128)S(1)} %get-tuple-element.140) | copy-start | bytes 6148
  935.6 300.1 %copy-start.77 = (f32[1,512]{1,0:T(1,128)}, f32[1,512]{1,0:T(1,128)S(1)}, u32[]{:S(2)}) copy-start(f32[1,512]{1,0:T(1,128)S(1)} %get-tuple-element.139) | copy-start | bytes 6148
  938.3 458.4 %copy-start.81 = (f32[1,512]{1,0:T(1,128)}, f32[1,512]{1,0:T(1,128)S(1)}, u32[]{:S(2)}) copy-start(f32[1,512]{1,0:T(1,128)S(1)} %get-tuple-element.141) | copy-start | bytes 6148
  938.3 458.4 %copy-start.82 = (f32[1,512]{1,0:T(1,128)}, f32[1,512]{1,0:T(1,128)S(1)}, u32[]{:S(2)}) copy-start(f32[1,512]{1,0:T(1,128)S(1)} %get-tuple-element.142) | copy-start | bytes 6148
  1156.7 10.4 copy-start.12
  1156.7 10.4 copy-start.50
  1156.7 15.2 slice-start
  1156.7 15.2 slice-start.1
  1169.1 66.5 %copy-start.51 = (f32[1,1024,512]{2,1,0:T(8,128)}, f32[1,1024,512]{2,1,0:T(8,128)S(1)}, u32[]{:S(2)}) copy-start(f32[1,1024,512]{2,1,0:T(8,128)S(1)} %get-tuple-element.137) | copy-start | bytes 6291460
  1172.3 20.7 copy-start.39
  1200.3 12.7 copy-start.34
  1213.1 20.2 copy-start.84
  1213.1 20.2 copy-start.86
  1213.1 121.3 %copy-start.73 = (f32[512]{0:T(512)}, f32[512]{0:T(512)S(1)}, u32[]{:S(2)}) copy-start(f32[512]{0:T(512)S(1)} %get-tuple-element.112) | copy-start | bytes 6148
  1238.0 10.0 copy-start.26
  1255.2 310.3 %all-gather.34.cloned.1.call-start = ((), (), s32[]{:S(2)}) async-start(), calls=%async_computation.16 | async-start | bytes 2162688 | tf_op jit(solution)/shard_map/all_gather | solution.py:169
  1334.3 40.7 %copy-start.71 = (f32[512]{0:T(512)}, f32[512]{0:T(512)S(1)}, u32[]{:S(2)}) copy-start(f32[512]{0:T(512)S(1)} %reduce_sum.232) | copy-start | bytes 6148
  1380.3 8.0 copy-start.88
  1380.3 8.0 copy-start.90
  1396.6 701.8 %all-reduce.39.cloned.1.call-start = ((), (), s32[]{:S(2)}) async-start(), calls=%async_computation.18 | async-start | bytes 47185920
  1396.7 10.0 copy-start.13
  1396.7 10.0 copy-start.19
  1396.7 10.0 copy-start.29
  1396.7 10.0 copy-start.30
  1424.2 10.1 copy-start.27
  1424.2 10.1 copy-start.33
  1424.2 10.1 copy-start.52
  1424.2 10.1 copy-start.78
  1424.2 10.1 copy-start.80
  1441.8 44.5 %copy-start.66 = (f32[32,512]{1,0:T(8,128)S(1)}, f32[32,512]{1,0:T(8,128)}, u32[]{:S(2)}) copy-start(f32[32,512]{1,0:T(8,128)} %get-tuple-element.152) | copy-start | bytes 196612
  1588.9 9.3 copy-start.9
  1713.3 25.0 %copy-start.21 = (f32[1,1024,512]{2,1,0:T(8,128)S(1)}, f32[1,1024,512]{2,1,0:T(8,128)}, u32[]{:S(2)}) copy-start(f32[1,1024,512]{2,1,0:T(8,128)} %copy-done.20) | copy-start | bytes 6291460
  1713.3 546.3 %reduce-scatter.8.cloned.1.call-start = ((), (), s32[]{:S(2)}) async-start(), calls=%async_computation.14 | async-start | bytes 12976128 | tf_op jit(solution)/shard_map/reduce_scatter | solution.py:213
  1713.4 24.9 %copy-start.44 = (f32[1,1024,512]{2,1,0:T(8,128)S(1)}, f32[1,1024,512]{2,1,0:T(8,128)}, u32[]{:S(2)}) copy-start(f32[1,1024,512]{2,1,0:T(8,128)} %get-tuple-element.119) | copy-start | bytes 6291460
  1713.4 24.9 %copy-start.45 = (f32[1,1024,512]{2,1,0:T(8,128)S(1)}, f32[1,1024,512]{2,1,0:T(8,128)}, u32[]{:S(2)}) copy-start(f32[1,1024,512]{2,1,0:T(8,128)} %get-tuple-element.120) | copy-start | bytes 6291460
  1713.4 24.9 %copy-start.89 = (f32[1,1024,512]{2,1,0:T(8,128)S(1)}, f32[1,1024,512]{2,1,0:T(8,128)}, u32[]{:S(2)}) copy-start(f32[1,1024,512]{2,1,0:T(8,128)} %get-tuple-element.107) | copy-start | bytes 6291460
  1713.4 24.9 %copy-start.91 = (f32[1,1024,512]{2,1,0:T(8,128)S(1)}, f32[1,1024,512]{2,1,0:T(8,128)}, u32[]{:S(2)}) copy-start(f32[1,1024,512]{2,1,0:T(8,128)} %get-tuple-element.108) | copy-start | bytes 6291460
  2267.8 59.2 %copy-start.1 = (f32[1,1024,512]{2,1,0:T(8,128)S(1)}, f32[1,1024,512]{2,1,0:T(8,128)}, u32[]{:S(2)}) copy-start(f32[1,1024,512]{2,1,0:T(8,128)} %param.20) | copy-start | bytes 6291460
  2272.0 54.3 %copy-start.55 = (f32[2,48,1024]{2,1,0:T(8,128)S(1)}, f32[2,48,1024]{2,1,0:T(8,128)}, u32[]{:S(2)}) copy-start(f32[2,48,1024]{2,1,0:T(8,128)} %reduce-scatter.8.cloned.1.call-done) | copy-start | bytes 1179652
  (48 other events, 209.5 us)
Sparse Core Ops, SparseCore 0:
  10.9 59.5 all-gather.23
  73.4 55.4 all-gather.21
  168.5 124.3 all-reduce.40
  295.7 55.4 all-gather.19
  353.9 55.4 all-gather.13
  416.1 124.1 all-reduce.36
  543.2 55.4 all-gather.25
  601.5 135.2 reduce-scatter.3
  739.8 132.3 reduce-scatter.5
  874.9 57.9 all-gather.27
  935.7 94.5 all-gather.15
  1033.1 60.1 all-gather.17
  1096.2 60.4 all-gather.29
  1255.3 55.1 all-gather.31
  1396.8 53.8 all-gather.33
  1713.4 384.9 all-reduce.38
  2104.3 155.2 reduce-scatter.7
where the time goes:
time: 2350 us; the launch traced here: 2330 us
  waiting for transfers between devices  1390 us (59%)
  matrix products  424 us (18%)
  blocking collectives  237 us (10%)
  local copies, waits for them, and re-layouts  165 us (7%)
  other arithmetic  87.5 us (4%)
  between operations  24.3 us (1%)
    unnamed x19, waiting for transfers between devices  439 us
    reduce_scatter x2, waiting for transfers between devices, on_device(): lax.psum_scatter(part_acc, 'items', scatter_dimension=0, tiled=True)  271 us
    dot_general x24, matrix products, matmul(): return jnp.dot(left, right, precision=HIGH)  255 us
    reduce_scatter x1, waiting for transfers between devices, on_device(): shards = lax.psum_scatter(stacked, 'items', scatter_dimension=1, tiled=True)  147 us
    pmax x1, waiting for transfers between devices, on_device(): top_score = lax.pmax(jnp.max(scores, axis=3), 'items')  123 us
    all_gather x1, waiting for transfers between devices, on_device(): lax.all_gather(conv_weight, 'items', axis=1, tiled=True)  92 us
    all_gather x2, blocking collectives, on_device(): lax.all_gather(log_total, 'items', axis=0, tiled=True)  76.5 us
    all_gather x2, blocking collectives, on_device(): lax.all_gather(row_terms, 'items', axis=0, tiled=True)  75.7 us
  transfers between devices with their start and end apart: 17, of which 14 were waited for; matrix products, arithmetic and copies ran while one was open for 16% of the time, Pallas kernels for 0%

commit v1 on v0

v1 whole, which is shorter than its diff:
```python
import math

import jax
import jax.numpy as jnp
from jax import lax
from jax.sharding import PartitionSpec as P

WIDTH = 512
GATES = 2 * WIDTH
HEADS = 8
HEAD_DIM = WIDTH // HEADS
QUERIES = 32
LAYERS = 2
CLIP_NORM = 1.0
AXIS = "items"
HIGH = lax.Precision.HIGH
HIGHEST = lax.Precision.HIGHEST
ROOT_HALF = math.sqrt(0.5)


def big_dot(left, right, left_dim=1, right_dim=0):
    return lax.dot_general(left, right, (((left_dim,), (right_dim,)), ((), ())), precision=HIGH)


def small_dot(left, right, left_dim=1, right_dim=0):
    return lax.dot_general(left, right, (((left_dim,), (right_dim,)), ((), ())), precision=HIGHEST)


def step_embedding(diffusion_step):
    half_width = WIDTH // 2
    ramp = jnp.arange(half_width, dtype=jnp.int32).astype(jnp.float32) / (half_width - 1)
    angles = diffusion_step.astype(jnp.float32) / 1000.0 * jnp.exp(ramp * math.log(100.0))
    return jnp.concatenate([jnp.sin(angles), jnp.cos(angles)])


class Ring:
    def __init__(self, count, size, stride):
        self.count, self.size, self.stride = count, size, stride
        self.digit = (lax.axis_index(AXIS) // stride) % size

    def shift(self, block, steps):
        perm = []
        for device in range(self.count):
            digit = (device // self.stride) % self.size
            target = (digit + steps) % self.size
            perm.append((device, device + (target - digit) * self.stride))
        return lax.ppermute(block, AXIS, perm)

    def gather(self, block):
        if self.size == 1:
            return block[None]
        others = [self.shift(block, steps) for steps in range(1, self.size)]
        if self.size == 2:
            first = jnp.where(self.digit == 0, block, others[0])
            second = jnp.where(self.digit == 0, others[0], block)
            return jnp.stack([first, second])
        out = jnp.broadcast_to(block, (self.size,) + block.shape)
        for steps, other in enumerate(others, 1):
            place = (self.digit - steps) % self.size
            out = lax.dynamic_update_index_in_dim(out, other, place, 0)
        return out

    def scatter_sum(self, blocks, dim):
        own = lax.dynamic_index_in_dim(blocks, self.digit, dim, keepdims=False)
        for steps in range(1, self.size):
            place = (self.digit + steps) % self.size
            own = own + self.shift(lax.dynamic_index_in_dim(blocks, place, dim, keepdims=False), steps)
        return own


def rings_of(count):
    bits = (count // 2).bit_length() - 1
    sizes = [2 ** ((bits + 2) // 3), 2 ** ((bits + 1) // 3), 2 ** (bits // 3), 2]
    rings, stride = [], count
    for size in sizes:
        stride //= size
        rings.append(Ring(count, size, stride))
    return rings


def gather_rows(shard, rings):
    far, mid, near, core = rings
    rows, columns = shard.shape
    half = rows // 2
    block = far.gather(shard)
    top = mid.gather(near.gather(block[:, :half]))
    low = near.gather(mid.gather(block[:, half:]))
    top = jnp.transpose(top, (2, 0, 1, 3, 4))
    low = jnp.transpose(low, (2, 1, 0, 3, 4))
    rail = jnp.concatenate([top, low], axis=3)
    both = core.gather(rail)
    return jnp.transpose(both, (1, 2, 3, 0, 4, 5)).reshape(-1, rows, columns)


def pick(terms, place, dim):
    return [lax.dynamic_index_in_dim(term, place, dim, keepdims=False) for term in terms]


def hop(terms, ring, dim):
    stays = pick(terms, ring.digit, dim)
    for steps in range(1, ring.size):
        goes = sum(pick(terms, (ring.digit + steps) % ring.size, dim))
        stays.append(ring.shift(goes, steps))
    return stays


class RowSum:
    def __init__(self, arrays, rings):
        self.rings = rings
        sizes = tuple(ring.size for ring in rings)
        self.state = [[array.reshape(sizes + array.shape[1:])] for array in arrays]

    def core(self):
        self.state = [hop(terms, self.rings[3], 3) for terms in self.state]

    def join(self):
        rows = [jnp.concatenate(parts, axis=3) for parts in zip(*self.state)]
        half = rows[0].shape[3] // 2
        self.state = [[term[:, :, :, :half] for term in rows], [term[:, :, :, half:] for term in rows]]

    def first(self):
        far, mid, near, core = self.rings
        top, low = self.state
        self.state = [hop(top, mid, 1), hop(low, near, 2)]

    def second(self):
        far, mid, near, core = self.rings
        top, low = self.state
        top, low = sum(hop(top, near, 1)), sum(hop(low, mid, 1))
        self.state = [[jnp.concatenate([top, low], axis=1)]]

    def last(self):
        self.state = sum(hop(self.state[0], self.rings[0], 0))


def tie(*groups):
    leaves, tree = jax.tree.flatten(groups)
    return jax.tree.unflatten(tree, lax.optimization_barrier(leaves))


def exchange(*parts):
    devices = parts[0].shape[0]
    parts = [part.reshape(devices, -1) for part in parts]
    sizes = [part.shape[1] for part in parts]
    joined = jnp.concatenate(parts, axis=1)
    joined = jnp.pad(joined, ((0, 0), (0, -joined.shape[1] % 1024))).reshape(devices, -1, 128)
    came = lax.all_to_all(joined, AXIS, split_axis=0, concat_axis=0, tiled=True).reshape(devices, -1)
    out, start = [], 0
    for size in sizes:
        out.append(came[:, start : start + size])
        start += size
    return out


def to_all(part, devices):
    return jnp.broadcast_to(part.reshape(1, -1), (devices, part.size))


def by_column(part, devices):
    cut = part.reshape(part.shape[:-1] + (devices, -1))
    return jnp.moveaxis(cut, -2, 0).reshape(devices, -1)


def head_rows(row):
    head = jnp.arange(WIDTH, dtype=jnp.int32)[None, :] // HEAD_DIM
    own = head == jnp.arange(HEADS, dtype=jnp.int32)[:, None]
    return jnp.where(own, row, 0.0)


def attention_back(weights, keys, probs, grad_film):
    grad_mixed = small_dot(grad_film, weights["film"], 1, 1)
    grad_row = small_dot(grad_mixed / QUERIES, weights["mixing"], 1, 1)
    grad_pooled = small_dot(head_rows(grad_row), weights["value"], 1, 1)
    grad_probs = small_dot(grad_pooled, keys, 1, 1)
    weighted = probs * grad_probs[:, None, :]
    row_terms = jnp.sum(weighted, axis=2, keepdims=True)
    grad_scores = (weighted - probs * row_terms) / math.sqrt(HEAD_DIM)
    grad_scores = grad_scores.reshape(HEADS * QUERIES, -1)
    grad_absorbed = small_dot(keys, grad_scores, 0, 1)
    key_heads = weights["key"].reshape(WIDTH, HEADS, HEAD_DIM)
    grad_query = jnp.einsum(
        "whq,whe->qhe", grad_absorbed.reshape(WIDTH, HEADS, QUERIES), key_heads, precision=HIGHEST
    ).reshape(QUERIES, WIDTH)
    return grad_absorbed, grad_query, grad_row, grad_mixed


def shifted(rows, steps):
    if steps > 0:
        return jnp.concatenate([jnp.zeros_like(rows[:steps]), rows[:-steps]], axis=0)
    return jnp.concatenate([rows[-steps:], jnp.zeros_like(rows[:-steps])], axis=0)


def taps_of(frames, step_row, live, dilation):
    hidden = (frames + step_row) * live
    return jnp.concatenate([shifted(hidden, dilation), hidden, shifted(hidden, -dilation)], axis=1)


def layer_gates(weights, taps, conditioning):
    pre_gate = big_dot(taps, weights["conv"]) + big_dot(conditioning, weights["cond"])
    return jnp.tanh(pre_gate[:, :WIDTH]), jax.nn.sigmoid(pre_gate[:, WIDTH:])


def layer_forward(weights, frames, skip, tanh, sig, live, film):
    modulated = tanh * sig * (1.0 + film[:, :WIDTH]) + film[:, WIDTH:]
    post = big_dot(modulated, weights["out"])
    frames = (frames + post[:, :WIDTH]) * (live * ROOT_HALF)
    skip = skip + post[:, WIDTH:] * live
    return frames, skip, modulated


def layer_back_gates(weights, tanh, sig, modulated, grad_frames, grad_skip, live, film):
    grad_post = jnp.concatenate([grad_frames * (live * ROOT_HALF), grad_skip * live], axis=1)
    grad_mod = big_dot(grad_post, weights["out"], 1, 1)
    grad_gamma = jnp.sum(grad_mod * (tanh * sig), axis=0, keepdims=True)
    grad_beta = jnp.sum(grad_mod, axis=0, keepdims=True)
    grad_gate = grad_mod * (1.0 + film[:, :WIDTH])
    grad_pre = jnp.concatenate(
        [grad_gate * sig * (1.0 - tanh * tanh), grad_gate * tanh * sig * (1.0 - sig)], axis=1
    )
    return grad_post, grad_pre, jnp.concatenate([grad_gamma, grad_beta], axis=1)


def layer_back_frames(weights, grad_pre, grad_frames, live, dilation):
    grad_taps = big_dot(grad_pre, weights["conv"], 1, 1)
    grad_hidden = (
        shifted(grad_taps[:, :WIDTH], -dilation)
        + grad_taps[:, WIDTH : 2 * WIDTH]
        + shifted(grad_taps[:, 2 * WIDTH :], dilation)
    ) * live
    return grad_frames * (live * ROOT_HALF) + grad_hidden, jnp.sum(grad_hidden, axis=0, keepdims=True)


def on_device(
    frames_in,
    conditioning,
    prompt,
    item_lengths,
    prompt_lengths,
    key_mask,
    diffusion_steps,
    step_proj,
    conv_weight,
    cond_proj,
    out_proj,
    query_seeds,
    query_proj,
    key_proj,
    value_proj,
    mixing_proj,
    film_proj,
    cot_frames,
    cot_skip,
    devices,
):
    rings = rings_of(devices)
    share = step_proj.shape[1]
    key_count = prompt.shape[1]
    extra_rows = -(-(key_count + LAYERS * share * QUERIES) // WIDTH)
    key_rows = -(-(key_count + extra_rows) // 8) * 8
    me = lax.axis_index(AXIS)

    frame_packs = [
        jnp.concatenate(
            [conv_weight[layer], cond_proj[layer], out_proj[layer], step_proj[layer].reshape(-1, GATES)], axis=0
        )
        for layer in range(LAYERS)
    ]
    frame_whole_0 = lax.all_gather(frame_packs[0], AXIS, axis=0, tiled=False)

    extra = jnp.concatenate(
        [key_mask.astype(jnp.float32), to_all(query_seeds, prompt.shape[0])], axis=1
    )
    extra = jnp.pad(extra, ((0, 0), (0, (key_rows - key_count) * WIDTH - extra.shape[1])))
    sent = jnp.concatenate([prompt, extra.reshape(prompt.shape[0], -1, WIDTH)], axis=1)
    query_key = jnp.concatenate([query_proj, key_proj], axis=2).reshape(LAYERS * share, GATES)
    query_key, sent = tie(query_key, sent)
    keys = lax.all_to_all(sent, AXIS, split_axis=0, concat_axis=0, tiled=True)
    extra = keys[:, key_count : key_count + extra_rows].reshape(devices, -1)
    key_place = (
        jnp.arange(devices, dtype=jnp.int32)[:, None] * key_count
        + jnp.arange(key_rows, dtype=jnp.int32)[None, :]
    )
    masked_in = jnp.pad(extra[:, :key_count], ((0, 0), (0, key_rows - key_count)))
    live_keys = (
        (jnp.arange(key_rows, dtype=jnp.int32)[None, :] < key_count)
        & (key_place < lax.dynamic_index_in_dim(prompt_lengths, me, 0, keepdims=False))
        & ((masked_in == 1.0) | (key_place == 0))
    ).reshape(-1)
    seeds = extra[:, key_count : key_count + LAYERS * share * QUERIES]
    seeds = jnp.moveaxis(seeds.reshape(devices, LAYERS, share, QUERIES), 1, 0)
    seeds = seeds.reshape(LAYERS, WIDTH, QUERIES)
    keys = keys.reshape(-1, WIDTH)

    query_key = gather_rows(query_key, rings).reshape(devices, LAYERS, share, GATES)
    query_key = jnp.moveaxis(query_key, 1, 0).reshape(LAYERS, WIDTH, GATES)
    query_rows = jnp.einsum("lwq,lwx->lqx", seeds, query_key[:, :, :WIDTH], precision=HIGHEST)
    query_heads = query_rows.reshape(LAYERS, QUERIES, HEADS, HEAD_DIM)
    key_heads = query_key[:, :, WIDTH:].reshape(LAYERS, WIDTH, HEADS, HEAD_DIM)
    absorbed = jnp.einsum("lqhe,lwhe->lhqw", query_heads, key_heads, precision=HIGHEST)
    absorbed = absorbed.reshape(LAYERS * HEADS * QUERIES, WIDTH) / math.sqrt(HEAD_DIM)

    scores = jnp.where(live_keys[None, :], small_dot(absorbed, keys, 1, 1), -1e30)
    exps = jnp.exp(scores - jnp.max(scores, axis=1, keepdims=True))
    probs = exps / jnp.sum(exps, axis=1, keepdims=True)
    probs = probs.reshape(LAYERS, HEADS, QUERIES, -1)
    pooled = jnp.mean(probs, axis=2).reshape(LAYERS * HEADS, -1)
    pooled_keys = small_dot(pooled, keys)

    frame_pack_1, frame_whole_0, pooled_keys = tie(frame_packs[1], frame_whole_0, pooled_keys)
    frame_whole_1 = lax.all_gather(frame_pack_1, AXIS, axis=0, tiled=False)

    (pooled_cut,) = exchange(by_column(pooled_keys, devices))
    pooled_cut = pooled_cut.reshape(devices, LAYERS, HEADS, share)
    value_heads = value_proj.reshape(LAYERS, share, HEADS, HEAD_DIM)
    mean_part = jnp.einsum("blhw,lwhe->blhe", pooled_cut, value_heads, precision=HIGHEST)
    (mean_cut,) = exchange(by_column(mean_part.reshape(devices, LAYERS, WIDTH), devices))
    mean_cut = jnp.sum(mean_cut, axis=0).reshape(devices, LAYERS, share)
    mixed_part = jnp.einsum("blw,lwx->blx", mean_cut, mixing_proj, precision=HIGHEST)
    (mixed_cut,) = exchange(by_column(mixed_part, devices))
    mixed_cut = jnp.sum(mixed_cut, axis=0).reshape(devices, LAYERS, share)
    film_part = jnp.einsum("blw,lwx->blx", mixed_cut, film_proj, precision=HIGHEST)
    (films,) = exchange(film_part)
    films = jnp.sum(films, axis=0).reshape(LAYERS, 1, GATES)

    attention_pack = jnp.concatenate(
        [
            part
            for layer in range(LAYERS)
            for part in (film_proj[layer], jnp.concatenate([value_proj[layer], mixing_proj[layer]], axis=1))
        ],
        axis=0,
    )
    attention_pack, frame_whole_1 = tie(attention_pack, frame_whole_1)
    weights = []
    for whole in (frame_whole_0, frame_whole_1):
        weights.append(
            {
                "conv": whole[:, : 3 * share].reshape(-1, GATES),
                "cond": whole[:, 3 * share : 4 * share].reshape(-1, GATES),
                "out": whole[:, 4 * share : 5 * share].reshape(-1, GATES),
                "step": whole[:, 5 * share :].reshape(-1, WIDTH),
            }
        )
    attention_whole = lax.all_gather(attention_pack, AXIS, axis=0, tiled=False)
    attention_whole = attention_whole.reshape(devices, LAYERS, -1, GATES)
    for layer in range(LAYERS):
        value_mixing = attention_whole[:, layer, share:]
        weights[layer]["film"] = attention_whole[:, layer, :share].reshape(-1, GATES)
        weights[layer]["value"] = value_mixing[:, :, :WIDTH].reshape(-1, WIDTH)
        weights[layer]["mixing"] = value_mixing[:, :, WIDTH:].reshape(-1, WIDTH)
        weights[layer]["key"] = query_key[layer, :, WIDTH:]

    live = (jnp.arange(frames_in.shape[1], dtype=jnp.int32) < item_lengths[0]).astype(jnp.float32)[:, None]
    embed = step_embedding(diffusion_steps[0])[None, :]
    frames, skip = frames_in[0], jnp.zeros_like(frames_in[0])
    kept = []
    for layer in range(LAYERS):
        step_row = small_dot(embed, weights[layer]["step"])
        taps = taps_of(frames, step_row, live, 2**layer)
        tanh, sig = layer_gates(weights[layer], taps, conditioning[0])
        frames, skip, modulated = layer_forward(weights[layer], frames, skip, tanh, sig, live, films[layer])
        kept.append((taps, tanh, sig, modulated))

    def by_device(grad):
        return grad.reshape(devices, -1, GATES)

    taps, tanh, sig, modulated = kept[1]
    grad_post, grad_pre_1, grad_film_1 = layer_back_gates(
        weights[1], tanh, sig, modulated, cot_frames[0], cot_skip[0], live, films[1]
    )
    grad_out = big_dot(modulated, grad_post, 0, 0)
    grad_cond = big_dot(conditioning[0], grad_pre_1, 0, 0)
    grad_conv = big_dot(taps, grad_pre_1, 0, 0)
    sum_1 = RowSum([by_device(grad_conv), by_device(grad_cond), by_device(grad_out)], rings)
    sum_1.core()
    grad_frames, step_sum_1 = layer_back_frames(weights[1], grad_pre_1, cot_frames[0], live, 2)
    sum_1.join()
    sum_1.first()

    taps, tanh, sig, modulated = kept[0]
    grad_post, grad_pre_0, grad_film_0 = layer_back_gates(
        weights[0], tanh, sig, modulated, grad_frames, cot_skip[0], live, films[0]
    )
    absorbed_1, query_1, row_1, mixed_1 = attention_back(weights[1], keys, probs[1], grad_film_1)
    grad_out = big_dot(modulated, grad_post, 0, 0)
    grad_cond = big_dot(conditioning[0], grad_pre_0, 0, 0)
    absorbed_0, query_0, row_0, mixed_0 = attention_back(weights[0], keys, probs[0], grad_film_0)
    absorbed_0, absorbed_1, taps, sum_1.state = tie(absorbed_0, absorbed_1, taps, sum_1.state)
    sum_1.second()
    grad_conv = big_dot(taps, grad_pre_0, 0, 0)
    sum_1.last()
    absorbed_grad = jnp.concatenate([absorbed_0, absorbed_1], axis=1)
    sum_0 = RowSum([by_device(grad) for grad in (grad_conv, grad_cond, grad_out, absorbed_grad)], rings)
    sum_0.core()
    sum_0.join()
    sum_0.first()
    grad_frames, step_sum_0 = layer_back_frames(weights[0], grad_pre_0, grad_frames, live, 1)
    sum_0.second()
    (query_cut,) = exchange(by_column(jnp.stack([query_0, query_1]), devices))
    query_cut = jnp.sum(query_cut, axis=0)
    sum_0.last()
    whole_rows = (row_0, row_1, mixed_0, mixed_1, grad_film_0, grad_film_1, step_sum_0, step_sum_1, query_cut)
    row_0, row_1, mixed_0, mixed_1, grad_film_0, grad_film_1, step_sum_0, step_sum_1, query_cuts, own_embeds = exchange(
        *(to_all(part, devices) for part in whole_rows), by_column(embed, devices)
    )
    query_grads = jnp.moveaxis(query_cuts.reshape(devices, LAYERS, QUERIES, share), 0, 2)
    query_grads = query_grads.reshape(LAYERS, QUERIES, WIDTH)
    absorbed_sums = jnp.moveaxis(sum_0.state[5 * share :].reshape(share, LAYERS, HEADS, QUERIES), 1, 0)

    frame_sums = [sum_0.state, sum_1.state]
    conv_grad = jnp.stack([sums[: 3 * share] for sums in frame_sums])
    cond_grad = jnp.stack([sums[3 * share : 4 * share] for sums in frame_sums])
    out_grad = jnp.stack([sums[4 * share : 5 * share] for sums in frame_sums])
    step_grad = jnp.einsum("bw,lbx->lwx", own_embeds, jnp.stack([step_sum_0, step_sum_1]), precision=HIGHEST)
    seeds_grad = jnp.einsum("lwx,lqx->lwq", query_proj, query_grads, precision=HIGHEST)
    query_grad = jnp.einsum("lwq,lqx->lwx", query_seeds, query_grads, precision=HIGHEST)
    key_grad = jnp.einsum("lwhq,lqhe->lwhe", absorbed_sums, query_heads, precision=HIGHEST)
    rows = jnp.stack([row_0, row_1]).reshape(LAYERS, devices, HEADS, HEAD_DIM)
    value_grad = QUERIES * jnp.einsum("blhw,lbhe->lwhe", pooled_cut, rows, precision=HIGHEST)
    mixing_grad = jnp.einsum("blw,lbx->lwx", mean_cut, jnp.stack([mixed_0, mixed_1]), precision=HIGHEST)
    film_grad = jnp.einsum(
        "blw,lbx->lwx", mixed_cut, jnp.stack([grad_film_0, grad_film_1]), precision=HIGHEST
    )
    grads = (
        step_grad,
        conv_grad,
        cond_grad,
        out_grad,
        seeds_grad,
        query_grad,
        key_grad.reshape(LAYERS, share, WIDTH),
        value_grad.reshape(LAYERS, share, WIDTH),
        mixing_grad,
        film_grad,
    )
    local_square = sum(jnp.sum(grad * grad) for grad in grads)
    squares = lax.all_to_all(
        jnp.full((devices, 8, 128), local_square), AXIS, split_axis=0, concat_axis=0, tiled=True
    )
    norm_square = jnp.sum(squares[:, 0, 0])
    clip_factor = jnp.minimum(1.0, CLIP_NORM / jnp.sqrt(norm_square))
    return (frames[None], skip[None], grad_frames[None]) + tuple(grad * clip_factor for grad in grads)


def solution(mesh):
    devices = mesh.shape[AXIS]

    def run(*args):
        return on_device(*args, devices=devices)

    items, rows = P(AXIS, None, None), P(None, AXIS, None)
    return jax.shard_map(
        run,
        mesh=mesh,
        in_specs=(items, items, rows, P(AXIS), P(), P(None, AXIS), P(AXIS)) + (rows,) * 10 + (items, items),
        out_specs=(items,) * 3 + (rows,) * 10,
        check_vma=False,
    )
```

time: 2350 us -> 727 us (0.31)
  waiting for transfers between devices: 1390 us -> 157 us
  blocking collectives: 237 us -> 0 us
  matrix products: 424 us -> 218 us
  starting transfers between devices: 0.85 us -> 74.9 us
    unnamed x19 -> x3, waiting for transfers between devices: 439 us -> 0.69 us
    reduce_scatter x3 -> x0, waiting for transfers between devices: 419 us -> none  [the longest x2 271 us: on_device(): lax.psum_scatter(part_acc, 'items', scatter_dimension=0, tiled=True)]
    all_gather x11 -> x3, waiting for transfers between devices: 414 us -> 0.02 us  [the longest x1 0.02 us: on_device(): frame_whole_1 = lax.all_gather(frame_pack_1, AXIS, axis=0, tiled=False)]
    dot_general x54 -> x44, matrix products: 424 us -> 218 us  [the longest x16 160 us: big_dot(): lax.dot_general(left, right, (((left_dim,), (right_dim,)), ((), ())), pre...]
    all_gather x5 -> x0, blocking collectives: 197 us -> none  [the longest x2 76.5 us: on_device(): lax.all_gather(log_total, 'items', axis=0, tiled=True)]
    pmax x1 -> x0, waiting for transfers between devices: 123 us -> none  [on_device(): top_score = lax.pmax(jnp.max(scores, axis=3), 'items')]
    ppermute x0 -> x29, waiting for transfers between devices: none -> 121 us  [shift(): return lax.ppermute(block, AXIS, perm)]
    ppermute x0 -> x29, starting transfers between devices: none -> 41.1 us  [shift(): return lax.ppermute(block, AXIS, perm)]
  transfers between devices with their start and end apart: 17 -> 40, of which waited for: 14 -> 17; matrix products, arithmetic and copies ran while one was open for 16% -> 60% of each run, Pallas kernels for 0% -> 0%
where the time goes in v1:
time: 727 us; the launch traced here: 720 us
  matrix products  218 us (30%)
  local copies, waits for them, and re-layouts  164 us (23%)
  waiting for transfers between devices  157 us (22%)
  other arithmetic  82.5 us (11%)
  starting transfers between devices  74.9 us (10%)
  between operations  24.4 us (3%)
    dot_general x16, matrix products, big_dot(): lax.dot_general(left, right, (((left_dim,), (right_dim,)), ((), ())), pre...  160 us
    ppermute x29, waiting for transfers between devices, shift(): return lax.ppermute(block, AXIS, perm)  121 us
    unnamed x198, local copies, waits for them, and re-layouts  45.4 us
    ppermute x29, starting transfers between devices, shift(): return lax.ppermute(block, AXIS, perm)  41.1 us
    dot_general x14, matrix products, small_dot(): lax.dot_general(left, right, (((left_dim,), (right_dim,)), ((), ())), pre...  34.5 us
    all_to_all x6, starting transfers between devices, exchange(): lax.all_to_all(joined, AXIS, split_axis=0, concat_axis=0, tiled=True)  23.4 us
    all_to_all x1, waiting for transfers between devices, on_device(): keys = lax.all_to_all(sent, AXIS, split_axis=0, concat_axis=0, tiled=True)  21.5 us
  transfers between devices with their start and end apart: 40, of which 17 were waited for; matrix products, arithmetic and copies ran while one was open for 60% of the time, Pallas kernels for 0%

profile of v1, /device:TPU:0, one launch (start us, length us, event | category | flops | bytes accessed | tf_op | source)
XLA Modules:
  0.0 720.3 jit_solution(9681675855813238576)
XLA Ops:
  15.7 3.0 collective-permute-start
  25.2 9.0 %collective-permute-done.1 = f32[32,1024]{1,0:T(8,128)S(1)} collective-permute-done((f32[32,1024]{1,0:T(8,128)S(1)}, f32[32,1024]{1,0:T(8,128)S(1)}, u32[]{:S(2)}, u32[]{:S(2)}) %collective-permute-start.1) | collective-permute-done | bytes 131104 | tf_op jit(solution)/shard_map/ppermute | solution.py:47
  37.8 7.7 %all-to-all-start = ((f32[32,32,512]{2,1,0:T(8,128)}), f32[32,32,512]{2,1,0:T(8,128)}, u32[]{:S(2)}, u32[]{:S(2)}) async-start(f32[32,32,512]{2,1,0:T(8,128)} %pad_maximum_fusion.25), calls=%async_computation | async-start | bytes 4194304 | tf_op jit(solution)/shard_map/all_to_all | solution.py:277
  50.2 39.2 %collective-permute-done.6 = f32[2,4,16,1024]{3,2,0,1:T(8,128)S(1)} collective-permute-done((f32[2,4,16,1024]{3,2,0,1:T(8,128)S(1)}, f32[2,4,16,1024]{3,2,0,1:T(8,128)S(1)}, u32[]{:S(2)}, u32[]{:S(2)}) %collective-permute-start.6) | collective-permute-done | bytes 524320 | tf_op jit(solution)/shard_map/ppermute | solution.py:47
  92.8 3.1 collective-permute-done.7
  102.9 3.0 copy.353
  106.0 21.5 %all-to-all-done = f32[32,32,512]{2,1,0:T(8,128)} async-done(((f32[32,32,512]{2,1,0:T(8,128)}), f32[32,32,512]{2,1,0:T(8,128)}, u32[]{:S(2)}, u32[]{:S(2)}) %all-to-all-start) | async-done | bytes 2097184 | tf_op jit(solution)/shard_map/all_to_all | solution.py:277
  129.7 2.9 fusion.26
  132.7 2.9 convolution_multiply_fusion
  135.6 5.5 select_reduce_fusion
  143.7 3.3 fusion.125
  148.0 2.9 copy.372
  152.1 2.9 copy.344
  155.0 3.2 copy.373
  167.0 6.6 slice.313
  180.2 3.3 all-to-all-start.1
  191.8 13.6 %fusion.188 = f32[1024,1024]{1,0:T(8,128)} fusion(f32[1536,1024]{1,0:T(8,128)S(1)} %bitcast.518, f32[1023,512]{0,1:T(8,128)S(1)} %get-tuple-element.194, f32[1023,512]{0,1:T(8,128)S(1)} %get-tuple-element.193, f32[1024,512]{0,1:T(8,128)S(1)} %fusion.32), kind=kOutput, calls=%fused_computation.402 | convolution fusion | flops 9673113600 | bytes 16773120 | tf_op jit(solution)/shard_map/dot_general | solution.py:22
  208.5 6.2 all-to-all-start.2
  214.7 5.2 select_maximum_fusion.2
  219.9 5.4 all-to-all-done.2
  228.0 3.8 all-to-all-start.3
  231.7 5.0 fusion.199
  236.8 4.5 all-to-all-done.3
  243.6 2.8 all-to-all-start.4
  247.2 7.3 %bitcast_add_fusion.1 = f32[1024,1024]{1,0:T(8,128)} fusion(f32[1024,1024]{1,0:T(8,128)} %fusion.188, f32[512,1024]{1,0:T(8,128)} %bitcast.512, f32[1,1024,512]{2,1,0:T(8,128)S(1)} %copy-done), kind=kOutput, calls=%fused_computation.12 | convolution fusion | flops 3222274048 | bytes 12582912 | tf_op jit(solution)/shard_map/dot_general | solution.py:22
  257.1 8.8 %fusion.33 = f32[1024,1024]{0,1:T(8,128)} fusion(f32[512,1024]{1,0:T(8,128)} %bitcast.555, f32[512]{0:T(512)S(1)} %bitcast.606, f32[512]{0:T(512)S(1)} %bitcast.603, f32[1024,1024]{1,0:T(8,128)} %bitcast_add_fusion.1), kind=kOutput, calls=%fused_computation.108 | convolution fusion | flops 3224371200 | bytes 10489856 | tf_op jit(solution)/shard_map/dot_general | solution.py:22
  265.9 3.2 slice.332
  272.2 4.2 fusion.198
  277.7 3.8 bitcast_multiply_fusion.1
  282.8 16.9 %fusion.5 = f32[1024,1024]{1,0:T(8,128)} fusion(f32[1536,1024]{1,0:T(8,128)} %bitcast.522, f32[1022,512]{0,1:T(8,128)S(1)} %get-tuple-element.192, f32[1022,512]{0,1:T(8,128)S(1)} %get-tuple-element.191, f32[1024,512]{0,1:T(8,128)S(1)} %get-tuple-element.241), kind=kOutput, calls=%fused_computation.28 | convolution fusion | flops 9673113600 | bytes 16769024 | tf_op jit(solution)/shard_map/dot_general | solution.py:22
  299.7 5.9 bitcast_add_fusion
  305.6 9.4 %multiply_reduce_fusion = (f32[512]{0:T(512)S(1)}, f32[512]{0:T(512)S(1)}, f32[1024,512]{1,0:T(8,128)}, f32[1024,512]{1,0:T(8,128)}) fusion(f32[1024,1024]{1,0:T(8,128)S(1)} %bitcast_add_fusion, f32[512]{0:T(512)S(1)} %bitcast.608, f32[512,1024]{1,0:T(8,128)S(1)} %bitcast.557, f32[1024,512]{0,1:T(8,128)S(1)} %get-tuple-element.242, ...), kind=kOutput, calls=%fused_computation.85 | convolution fusion | flops 3230661632 | bytes 14686208 | tf_op jit(solution)/shard_map/dot_general | solution.py:22
  315.1 15.2 %fusion.10 = f32[1024,1536]{0,1:T(8,128)S(1)} fusion(f32[1536,1024]{1,0:T(8,128)S(1)} %bitcast.525, f32[1024,512]{1,0:T(8,128)} %get-tuple-element.140, f32[1024,512]{1,0:T(8,128)} %get-tuple-element.141), kind=kOutput, calls=%fused_computation.33 | convolution fusion | flops 9664724992 | bytes 16777216 | tf_op jit(solution)/shard_map/dot_general | solution.py:22
  332.7 5.9 fusion.34
  338.7 6.0 fusion.16
  344.7 2.9 copy.442
  347.6 3.0 copy.443
  350.6 10.3 %fusion = f32[512,1024]{1,0:T(8,128)S(1)} fusion(f32[1024,512]{0,1:T(8,128)} %copy-done.33, f32[1024,512]{0,1:T(8,128)} %get-tuple-element.240, f32[512]{0:T(512)S(1)} %bitcast.612, f32[512]{0:T(512)S(1)} %bitcast.610, f32[1024,1024]{1,0:T(8,128)} %copy-done.29), kind=kOutput, calls=%fused_computation.13 | convolution fusion | flops 3225419776 | bytes 10489856 | tf_op jit(solution)/shard_map/dot_general | solution.py:22
  363.1 3.5 fusion.9
  368.8 15.2 %fusion.4 = f32[1536,1024]{1,0:T(8,128)S(1)} fusion(f32[1022,512]{0,1:T(8,128)S(1)} %copy-done.42, f32[1022,512]{0,1:T(8,128)S(1)} %copy-done.40, f32[1024,512]{0,1:T(8,128)S(1)} %copy-done.7, f32[1024,512]{1,0:T(8,128)} %get-tuple-element.140, f32[1024,512]{1,0:T(8,128)} %get-tuple-element.141), kind=kOutput, calls=%fused_computation.27 | convolution fusion | flops 9674162176 | bytes 16769024 | tf_op jit(solution)/shard_map/dot_general | solution.py:22
  391.5 7.1 fusion.2
  402.2 9.5 %multiply_reduce_fusion.1 = (f32[512]{0:T(512)S(1)}, f32[512]{0:T(512)S(1)}, f32[1024,512]{1,0:T(8,128)}, f32[1024,512]{1,0:T(8,128)}) fusion(f32[1024,1024]{1,0:T(8,128)S(1)} %copy-done.28, f32[512]{0:T(512)S(1)} %bitcast.605, f32[512,1024]{1,0:T(8,128)S(1)} %bitcast.556, f32[1024,512]{0,1:T(8,128)S(1)} %copy-done.34, f32[1024,512]{0,1:T(8,128)S(1)} %copy-done.17), kind=kOutput, calls=%fused_computation.86 | convolution fusion | flops 3230661632 | bytes 14686208 | tf_op jit(solution)/shard_map/dot_general | solution.py:22
  411.7 5.9 fusion.6
  417.6 12.7 %fusion.8 = f32[1024,1536]{0,1:T(8,128)S(1)} fusion(f32[1536,1024]{1,0:T(8,128)S(1)} %bitcast.521, f32[1024,512]{1,0:T(8,128)S(1)} %copy-done.37, f32[1024,512]{1,0:T(8,128)} %get-tuple-element.143), kind=kOutput, calls=%fused_computation.31 | convolution fusion | flops 9664724992 | bytes 16777216 | tf_op jit(solution)/shard_map/dot_general | solution.py:22
  447.6 4.3 slice_bitcast_fusion
  458.1 3.8 fusion.214
  463.8 3.4 fusion.215
  467.5 3.7 fusion.43
  471.2 4.7 fusion.47
  496.5 13.2 %fusion.7 = f32[1536,1024]{1,0:T(8,128)S(1)} fusion(f32[1024,1536]{0,1:T(8,128)} %select_maximum_fusion.2, f32[1024,512]{1,0:T(8,128)S(1)} %copy-done.38, f32[1024,512]{1,0:T(8,128)} %get-tuple-element.143), kind=kOutput, calls=%fused_computation.30 | convolution fusion | flops 9664724992 | bytes 16777216 | tf_op jit(solution)/shard_map/dot_general | solution.py:22
  527.9 6.1 collective-permute-done.25
  536.8 3.3 collective-permute-start.28
  543.8 4.3 all-to-all-start.6
  548.6 23.9 %collective-permute-done.27 = f32[80,1024]{1,0:T(8,128)} collective-permute-done((f32[80,1024]{1,0:T(8,128)}, f32[80,1024]{1,0:T(8,128)}, u32[]{:S(2)}, u32[]{:S(2)}) %collective-permute-start.27) | collective-permute-done | bytes 327712 | tf_op jit(solution)/shard_map/ppermute | solution.py:47
  572.8 4.0 pad_maximum_fusion.12
  576.8 5.0 collective-permute-done.26
  583.0 3.9 pad_maximum_fusion.9
  594.8 3.5 copy.386
  631.6 7.4 %collective-permute-done.15 = f32[4,44,1024]{2,0,1:T(4,128)S(1)} collective-permute-done((f32[4,44,1024]{2,0,1:T(4,128)S(1)}, f32[4,44,1024]{2,0,1:T(4,128)S(1)}, u32[]{:S(2)}, u32[]{:S(2)}) %collective-permute-start.15) | collective-permute-done | bytes 720928 | tf_op jit(solution)/shard_map/ppermute | solution.py:47
  643.4 8.5 %collective-permute-start.23 = (f32[88,1024]{1,0:T(8,128)S(1)}, f32[88,1024]{1,0:T(8,128)S(1)}, u32[]{:S(2)}, u32[]{:S(2)}) collective-permute-start(f32[88,1024]{1,0:T(8,128)S(1)} %get-tuple-element.197), channel_id=1, source_target_pairs={{0,24},{1,25},{2,26},{3,27},{4,28},{5,29},{6,30},{7,31},{8,0},{9,1... | collective-permute-start | bytes 1081352 | tf_op jit(solution)/shard_map/ppermute | solution.py:47
  651.9 3.3 collective-permute-start.22
  661.3 22.7 %collective-permute-done.22 = f32[88,1024]{1,0:T(8,128)S(1)} collective-permute-done((f32[88,1024]{1,0:T(8,128)S(1)}, f32[88,1024]{1,0:T(8,128)S(1)}, u32[]{:S(2)}, u32[]{:S(2)}) %collective-permute-start.22) | collective-permute-done | bytes 360480 | tf_op jit(solution)/shard_map/ppermute | solution.py:47
  697.1 4.1 add_bitcast_fusion
  701.2 2.9 copy.444
  (462 shorter events, 236.5 us)
Async XLA Ops:
  7.2 240.0 %copy-start = (f32[1,1024,512]{2,1,0:T(8,128)S(1)}, f32[1,1024,512]{2,1,0:T(8,128)}, u32[]{:S(2)}) copy-start(f32[1,1024,512]{2,1,0:T(8,128)} %param.20) | copy-start | bytes 6291460
  7.2 139.9 %all-gather.7.cloned.1.call-start = ((), (), s32[]{:S(2)}) async-start(), calls=%async_computation.8 | async-start | bytes 11894784 | tf_op jit(solution)/shard_map/all_gather | solution.py:268
  15.7 9.5 %collective-permute-start = (f32[32,1024]{1,0:T(8,128)S(1)}, f32[32,1024]{1,0:T(8,128)S(1)}, u32[]{:S(2)}, u32[]{:S(2)}) collective-permute-start(f32[32,1024]{1,0:T(8,128)S(1)} %bitcast.570), channel_id=1, source_target_pairs={{0,8},{1,9},{2,10},{3,11},{4,12},{5,13},{6,14},{7,15},{8,16},{9,17... | collective-permute-start | bytes 393224 | tf_op jit(solution)/shard_map/ppermute | solution.py:47
  18.7 15.5 %collective-permute-start.1 = (f32[32,1024]{1,0:T(8,128)S(1)}, f32[32,1024]{1,0:T(8,128)S(1)}, u32[]{:S(2)}, u32[]{:S(2)}) collective-permute-start(f32[32,1024]{1,0:T(8,128)S(1)} %bitcast.571), channel_id=1, source_target_pairs={{0,16},{1,17},{2,18},{3,19},{4,20},{5,21},{6,22},{7,23},{8,24},{9,... | collective-permute-start | bytes 393224 | tf_op jit(solution)/shard_map/ppermute | solution.py:47
  21.3 13.3 %collective-permute-start.2 = (f32[32,1024]{1,0:T(8,128)S(1)}, f32[32,1024]{1,0:T(8,128)S(1)}, u32[]{:S(2)}, u32[]{:S(2)}) collective-permute-start(f32[32,1024]{1,0:T(8,128)S(1)} %bitcast.572), channel_id=1, source_target_pairs={{0,24},{1,25},{2,26},{3,27},{4,28},{5,29},{6,30},{7,31},{8,0},{9,1... | collective-permute-start | bytes 393224 | tf_op jit(solution)/shard_map/ppermute | solution.py:47
  34.6 11.0 %collective-permute-start.3 = (f32[4,16,1024]{2,1,0:T(8,128)S(1)}, f32[4,16,1024]{2,1,0:T(8,128)}, u32[]{:S(2)}, u32[]{:S(2)}) collective-permute-start(f32[4,16,1024]{2,1,0:T(8,128)S(1)} %get-tuple-element.217), channel_id=1, source_target_pairs={{0,2},{1,3},{2,0},{3,1},{4,6},{5,7},{6,4},{7,5},{8,10},{9,11},{10,... | collective-permute-start | bytes 786440 | tf_op jit(solution)/shard_map/ppermute | solution.py:47
  36.3 9.3 %collective-permute-start.5 = (f32[4,16,1024]{2,1,0:T(8,128)S(1)}, f32[4,16,1024]{2,1,0:T(8,128)}, u32[]{:S(2)}, u32[]{:S(2)}) collective-permute-start(f32[4,16,1024]{2,1,0:T(8,128)S(1)} %get-tuple-element.218), channel_id=1, source_target_pairs={{0,4},{1,5},{2,6},{3,7},{4,0},{5,1},{6,2},{7,3},{8,12},{9,13},{10,... | collective-permute-start | bytes 786440 | tf_op jit(solution)/shard_map/ppermute | solution.py:47
  37.8 89.7 %all-to-all-start = ((f32[32,32,512]{2,1,0:T(8,128)}), f32[32,32,512]{2,1,0:T(8,128)}, u32[]{:S(2)}, u32[]{:S(2)}) async-start(f32[32,32,512]{2,1,0:T(8,128)} %pad_maximum_fusion.25), calls=%async_computation | async-start | bytes 4194304 | tf_op jit(solution)/shard_map/all_to_all | solution.py:277
  45.5 201.0 %all-gather.9.cloned.1.call-start = ((), (), s32[]{:S(2)}) async-start(), calls=%async_computation.9 | async-start | bytes 11894784 | tf_op jit(solution)/shard_map/all_gather | solution.py:310
  46.9 42.5 %collective-permute-start.6 = (f32[2,4,16,1024]{3,2,0,1:T(8,128)S(1)}, f32[2,4,16,1024]{3,2,0,1:T(8,128)S(1)}, u32[]{:S(2)}, u32[]{:S(2)}) collective-permute-start(f32[2,4,16,1024]{3,2,0,1:T(8,128)S(1)} %pad_maximum_fusion.29), channel_id=1, source_target_pairs={{0,2},{1,3},{2,0},{3,1},{4,6},{5,7},{6,4},{7,5},{8,10},{9,11},{10,... | collective-permute-start | bytes 1572872 | tf_op jit(solution)/shard_map/ppermute | solution.py:47
  48.6 41.0 %collective-permute-start.4 = (f32[2,4,16,1024]{3,2,1,0:T(8,128)S(1)}, f32[2,4,16,1024]{3,2,1,0:T(8,128)S(1)}, u32[]{:S(2)}, u32[]{:S(2)}) collective-permute-start(f32[2,4,16,1024]{3,2,1,0:T(8,128)S(1)} %pad_maximum_fusion.28), channel_id=1, source_target_pairs={{0,4},{1,5},{2,6},{3,7},{4,0},{5,1},{6,2},{7,3},{8,12},{9,13},{10,... | collective-permute-start | bytes 1572872 | tf_op jit(solution)/shard_map/ppermute | solution.py:47
  91.4 4.5 collective-permute-start.7
  102.9 25.8 %copy-start.81 = (pred[32]{0:T(512)(128)(4,1)S(1)}, pred[32]{0:T(512)(128)(4,1)}, u32[]{:S(2)}) copy-start(pred[32]{0:T(512)(128)(4,1)} %constant.543.clone.1) | copy-start | bytes 100
  180.2 25.2 %all-to-all-start.1 = ((f32[32,8,128]{2,1,0:T(8,128)}), f32[32,8,128]{2,1,0:T(8,128)S(1)}, u32[]{:S(2)}, u32[]{:S(2)}) async-start(f32[32,8,128]{2,1,0:T(8,128)} %copy.357), calls=%async_computation.1 | async-start | bytes 262144 | tf_op jit(solution)/shard_map/all_to_all | solution.py:147
  191.8 14.5 %copy-start.53 = (f32[2,16,8,64]{3,2,1,0:T(8,128)S(1)}, f32[2,16,8,64]{3,2,1,0:T(8,128)}, u32[]{:S(2)}) copy-start(f32[2,16,8,64]{3,2,1,0:T(8,128)} %reshape.382) | copy-start | bytes 196612
  208.5 16.8 %all-to-all-start.2 = ((f32[32,8,128]{2,1,0:T(8,128)}), f32[32,8,128]{2,1,0:T(8,128)S(1)}, u32[]{:S(2)}, u32[]{:S(2)}) async-start(f32[32,8,128]{2,1,0:T(8,128)} %copy.362), calls=%async_computation.2 | async-start | bytes 262144 | tf_op jit(solution)/shard_map/all_to_all | solution.py:147
  214.7 11.4 %copy-start.62 = (f32[2,16,512]{2,1,0:T(8,128)S(1)}, f32[2,16,512]{2,1,0:T(8,128)}, u32[]{:S(2)}) copy-start(f32[2,16,512]{2,1,0:T(8,128)} %param.34) | copy-start | bytes 196612
  228.0 13.2 %all-to-all-start.3 = ((f32[32,8,128]{2,1,0:T(8,128)}), f32[32,8,128]{2,1,0:T(8,128)S(1)}, u32[]{:S(2)}, u32[]{:S(2)}) async-start(f32[32,8,128]{2,1,0:T(8,128)} %copy.366), calls=%async_computation.3 | async-start | bytes 262144 | tf_op jit(solution)/shard_map/all_to_all | solution.py:147
  243.6 13.4 %all-to-all-start.4 = ((f32[32,16,128]{2,1,0:T(8,128)}), f32[32,16,128]{2,1,0:T(8,128)S(1)}, u32[]{:S(2)}, u32[]{:S(2)}) async-start(f32[32,16,128]{2,1,0:T(8,128)} %reshape.388), calls=%async_computation.4 | async-start | bytes 524288 | tf_op jit(solution)/shard_map/all_to_all | solution.py:147
  246.4 201.2 %all-gather.11.cloned.1.call-start = ((), (), s32[]{:S(2)}) async-start(), calls=%async_computation.10 | async-start | bytes 8650752 | tf_op jit(solution)/shard_map/all_gather | solution.py:344
  281.4 24.2 %copy-start.33 = (f32[1024,512]{0,1:T(8,128)}, f32[1024,512]{0,1:T(8,128)S(1)}, u32[]{:S(2)}) copy-start(f32[1024,512]{0,1:T(8,128)S(1)} %get-tuple-element.242) | copy-start | bytes 6291460
  282.3 17.4 %copy-start.39 = (f32[1022,512]{0,1:T(8,128)}, f32[1022,512]{0,1:T(8,128)S(1)}, u32[]{:S(2)}) copy-start(f32[1022,512]{0,1:T(8,128)S(1)} %get-tuple-element.191) | copy-start | bytes 6279172
  282.3 17.4 %copy-start.41 = (f32[1022,512]{0,1:T(8,128)}, f32[1022,512]{0,1:T(8,128)S(1)}, u32[]{:S(2)}) copy-start(f32[1022,512]{0,1:T(8,128)S(1)} %get-tuple-element.192) | copy-start | bytes 6279172
  299.7 15.4 %slice-start.4 = ((s8[6291456]{0:T(1024)(128)(4,1)}), s8[4194304]{0:T(1024)(128)(4,1)S(1)}, s32[]{:S(2)}) async-start(s8[6291456]{0:T(1024)(128)(4,1)} %bitcast.523), calls=%async_computation.15 | async-start | bytes 8388608
  305.6 27.1 %copy-start.29 = (f32[1024,1024]{1,0:T(8,128)}, f32[1024,1024]{1,0:T(8,128)S(1)}, u32[]{:S(2)}) copy-start(f32[1024,1024]{1,0:T(8,128)S(1)} %bitcast_add_fusion) | copy-start | bytes 12582916
  305.6 9.5 %slice-start.5 = ((s8[6291456]{0:T(1024)(128)(4,1)}), s8[2097152]{0:T(1024)(128)(4,1)S(1)}, s32[]{:S(2)}) async-start(s8[6291456]{0:T(1024)(128)(4,1)} %bitcast.523), calls=%async_computation.16 | async-start | bytes 4194304
  385.8 106.6 %copy-start.20 = (f32[4,1,2,40,1024]{4,3,0,2,1:T(8,128)}, f32[4,1,2,40,1024]{4,3,0,2,1:T(8,128)S(1)}, u32[]{:S(2)}) copy-start(f32[4,1,2,40,1024]{4,3,0,2,1:T(8,128)S(1)} %copy.521) | copy-start | bytes 3932164
  386.9 50.7 %collective-permute-start.11 = (f32[4,2,2,16,1024]{4,3,0,2,1:T(8,128)}, f32[4,2,2,16,1024]{4,3,0,2,1:T(8,128)S(1)}, u32[]{:S(2)}, u32[]{:S(2)}) collective-permute-start(f32[4,2,2,16,1024]{4,3,0,2,1:T(8,128)} %copy.399), channel_id=1, source_target_pairs={{0,1},{1,0},{2,3},{3,2},{4,5},{5,4},{6,7},{7,6},{8,9},{9,8},{10,11... | collective-permute-start | bytes 3145736 | tf_op jit(solution)/shard_map/ppermute | solution.py:47
  388.1 49.4 %collective-permute-start.10 = (f32[4,2,2,16,1024]{4,3,0,2,1:T(8,128)}, f32[4,2,2,16,1024]{4,3,0,2,1:T(8,128)}, u32[]{:S(2)}, u32[]{:S(2)}) collective-permute-start(f32[4,2,2,16,1024]{4,3,0,2,1:T(8,128)} %copy.397), channel_id=1, source_target_pairs={{0,1},{1,0},{2,3},{3,2},{4,5},{5,4},{6,7},{7,6},{8,9},{9,8},{10,11... | collective-permute-start | bytes 3145736 | tf_op jit(solution)/shard_map/ppermute | solution.py:47
  388.9 48.6 %collective-permute-start.8 = (f32[4,2,2,48,1024]{4,3,0,2,1:T(8,128)S(1)}, f32[4,2,2,48,1024]{4,3,0,2,1:T(8,128)S(1)}, u32[]{:S(2)}, u32[]{:S(2)}) collective-permute-start(f32[4,2,2,48,1024]{4,3,0,2,1:T(8,128)S(1)} %copy.392), channel_id=1, source_target_pairs={{0,1},{1,0},{2,3},{3,2},{4,5},{5,4},{6,7},{7,6},{8,9},{9,8},{10,11... | collective-permute-start | bytes 9437192 | tf_op jit(solution)/shard_map/ppermute | solution.py:47
  398.6 19.0 %slice-start.2 = ((s8[6291456]{0:T(1024)(128)(4,1)}), s8[4194304]{0:T(1024)(128)(4,1)S(1)}, s32[]{:S(2)}) async-start(s8[6291456]{0:T(1024)(128)(4,1)} %bitcast.519), calls=%async_computation.13 | async-start | bytes 8388608
  400.9 16.6 %slice-start.3 = ((s8[6291456]{0:T(1024)(128)(4,1)}), s8[2097152]{0:T(1024)(128)(4,1)S(1)}, s32[]{:S(2)}) async-start(s8[6291456]{0:T(1024)(128)(4,1)} %bitcast.519), calls=%async_computation.14 | async-start | bytes 4194304
  400.9 182.1 %collective-permute-start.17 = (f32[4,2,2,16,1024]{4,3,0,2,1:T(8,128)}, f32[4,2,2,16,1024]{4,3,0,2,1:T(8,128)}, u32[]{:S(2)}, u32[]{:S(2)}) collective-permute-start(f32[4,2,2,16,1024]{4,3,0,2,1:T(8,128)} %copy.416), channel_id=1, source_target_pairs={{0,1},{1,0},{2,3},{3,2},{4,5},{5,4},{6,7},{7,6},{8,9},{9,8},{10,11... | collective-permute-start | bytes 3145736 | tf_op jit(solution)/shard_map/ppermute | solution.py:47
  432.6 150.4 %collective-permute-start.16 = (f32[4,2,2,16,1024]{4,3,0,2,1:T(8,128)}, f32[4,2,2,16,1024]{4,3,0,2,1:T(8,128)}, u32[]{:S(2)}, u32[]{:S(2)}) collective-permute-start(f32[4,2,2,16,1024]{4,3,0,2,1:T(8,128)} %copy.414), channel_id=1, source_target_pairs={{0,1},{1,0},{2,3},{3,2},{4,5},{5,4},{6,7},{7,6},{8,9},{9,8},{10,11... | collective-permute-start | bytes 3145736 | tf_op jit(solution)/shard_map/ppermute | solution.py:47
  441.7 50.6 %collective-permute-start.9 = (f32[4,2,40,1024]{3,2,0,1:T(8,128)}, f32[4,2,40,1024]{3,2,0,1:T(8,128)}, u32[]{:S(2)}, u32[]{:S(2)}) collective-permute-start(f32[4,2,40,1024]{3,2,0,1:T(8,128)} %get-tuple-element.173), channel_id=1, source_target_pairs={{0,4},{1,5},{2,6},{3,7},{4,0},{5,1},{6,2},{7,3},{8,12},{9,13},{10,... | collective-permute-start | bytes 3932168 | tf_op jit(solution)/shard_map/ppermute | solution.py:47
  447.0 45.4 %collective-permute-start.12 = (f32[4,2,40,1024]{3,2,1,0:T(8,128)}, f32[4,2,40,1024]{3,2,1,0:T(8,128)}, u32[]{:S(2)}, u32[]{:S(2)}) collective-permute-start(f32[4,2,40,1024]{3,2,1,0:T(8,128)} %get-tuple-element.169), channel_id=1, source_target_pairs={{0,2},{1,3},{2,0},{3,1},{4,6},{5,7},{6,4},{7,5},{8,10},{9,11},{10,... | collective-permute-start | bytes 3932168 | tf_op jit(solution)/shard_map/ppermute | solution.py:47
  486.9 39.0 %all-to-all-start.5 = ((f32[32,8,128]{2,1,0:T(8,128)}), f32[32,8,128]{2,1,0:T(8,128)S(1)}, u32[]{:S(2)}, u32[]{:S(2)}) async-start(f32[32,8,128]{2,1,0:T(8,128)} %copy.385), calls=%async_computation.5 | async-start | bytes 262144 | tf_op jit(solution)/shard_map/all_to_all | solution.py:147
  494.6 31.4 %collective-permute-start.24 = (f32[4,40,1024]{2,1,0:T(8,128)}, f32[4,40,1024]{2,1,0:T(8,128)}, u32[]{:S(2)}, u32[]{:S(2)}) collective-permute-start(f32[4,40,1024]{2,1,0:T(8,128)} %add_bitcast_fusion.1), channel_id=1, source_target_pairs={{0,2},{1,3},{2,0},{3,1},{4,6},{5,7},{6,4},{7,5},{8,10},{9,11},{10,... | collective-permute-start | bytes 1966088 | tf_op jit(solution)/shard_map/ppermute | solution.py:47
  514.2 68.9 %collective-permute-start.13 = (f32[4,2,2,48,1024]{4,3,0,2,1:T(8,128)}, f32[4,2,2,48,1024]{4,3,0,2,1:T(8,128)}, u32[]{:S(2)}, u32[]{:S(2)}) collective-permute-start(f32[4,2,2,48,1024]{4,3,0,2,1:T(8,128)} %copy.404), channel_id=1, source_target_pairs={{0,1},{1,0},{2,3},{3,2},{4,5},{5,4},{6,7},{7,6},{8,9},{9,8},{10,11... | collective-permute-start | bytes 9437192 | tf_op jit(solution)/shard_map/ppermute | solution.py:47
  517.1 16.8 %collective-permute-start.25 = (f32[4,40,1024]{2,1,0:T(8,128)}, f32[4,40,1024]{2,1,0:T(8,128)}, u32[]{:S(2)}, u32[]{:S(2)}) collective-permute-start(f32[4,40,1024]{2,1,0:T(8,128)} %fusion.73), channel_id=1, source_target_pairs={{0,4},{1,5},{2,6},{3,7},{4,0},{5,1},{6,2},{7,3},{8,12},{9,13},{10,... | collective-permute-start | bytes 1966088 | tf_op jit(solution)/shard_map/ppermute | solution.py:47
  527.9 13.0 %copy-start.73 = (f32[16,16]{1,0:T(8,128)S(1)}, f32[16,16]{1,0:T(8,128)}, u32[]{:S(2)}) copy-start(f32[16,16]{1,0:T(8,128)} %get-tuple-element.267) | copy-start | bytes 3076
  527.9 13.0 %copy-start.74 = (f32[16,16]{1,0:T(8,128)S(1)}, f32[16,16]{1,0:T(8,128)}, u32[]{:S(2)}) copy-start(f32[16,16]{1,0:T(8,128)} %get-tuple-element.268) | copy-start | bytes 3076
  536.8 11.8 %collective-permute-start.28 = (f32[80,1024]{1,0:T(8,128)}, f32[80,1024]{1,0:T(8,128)}, u32[]{:S(2)}, u32[]{:S(2)}) collective-permute-start(f32[80,1024]{1,0:T(8,128)} %get-tuple-element.204), channel_id=1, source_target_pairs={{0,24},{1,25},{2,26},{3,27},{4,28},{5,29},{6,30},{7,31},{8,0},{9,1... | collective-permute-start | bytes 983048 | tf_op jit(solution)/shard_map/ppermute | solution.py:47
  540.2 32.4 %collective-permute-start.27 = (f32[80,1024]{1,0:T(8,128)}, f32[80,1024]{1,0:T(8,128)}, u32[]{:S(2)}, u32[]{:S(2)}) collective-permute-start(f32[80,1024]{1,0:T(8,128)} %get-tuple-element.203), channel_id=1, source_target_pairs={{0,16},{1,17},{2,18},{3,19},{4,20},{5,21},{6,22},{7,23},{8,24},{9,... | collective-permute-start | bytes 983048 | tf_op jit(solution)/shard_map/ppermute | solution.py:47
  543.8 51.0 %all-to-all-start.6 = ((f32[32,56,128]{2,1,0:T(8,128)}), f32[32,56,128]{2,1,0:T(8,128)}, u32[]{:S(2)}, u32[]{:S(2)}) async-start(f32[32,56,128]{2,1,0:T(8,128)} %bitcast.543), calls=%async_computation.6 | async-start | bytes 1835008 | tf_op jit(solution)/shard_map/all_to_all | solution.py:147
  548.6 34.4 %collective-permute-start.18 = (f32[4,2,2,8,1024]{4,3,0,2,1:T(8,128)}, f32[4,2,2,8,1024]{4,3,0,2,1:T(8,128)S(1)}, u32[]{:S(2)}, u32[]{:S(2)}) collective-permute-start(f32[4,2,2,8,1024]{4,3,0,2,1:T(8,128)} %bitcast.574), channel_id=1, source_target_pairs={{0,1},{1,0},{2,3},{3,2},{4,5},{5,4},{6,7},{7,6},{8,9},{9,8},{10,11... | collective-permute-start | bytes 1572872 | tf_op jit(solution)/shard_map/ppermute | solution.py:47
  572.6 9.3 %collective-permute-start.26 = (f32[80,1024]{1,0:T(8,128)}, f32[80,1024]{1,0:T(8,128)S(1)}, u32[]{:S(2)}, u32[]{:S(2)}) collective-permute-start(f32[80,1024]{1,0:T(8,128)} %get-tuple-element.202), channel_id=1, source_target_pairs={{0,8},{1,9},{2,10},{3,11},{4,12},{5,13},{6,14},{7,15},{8,16},{9,17... | collective-permute-start | bytes 983048 | tf_op jit(solution)/shard_map/ppermute | solution.py:47
  576.8 10.1 %copy-start.14 = (f32[4,2,2,44,1024]{4,3,2,1,0:T(8,128)}, f32[4,2,2,44,1024]{4,3,2,1,0:T(8,128)S(1)}, u32[]{:S(2)}) copy-start(f32[4,2,2,44,1024]{4,3,2,1,0:T(8,128)S(1)} %get-tuple-element.162) | copy-start | bytes 8650756
  576.8 14.4 %copy-start.12 = (f32[4,2,2,44,1024]{4,3,2,1,0:T(8,128)}, f32[4,2,2,44,1024]{4,3,2,1,0:T(8,128)S(1)}, u32[]{:S(2)}) copy-start(f32[4,2,2,44,1024]{4,3,2,1,0:T(8,128)S(1)} %get-tuple-element.161) | copy-start | bytes 8650756
  589.7 31.0 %collective-permute-start.14 = (f32[4,2,44,1024]{3,0,2,1:T(4,128)}, f32[4,2,44,1024]{3,0,2,1:T(4,128)}, u32[]{:S(2)}, u32[]{:S(2)}) collective-permute-start(f32[4,2,44,1024]{3,0,2,1:T(4,128)} %copy.405), channel_id=1, source_target_pairs={{0,4},{1,5},{2,6},{3,7},{4,0},{5,1},{6,2},{7,3},{8,12},{9,13},{10,... | collective-permute-start | bytes 4325384 | tf_op jit(solution)/shard_map/ppermute | solution.py:47
  593.6 32.5 %collective-permute-start.19 = (f32[4,2,44,1024]{3,0,2,1:T(4,128)}, f32[4,2,44,1024]{3,0,2,1:T(4,128)}, u32[]{:S(2)}, u32[]{:S(2)}) collective-permute-start(f32[4,2,44,1024]{3,0,2,1:T(4,128)} %copy.419), channel_id=1, source_target_pairs={{0,2},{1,3},{2,0},{3,1},{4,6},{5,7},{6,4},{7,5},{8,10},{9,11},{10,... | collective-permute-start | bytes 4325384 | tf_op jit(solution)/shard_map/ppermute | solution.py:47
  604.5 11.0 %copy-start.67 = (f32[32,2,16]{0,2,1:T(8,128)S(1)}, f32[32,2,16]{0,2,1:T(8,128)}, u32[]{:S(2)}) copy-start(f32[32,2,16]{0,2,1:T(8,128)} %copy-done.66) | copy-start | bytes 12292
  604.5 13.6 %copy-start.48 = (f32[32,256]{0,1:T(8,128)S(1)}, f32[32,256]{0,1:T(8,128)}, u32[]{:S(2)}) copy-start(f32[32,256]{0,1:T(8,128)} %copy-done.47) | copy-start | bytes 98308
  624.5 14.5 %collective-permute-start.15 = (f32[4,44,1024]{2,0,1:T(4,128)S(1)}, f32[4,44,1024]{2,0,1:T(4,128)S(1)}, u32[]{:S(2)}, u32[]{:S(2)}) collective-permute-start(f32[4,44,1024]{2,0,1:T(4,128)S(1)} %copy.408), channel_id=1, source_target_pairs={{0,2},{1,3},{2,0},{3,1},{4,6},{5,7},{6,4},{7,5},{8,10},{9,11},{10,... | collective-permute-start | bytes 2162696 | tf_op jit(solution)/shard_map/ppermute | solution.py:47
  628.5 13.8 %collective-permute-start.20 = (f32[4,44,1024]{2,0,1:T(4,128)S(1)}, f32[4,44,1024]{2,0,1:T(4,128)S(1)}, u32[]{:S(2)}, u32[]{:S(2)}) collective-permute-start(f32[4,44,1024]{2,0,1:T(4,128)S(1)} %copy.422), channel_id=1, source_target_pairs={{0,4},{1,5},{2,6},{3,7},{4,0},{5,1},{6,2},{7,3},{8,12},{9,13},{10,... | collective-permute-start | bytes 2162696 | tf_op jit(solution)/shard_map/ppermute | solution.py:47
  643.3 14.1 %copy-start.54 = (f32[1,32,512]{2,1,0:T(8,128)S(1)}, f32[1,32,512]{2,1,0:T(8,128)}, u32[]{:S(2)}) copy-start(f32[1,32,512]{2,1,0:T(8,128)} %copy.388) | copy-start | bytes 196612
  643.3 14.1 %copy-start.55 = (f32[1,32,512]{2,1,0:T(8,128)S(1)}, f32[1,32,512]{2,1,0:T(8,128)}, u32[]{:S(2)}) copy-start(f32[1,32,512]{2,1,0:T(8,128)} %copy.387) | copy-start | bytes 196612
  643.3 16.2 %copy-start.71 = (f32[2,16,32]{2,1,0:T(8,128)S(1)}, f32[2,16,32]{2,1,0:T(8,128)}, u32[]{:S(2)}) copy-start(f32[2,16,32]{2,1,0:T(8,128)} %param.30) | copy-start | bytes 12292
  643.4 17.9 %collective-permute-start.23 = (f32[88,1024]{1,0:T(8,128)S(1)}, f32[88,1024]{1,0:T(8,128)S(1)}, u32[]{:S(2)}, u32[]{:S(2)}) collective-permute-start(f32[88,1024]{1,0:T(8,128)S(1)} %get-tuple-element.197), channel_id=1, source_target_pairs={{0,24},{1,25},{2,26},{3,27},{4,28},{5,29},{6,30},{7,31},{8,0},{9,1... | collective-permute-start | bytes 1081352 | tf_op jit(solution)/shard_map/ppermute | solution.py:47
  651.9 32.2 %collective-permute-start.22 = (f32[88,1024]{1,0:T(8,128)S(1)}, f32[88,1024]{1,0:T(8,128)S(1)}, u32[]{:S(2)}, u32[]{:S(2)}) collective-permute-start(f32[88,1024]{1,0:T(8,128)S(1)} %get-tuple-element.196), channel_id=1, source_target_pairs={{0,16},{1,17},{2,18},{3,19},{4,20},{5,21},{6,22},{7,23},{8,24},{9,... | collective-permute-start | bytes 1081352 | tf_op jit(solution)/shard_map/ppermute | solution.py:47
  655.2 28.9 %collective-permute-start.21 = (f32[88,1024]{1,0:T(8,128)S(1)}, f32[88,1024]{1,0:T(8,128)S(1)}, u32[]{:S(2)}, u32[]{:S(2)}) collective-permute-start(f32[88,1024]{1,0:T(8,128)S(1)} %get-tuple-element.195), channel_id=1, source_target_pairs={{0,8},{1,9},{2,10},{3,11},{4,12},{5,13},{6,14},{7,15},{8,16},{9,17... | collective-permute-start | bytes 1081352 | tf_op jit(solution)/shard_map/ppermute | solution.py:47
  661.3 23.0 %copy-start.32 = (f32[2,32,8,64]{3,2,1,0:T(8,128)S(1)}, f32[2,32,8,64]{3,2,1,0:T(8,128)}, u32[]{:S(2)}) copy-start(f32[2,32,8,64]{3,2,1,0:T(8,128)} %copy-done.31) | copy-start | bytes 393220
  661.3 26.0 %copy-start.49 = (f32[1,16,1024]{2,1,0:T(8,128)S(1)}, f32[1,16,1024]{2,1,0:T(8,128)}, u32[]{:S(2)}) copy-start(f32[1,16,1024]{2,1,0:T(8,128)} %get-tuple-element.224) | copy-start | bytes 196612
  694.4 10.9 %all-to-all-start.7 = ((f32[32,8,128]{2,1,0:T(8,128)}), f32[32,8,128]{2,1,0:T(8,128)S(1)}, u32[]{:S(2)}, u32[]{:S(2)}) async-start(f32[32,8,128]{2,1,0:T(8,128)} %broadcast_in_dim.169), calls=%async_computation.7 | async-start | bytes 262144 | tf_op jit(solution)/shard_map/all_to_all | solution.py:437
  (65 other events, 250.6 us)
Sparse Core Ops, SparseCore 0:
  11.1 131.7 all-gather.6
  147.2 96.1 all-gather.8
  250.1 78.6 all-gather.10

commit v2 on v1

v2 whole, which is shorter than its diff:
```python
import functools
import math

import jax
import jax.numpy as jnp
from jax import lax
from jax.experimental import pallas as pl
from jax.experimental.pallas import tpu as pltpu
from jax.sharding import PartitionSpec as P

WIDTH = 512
GATES = 2 * WIDTH
HEADS = 8
HEAD_DIM = WIDTH // HEADS
QUERIES = 32
LAYERS = 2
CLIP_NORM = 1.0
AXIS = "items"
HIGH = lax.Precision.HIGH
HIGHEST = lax.Precision.HIGHEST
ROOT_HALF = math.sqrt(0.5)


def big_dot(left, right, left_dim=1, right_dim=0):
    return lax.dot_general(left, right, (((left_dim,), (right_dim,)), ((), ())), precision=HIGH)


def small_dot(left, right, left_dim=1, right_dim=0):
    return lax.dot_general(left, right, (((left_dim,), (right_dim,)), ((), ())), precision=HIGHEST)


def step_embedding(diffusion_step):
    half_width = WIDTH // 2
    ramp = jnp.arange(half_width, dtype=jnp.int32).astype(jnp.float32) / (half_width - 1)
    angles = diffusion_step.astype(jnp.float32) / 1000.0 * jnp.exp(ramp * math.log(100.0))
    return jnp.concatenate([jnp.sin(angles), jnp.cos(angles)])


class Ring:
    def __init__(self, count, size, stride):
        self.count, self.size, self.stride = count, size, stride
        self.digit = (lax.axis_index(AXIS) // stride) % size

    def shift(self, block, steps):
        perm = []
        for device in range(self.count):
            digit = (device // self.stride) % self.size
            target = (digit + steps) % self.size
            perm.append((device, device + (target - digit) * self.stride))
        return lax.ppermute(block, AXIS, perm)

    def gather(self, block):
        if self.size == 1:
            return block[None]
        others = [self.shift(block, steps) for steps in range(1, self.size)]
        if self.size == 2:
            first = jnp.where(self.digit == 0, block, others[0])
            second = jnp.where(self.digit == 0, others[0], block)
            return jnp.stack([first, second])
        out = jnp.broadcast_to(block, (self.size,) + block.shape)
        for steps, other in enumerate(others, 1):
            place = (self.digit - steps) % self.size
            out = lax.dynamic_update_index_in_dim(out, other, place, 0)
        return out

    def scatter_sum(self, blocks, dim):
        own = lax.dynamic_index_in_dim(blocks, self.digit, dim, keepdims=False)
        for steps in range(1, self.size):
            place = (self.digit + steps) % self.size
            own = own + self.shift(lax.dynamic_index_in_dim(blocks, place, dim, keepdims=False), steps)
        return own


def rings_of(count):
    bits = (count // 2).bit_length() - 1
    sizes = [2 ** ((bits + 2) // 3), 2 ** ((bits + 1) // 3), 2 ** (bits // 3), 2]
    rings, stride = [], count
    for size in sizes:
        stride //= size
        rings.append(Ring(count, size, stride))
    return rings


def pairs_of(count):
    return [Ring(count, 2, 2**bit) for bit in reversed(range(count.bit_length() - 1))]


def gather_rows(shard, rings):
    far, mid, near, core = rings
    rows, columns = shard.shape
    half = rows // 2
    block = far.gather(shard)
    top = mid.gather(near.gather(block[:, :half]))
    low = near.gather(mid.gather(block[:, half:]))
    top = jnp.transpose(top, (2, 0, 1, 3, 4))
    low = jnp.transpose(low, (2, 1, 0, 3, 4))
    rail = jnp.concatenate([top, low], axis=3)
    both = core.gather(rail)
    return jnp.transpose(both, (1, 2, 3, 0, 4, 5)).reshape(-1, rows, columns)


def hop(terms, ring, dim, gates=()):
    def pick(place):
        return [lax.dynamic_index_in_dim(term, place, dim, keepdims=False) for term in terms]

    goes, gates = tie(sum(pick(1 - ring.digit)), gates) if gates else (sum(pick(1 - ring.digit)), gates)
    return pick(ring.digit) + [ring.shift(goes, 1)], gates


class RowSum:
    def __init__(self, arrays, pairs, far_first=False):
        count = len(pairs)
        self.pairs, self.at, bits = pairs, 0, list(range(count))
        self.orders = []
        for k in range(len(arrays)):
            near = bits[-3:-1] if k % 2 == 0 else bits[-3:-1][::-1]
            far = bits[:-3][::-1]
            self.orders.append(bits[-1:] + (far + near if far_first else near + far))
        self.left = [list(bits) for _ in arrays]
        self.state = [[array.reshape((2,) * count + array.shape[1:])] for array in arrays]

    def add(self, other):
        self.state, self.orders, self.left = (
            self.state + other.state,
            self.orders + other.orders,
            self.left + other.left,
        )

    def join(self):
        parts = self.state if self.at == 1 else [[sum(terms)] for terms in self.state]
        axis = parts[0][0].ndim - 2
        self.state = [[jnp.concatenate(terms, axis=axis) for terms in zip(*parts)]]

    def halve(self):
        (terms,) = self.state
        half = terms[0].shape[-2] // 2
        self.state = [[term[..., :half, :] for term in terms], [term[..., half:, :] for term in terms]]

    def step(self, *gates):
        for k, terms in enumerate(self.state):
            bit = self.orders[k][self.at]
            if self.at >= 3:
                terms = [sum(terms)]
            self.state[k], gates = hop(terms, self.pairs[bit], self.left[k].index(bit), gates)
            self.left[k].remove(bit)
        self.at += 1
        return gates

    def result(self):
        while self.at < len(self.pairs):
            self.step()
        (terms,) = self.state
        return sum(terms)


def beside(sums, work, *inputs):
    for rows in sums:
        inputs = rows.step(*inputs)
    out = work(*inputs)
    came, out = tie([[terms[-1] for terms in rows.state] for rows in sums], out)
    for rows, last in zip(sums, came):
        rows.state = [terms[:-1] + [term] for terms, term in zip(rows.state, last)]
    return out


def tie(*groups):
    leaves, tree = jax.tree.flatten(groups)
    return jax.tree.unflatten(tree, lax.optimization_barrier(leaves))


def exchange(*parts):
    devices = parts[0].shape[0]
    parts = [part.reshape(devices, -1) for part in parts]
    sizes = [part.shape[1] for part in parts]
    joined = jnp.concatenate(parts, axis=1)
    joined = jnp.pad(joined, ((0, 0), (0, -joined.shape[1] % 1024))).reshape(devices, -1, 128)
    came = lax.all_to_all(joined, AXIS, split_axis=0, concat_axis=0, tiled=True).reshape(devices, -1)
    out, start = [], 0
    for size in sizes:
        out.append(came[:, start : start + size])
        start += size
    return out


def to_all(part, devices):
    return jnp.broadcast_to(part.reshape(1, -1), (devices, part.size))


def regrouped(whole, share):
    sizes, start, pieces = (3 * share, share, share, share // 2), 0, []
    for size in sizes:
        pieces.append(whole[:, start : start + size].reshape(PARTS, -1, GATES))
        start += size
    return jnp.concatenate(pieces, axis=1)


def by_column(part, devices):
    cut = part.reshape(part.shape[:-1] + (devices, -1))
    return jnp.moveaxis(cut, -2, 0).reshape(devices, -1)


def head_rows(row):
    head = jnp.arange(WIDTH, dtype=jnp.int32)[None, :] // HEAD_DIM
    own = head == jnp.arange(HEADS, dtype=jnp.int32)[:, None]
    return jnp.where(own, row, 0.0)


def exact_dot(left, right, left_dim=1, right_dim=0):
    return lax.dot_general(
        left, right, (((left_dim,), (right_dim,)), ((), ())), precision=HIGHEST, preferred_element_type=jnp.float32
    )


def head_of(shape, dim, per_head):
    return lax.broadcasted_iota(jnp.int32, shape, dim) // per_head


def attention_back_kernel(
    grad_film, film_w, value_mixing, key_w, probs, keys, absorbed_out, query_out, row_out, mixed_out
):
    film = film_w[...].reshape(WIDTH, GATES)
    value = value_mixing[..., :WIDTH].reshape(WIDTH, WIDTH)
    mixing = value_mixing[..., WIDTH:].reshape(WIDTH, WIDTH)
    grad_mixed = exact_dot(jnp.broadcast_to(grad_film[...], (8, GATES)), film, 1, 1)
    grad_row = exact_dot(grad_mixed * (1.0 / QUERIES), mixing, 1, 1)
    mixed_out[...] = grad_mixed[:1]
    row_out[...] = grad_row[:1]
    own = head_of((HEADS, WIDTH), 1, HEAD_DIM) == head_of((HEADS, WIDTH), 0, 1)
    grad_pooled = exact_dot(jnp.where(own, grad_row, 0.0), value, 1, 1)
    grad_probs = exact_dot(grad_pooled, keys[...], 1, 1)
    prob = probs[0]
    weighted = prob * grad_probs[:, None, :]
    row_terms = jnp.sum(weighted, axis=2, keepdims=True)
    grad_scores = (weighted - prob * row_terms) * (1.0 / math.sqrt(HEAD_DIM))
    grad_scores = grad_scores.reshape(HEADS * QUERIES, -1)
    grad_absorbed = exact_dot(grad_scores, keys[...])
    absorbed_out[...] = grad_absorbed.T
    grad_query = exact_dot(grad_absorbed, key_w[0])
    shape = grad_query.shape
    grad_query = jnp.where(head_of(shape, 1, HEAD_DIM) == head_of(shape, 0, QUERIES), grad_query, 0.0)
    query_out[...] = jnp.sum(grad_query.reshape(HEADS, QUERIES, WIDTH), axis=0)


def attention_back(layer, grad_film, attention_whole, key_w, probs, keys):
    parts, _, _, rows, _ = attention_whole.shape
    count = keys.shape[0]

    def one(shape):
        return pl.BlockSpec((1,) + shape, lambda k: (layer,) + (0,) * len(shape))

    return kernel_call(
        attention_back_kernel,
        (1,),
        [
            fixed(1, GATES),
            pl.BlockSpec((parts, 1, 1, rows, GATES), lambda k: (0, layer, 0, 0, 0)),
            pl.BlockSpec((parts, 1, 1, rows, GATES), lambda k: (0, layer, 1, 0, 0)),
            one((WIDTH, WIDTH)),
            one((HEADS, QUERIES, count)),
            fixed(count, WIDTH),
        ],
        [fixed(WIDTH, HEADS * QUERIES), fixed(QUERIES, WIDTH), fixed(1, WIDTH), fixed(1, WIDTH)],
        [(WIDTH, HEADS * QUERIES), (QUERIES, WIDTH), (1, WIDTH), (1, WIDTH)],
        [],
        10 * WIDTH * HEADS * QUERIES * count // 4,
    )(grad_film, attention_whole, attention_whole, key_w, probs, keys)


def factor_kernel(
    rows, pooled, means, mixeds, embeds, absorbed, query_rows, seeds, query_w,
    step_out, seeds_out, query_out, key_out, value_out, mixing_out, film_out, square_out,
):
    share = embeds.shape[1]
    at = {}
    start = 0
    for name, size in (("row", WIDTH), ("mixed", WIDTH), ("film", GATES), ("step", WIDTH)):
        for layer in range(LAYERS):
            at[name, layer] = rows[:, start : start + size]
            start += size
    square = jnp.zeros((1, 1), jnp.float32)
    own = head_of((HEADS, share, WIDTH), 2, HEAD_DIM) == head_of((HEADS, share, WIDTH), 0, 1)
    near = head_of((HEADS * QUERIES, WIDTH), 1, HEAD_DIM) == head_of((HEADS * QUERIES, WIDTH), 0, QUERIES)
    for layer in range(LAYERS):
        value = exact_dot(pooled[layer], at["row", layer], 0, 0).reshape(HEADS, share, WIDTH)
        spread = jnp.where(near, jnp.concatenate([query_rows[0, layer]] * HEADS, axis=0), 0.0)
        grads = (
            (step_out, exact_dot(embeds[...], at["step", layer], 0, 0)),
            (seeds_out, exact_dot(query_w[layer], query_rows[1, layer], 1, 1)),
            (query_out, exact_dot(seeds[layer], query_rows[1, layer])),
            (key_out, exact_dot(absorbed[layer], spread)),
            (value_out, QUERIES * jnp.sum(jnp.where(own, value, 0.0), axis=0)),
            (mixing_out, exact_dot(means[layer], at["mixed", layer], 0, 0)),
            (film_out, exact_dot(mixeds[layer], at["film", layer], 0, 0)),
        )
        for out, grad in grads:
            out[layer] = grad
            square = square + jnp.sum(jnp.sum(grad * grad, axis=1, keepdims=True), axis=0, keepdims=True)
    square_out[...] = square


def square_kernel(square, *refs):
    *sums, out = refs
    total = square[...]
    for part in sums:
        total = total + jnp.sum(jnp.sum(part[...] * part[...], axis=1, keepdims=True), axis=0, keepdims=True)
    out[...] = jnp.broadcast_to(total[None], out.shape)


def clip_kernel(squares, sums_0, sums_1, *refs):
    places = squares[:, 0, :1]
    norm_square = jnp.sum(places, axis=0, keepdims=True)
    factor = jnp.minimum(1.0, CLIP_NORM / jnp.sqrt(norm_square))
    count = (len(refs) - 3) // 2
    grads, outs = refs[:count], refs[count : 2 * count]
    conv_out, cond_out, out_out = refs[2 * count :]
    for grad, out in zip(grads, outs):
        for layer in range(LAYERS):
            out[layer] = grad[layer] * factor
    share = cond_out.shape[1]
    for layer, sums in enumerate((sums_0, sums_1)):
        conv_out[layer] = sums[: 3 * share] * factor
        cond_out[layer] = sums[3 * share : 4 * share] * factor
        out_out[layer] = sums[4 * share :] * factor


def shapes_of(*shapes):
    return [jax.ShapeDtypeStruct(shape, jnp.float32) for shape in shapes]


HALF = jnp.bfloat16
PARTS = 32
CONV_ROWS, PART_ROWS, STEP_ROWS = 3 * WIDTH // PARTS, WIDTH // PARTS, WIDTH // PARTS // 2
TILE = 256


def halves_of(array):
    high = array.astype(HALF)
    return high, (array - high.astype(jnp.float32)).astype(HALF)


def three_dots(left, right, left_dim, right_dim):
    def dot(one, other):
        dims = (((left_dim,), (right_dim,)), ((), ()))
        return lax.dot_general(one, other, dims, preferred_element_type=jnp.float32)

    return dot(left[0], right[0]) + (dot(left[0], right[1]) + dot(left[1], right[0]))


def tile_of(pair, start, dim, size=TILE):
    return tuple(lax.slice_in_dim(half, start, start + size, axis=dim) for half in pair)


def moved(rows, steps):
    count = rows.shape[0]
    place = lax.broadcasted_iota(jnp.int32, rows.shape, 0) - steps
    return jnp.where((place >= 0) & (place < count), pltpu.roll(rows, steps % count, 0), 0.0)


def kernel_call(kernel, grid, in_specs, out_specs, out_shapes, scratch, macs):
    return pl.pallas_call(
        kernel,
        grid=grid,
        in_specs=in_specs,
        out_specs=out_specs,
        out_shape=[jax.ShapeDtypeStruct(shape, jnp.float32) for shape in out_shapes],
        scratch_shapes=scratch,
        compiler_params=pltpu.CompilerParams(vmem_limit_bytes=60 * 2**20),
        cost_estimate=pl.CostEstimate(flops=6 * macs, bytes_accessed=16 * 2**20, transcendentals=0),
    )


def fixed(*shape):
    return pl.BlockSpec(shape, lambda k: (0,) * len(shape))


def part_rows(size, at):
    return pl.BlockSpec((PARTS, size, GATES), lambda k: (0, at, 0))


CONV_SPEC = pl.BlockSpec((PARTS // 2, CONV_ROWS, GATES), lambda k: (jnp.minimum(k, 1), 0, 0))
COND_SPEC = part_rows(PART_ROWS, 3)
OUT_SPEC = part_rows(PART_ROWS, 4)


def gates_kernel(dilation, frames, cond, conv_w, cond_w, step_w, embed, live, tanh, sig, step_row, total):
    k = pl.program_id(0)

    @pl.when(k == 0)
    def _():
        pairs = step_w[...].reshape(-1, GATES)
        row = exact_dot(jnp.broadcast_to(embed[:1], (8, embed.shape[1])), pairs[:, :WIDTH])
        row = row + exact_dot(jnp.broadcast_to(embed[1:], (8, embed.shape[1])), pairs[:, WIDTH:])
        step_row[...] = row[:1]

    def add(left, right, first):
        for start in range(0, GATES, TILE):
            part = three_dots(left, tile_of(right, start, 1), 1, 0)
            total[:, start : start + TILE] = part if first else total[:, start : start + TILE] + part

    @pl.when(k == 0)
    def _():
        hidden = (frames[...] + step_row[...]) * live[...]
        taps = jnp.concatenate([moved(hidden, dilation), hidden[:, : WIDTH // 2]], axis=1)
        add(halves_of(taps), halves_of(conv_w[...].reshape(-1, GATES)), True)

    @pl.when(k == 1)
    def _():
        hidden = (frames[...] + step_row[...]) * live[...]
        taps = jnp.concatenate([hidden[:, WIDTH // 2 :], moved(hidden, -dilation)], axis=1)
        add(halves_of(taps), halves_of(conv_w[...].reshape(-1, GATES)), False)

    @pl.when(k == 2)
    def _():
        left, right = halves_of(cond[...]), halves_of(cond_w[...].reshape(-1, GATES))
        for start in range(0, WIDTH, TILE):
            part = three_dots(left, tile_of(right, start, 1), 1, 0)
            tanh[:, start : start + TILE] = jnp.tanh(total[:, start : start + TILE] + part)
        for start in range(0, WIDTH, TILE):
            part = three_dots(left, tile_of(right, WIDTH + start, 1), 1, 0)
            sig[:, start : start + TILE] = jax.nn.sigmoid(total[:, WIDTH + start : WIDTH + start + TILE] + part)


def layer_gates(whole, frames, cond, embed, live, dilation):
    count = frames.shape[0]
    return kernel_call(
        functools.partial(gates_kernel, dilation),
        (3,),
        [fixed(count, WIDTH)] * 2
        + [CONV_SPEC, COND_SPEC, part_rows(STEP_ROWS, 10), fixed(2, WIDTH // 2), fixed(count, 1)],
        [fixed(count, WIDTH)] * 2 + [fixed(1, WIDTH)],
        [(count, WIDTH)] * 2 + [(1, WIDTH)],
        [pltpu.VMEM((count, GATES), jnp.float32)],
        4 * count * WIDTH * GATES,
    )(frames, cond, whole, whole, whole, embed, live)


def post_kernel(tanh, sig, film, out_w, frames, skip, live, frames_next, skip_next, high, low):
    @pl.when(pl.program_id(0) == 0)
    def _():
        high[...], low[...] = halves_of(out_w[...].reshape(-1, GATES))

    modulated = halves_of(tanh[...] * sig[...] * (1.0 + film[:1]) + film[1:])
    for start in range(0, WIDTH, TILE):
        cut = slice(start, start + TILE)
        post = three_dots(modulated, (high[:, cut], low[:, cut]), 1, 0)
        frames_next[:, cut] = (frames[:, cut] + post) * (live[...] * ROOT_HALF)
    for start in range(0, WIDTH, TILE):
        cut, far = slice(start, start + TILE), slice(WIDTH + start, WIDTH + start + TILE)
        post = three_dots(modulated, (high[:, far], low[:, far]), 1, 0)
        skip_next[:, cut] = skip[:, cut] + post * live[...]


def layer_post(whole, tanh, sig, film, frames, skip, live):
    count = frames.shape[0]
    rows = pl.BlockSpec((count // 2, WIDTH), lambda k: (k, 0))
    return kernel_call(
        post_kernel,
        (2,),
        [rows, rows, fixed(2, WIDTH), OUT_SPEC, rows, rows, pl.BlockSpec((count // 2, 1), lambda k: (k, 0))],
        [rows, rows],
        [(count, WIDTH)] * 2,
        [pltpu.VMEM((WIDTH, GATES), HALF)] * 2,
        count * WIDTH * GATES,
    )(tanh, sig, film.reshape(2, WIDTH), whole, frames, skip, live)


def back_gates_kernel(grad_frames, grad_skip, live, tanh, sig, film, out_w, grad_pre, grad_film, grad_out, high, low):
    k = pl.program_id(0)

    @pl.when(k == 0)
    def _():
        high[...], low[...] = halves_of(out_w[...].reshape(-1, GATES))
        grad_film[...] = jnp.zeros_like(grad_film)

    post = jnp.concatenate([grad_frames[...] * (live[...] * ROOT_HALF), grad_skip[...] * live[...]], axis=1)
    post = halves_of(post)
    for start in range(0, WIDTH, TILE):
        cut, far = slice(start, start + TILE), slice(WIDTH + start, WIDTH + start + TILE)
        grad_mod = three_dots(post, (high[cut, :], low[cut, :]), 1, 1)
        t, s = tanh[:, cut], sig[:, cut]
        gate = t * s
        grad_film[0:1, cut] += jnp.sum(grad_mod * gate, axis=0, keepdims=True)
        grad_film[1:2, cut] += jnp.sum(grad_mod, axis=0, keepdims=True)
        grad_gate = grad_mod * (1.0 + film[:1, cut])
        grad_pre[:, cut] = grad_gate * (s * (1.0 - t * t))
        grad_pre[:, far] = grad_gate * (gate * (1.0 - s))
    modulated = tanh[...] * sig[...] * (1.0 + film[:1]) + film[1:]
    modulated = halves_of(modulated.T)

    @pl.when(k == 0)
    def _():
        for start in range(0, GATES, TILE):
            grad_out[:, start : start + TILE] = three_dots(modulated, tile_of(post, start, 1), 1, 0)

    @pl.when(k > 0)
    def _():
        for start in range(0, GATES, TILE):
            grad_out[:, start : start + TILE] += three_dots(modulated, tile_of(post, start, 1), 1, 0)


def layer_back_gates(whole, tanh, sig, film, grad_frames, grad_skip, live):
    count = tanh.shape[0]
    rows = pl.BlockSpec((count // 2, WIDTH), lambda k: (k, 0))
    return kernel_call(
        back_gates_kernel,
        (2,),
        [rows, rows, pl.BlockSpec((count // 2, 1), lambda k: (k, 0)), rows, rows, fixed(2, WIDTH), OUT_SPEC],
        [pl.BlockSpec((count // 2, GATES), lambda k: (k, 0)), fixed(2, WIDTH), fixed(WIDTH, GATES)],
        [(count, GATES), (2, WIDTH), (WIDTH, GATES)],
        [pltpu.VMEM((WIDTH, GATES), HALF)] * 2,
        2 * count * WIDTH * GATES,
    )(grad_frames, grad_skip, live, tanh, sig, film.reshape(2, WIDTH), whole)


def back_weights_kernel(dilation, frames, cond, step_row, live, grad_pre, grad_conv, grad_cond, high, low):
    @pl.when(pl.program_id(0) == 0)
    def _():
        hidden = ((frames[...] + step_row[...]) * live[...]).T
        count = hidden.shape[1]
        for tap, steps in enumerate((dilation, 0, -dilation)):
            moved_rows = hidden
            if steps:
                place = lax.broadcasted_iota(jnp.int32, hidden.shape, 1) - steps
                moved_rows = pltpu.roll(hidden, steps % count, 1)
                moved_rows = jnp.where((place >= 0) & (place < count), moved_rows, 0.0)
            cut = slice(tap * WIDTH, (tap + 1) * WIDTH)
            high[cut, :], low[cut, :] = halves_of(moved_rows)
        cut = slice(3 * WIDTH, 4 * WIDTH)
        high[cut, :], low[cut, :] = halves_of(cond[...].T)

    grad = halves_of(grad_pre[...])
    for start in range(0, 4 * WIDTH, 2 * TILE):
        cut = slice(start, start + 2 * TILE)
        part = three_dots((high[cut, :], low[cut, :]), grad, 1, 0)
        if start < 3 * WIDTH:
            grad_conv[cut, :] = part
        else:
            grad_cond[start - 3 * WIDTH : start - 3 * WIDTH + 2 * TILE, :] = part


def layer_back_weights(frames, cond, step_row, live, grad_pre, dilation):
    count = frames.shape[0]
    return kernel_call(
        functools.partial(back_weights_kernel, dilation),
        (GATES // TILE,),
        [fixed(count, WIDTH)] * 2
        + [fixed(1, WIDTH), fixed(count, 1), pl.BlockSpec((count, TILE), lambda k: (0, k))],
        [pl.BlockSpec((3 * WIDTH, TILE), lambda k: (0, k)), pl.BlockSpec((WIDTH, TILE), lambda k: (0, k))],
        [(3 * WIDTH, GATES), (WIDTH, GATES)],
        [pltpu.VMEM((4 * WIDTH, count), HALF)] * 2,
        4 * count * WIDTH * GATES,
    )(frames, cond, step_row, live, grad_pre)


def back_frames_kernel(dilation, grad_pre, conv_w, grad_frames, live, grad_next, step_sum, high, low, total):
    k = pl.program_id(0)
    middle = WIDTH // 2

    @pl.when(k == 0)
    def _():
        high[...], low[...] = halves_of(grad_pre[...])

    grad, weight = (high[...], low[...]), halves_of(conv_w[...].reshape(-1, GATES))

    def taps(start):
        return three_dots(grad, tile_of(weight, start, 0), 1, 1)

    @pl.when(k == 0)
    def _():
        for start in range(0, WIDTH, TILE):
            total[:, start : start + TILE] = moved(taps(start), -dilation)
        total[:, :middle] += taps(WIDTH)

    @pl.when(k == 1)
    def _():
        total[:, middle:] += taps(0)
        for start in range(0, WIDTH, TILE):
            cut = slice(start, start + TILE)
            hidden = (total[:, cut] + moved(taps(middle + start), dilation)) * live[...]
            step_sum[:, cut] = jnp.sum(hidden, axis=0, keepdims=True)
            grad_next[:, cut] = grad_frames[:, cut] * (live[...] * ROOT_HALF) + hidden


def layer_back_frames(whole, grad_pre, grad_frames, live, dilation):
    count = grad_pre.shape[0]
    return kernel_call(
        functools.partial(back_frames_kernel, dilation),
        (2,),
        [fixed(count, GATES), CONV_SPEC, fixed(count, WIDTH), fixed(count, 1)],
        [fixed(count, WIDTH), fixed(1, WIDTH)],
        [(count, WIDTH), (1, WIDTH)],
        [pltpu.VMEM((count, GATES), HALF)] * 2 + [pltpu.VMEM((count, WIDTH), jnp.float32)],
        3 * count * WIDTH * GATES,
    )(grad_pre, whole, grad_frames, live)


def on_device(
    frames_in,
    conditioning,
    prompt,
    item_lengths,
    prompt_lengths,
    key_mask,
    diffusion_steps,
    step_proj,
    conv_weight,
    cond_proj,
    out_proj,
    query_seeds,
    query_proj,
    key_proj,
    value_proj,
    mixing_proj,
    film_proj,
    cot_frames,
    cot_skip,
    devices,
):
    rings, pairs = rings_of(devices), pairs_of(devices)
    share = step_proj.shape[1]
    key_count = prompt.shape[1]
    extra_rows = -(-(key_count + LAYERS * share * QUERIES) // WIDTH)
    key_rows = -(-(key_count + extra_rows) // 8) * 8
    me = lax.axis_index(AXIS)

    frame_packs = [
        jnp.concatenate(
            [conv_weight[layer], cond_proj[layer], out_proj[layer], step_proj[layer].reshape(-1, GATES)], axis=0
        )
        for layer in range(LAYERS)
    ]
    frame_whole_0 = lax.all_gather(frame_packs[0], AXIS, axis=0, tiled=False)

    extra = jnp.concatenate(
        [key_mask.astype(jnp.float32), to_all(query_seeds, prompt.shape[0])], axis=1
    )
    extra = jnp.pad(extra, ((0, 0), (0, (key_rows - key_count) * WIDTH - extra.shape[1])))
    sent = jnp.concatenate([prompt, extra.reshape(prompt.shape[0], -1, WIDTH)], axis=1)
    query_key = jnp.concatenate([query_proj, key_proj], axis=2).reshape(LAYERS * share, GATES)
    query_key, sent = tie(query_key, sent)
    keys = lax.all_to_all(sent, AXIS, split_axis=0, concat_axis=0, tiled=True)
    extra = keys[:, key_count : key_count + extra_rows].reshape(devices, -1)
    key_place = (
        jnp.arange(devices, dtype=jnp.int32)[:, None] * key_count
        + jnp.arange(key_rows, dtype=jnp.int32)[None, :]
    )
    masked_in = jnp.pad(extra[:, :key_count], ((0, 0), (0, key_rows - key_count)))
    live_keys = (
        (jnp.arange(key_rows, dtype=jnp.int32)[None, :] < key_count)
        & (key_place < lax.dynamic_index_in_dim(prompt_lengths, me, 0, keepdims=False))
        & ((masked_in == 1.0) | (key_place == 0))
    ).reshape(-1)
    seeds = extra[:, key_count : key_count + LAYERS * share * QUERIES]
    seeds = jnp.moveaxis(seeds.reshape(devices, LAYERS, share, QUERIES), 1, 0)
    seeds = seeds.reshape(LAYERS, WIDTH, QUERIES)
    keys = keys.reshape(-1, WIDTH)

    query_key = gather_rows(query_key, rings).reshape(devices, LAYERS, share, GATES)
    query_key = jnp.moveaxis(query_key, 1, 0).reshape(LAYERS, WIDTH, GATES)
    query_rows = jnp.einsum("lwq,lwx->lqx", seeds, query_key[:, :, :WIDTH], precision=HIGHEST)
    query_heads = query_rows.reshape(LAYERS, QUERIES, HEADS, HEAD_DIM)
    key_heads = query_key[:, :, WIDTH:].reshape(LAYERS, WIDTH, HEADS, HEAD_DIM)
    absorbed = jnp.einsum("lqhe,lwhe->lhqw", query_heads, key_heads, precision=HIGHEST)
    absorbed = absorbed.reshape(LAYERS * HEADS * QUERIES, WIDTH) / math.sqrt(HEAD_DIM)

    scores = jnp.where(live_keys[None, :], small_dot(absorbed, keys, 1, 1), -1e30)
    exps = jnp.exp(scores - jnp.max(scores, axis=1, keepdims=True))
    probs = exps / jnp.sum(exps, axis=1, keepdims=True)
    probs = probs.reshape(LAYERS, HEADS, QUERIES, -1)
    pooled = jnp.mean(probs, axis=2).reshape(LAYERS * HEADS, -1)
    pooled_keys = small_dot(pooled, keys)

    frame_pack_1, frame_whole_0, pooled_keys = tie(frame_packs[1], frame_whole_0, pooled_keys)
    frame_whole_1 = lax.all_gather(frame_pack_1, AXIS, axis=0, tiled=False)

    (pooled_cut,) = exchange(by_column(pooled_keys, devices))
    pooled_cut = pooled_cut.reshape(devices, LAYERS, HEADS, share)
    pooled_cut, frame_whole_0, frames_in, conditioning = tie(pooled_cut, frame_whole_0, frames_in, conditioning)
    value_heads = value_proj.reshape(LAYERS, share, HEADS, HEAD_DIM)
    mean_part = jnp.einsum("blhw,lwhe->blhe", pooled_cut, value_heads, precision=HIGHEST)
    (mean_cut,) = exchange(by_column(mean_part.reshape(devices, LAYERS, WIDTH), devices))
    mean_cut = jnp.sum(mean_cut, axis=0).reshape(devices, LAYERS, share)
    mixed_part = jnp.einsum("blw,lwx->blx", mean_cut, mixing_proj, precision=HIGHEST)
    (mixed_cut,) = exchange(by_column(mixed_part, devices))
    mixed_cut = jnp.sum(mixed_cut, axis=0).reshape(devices, LAYERS, share)
    film_part = jnp.einsum("blw,lwx->blx", mixed_cut, film_proj, precision=HIGHEST)
    (films,) = exchange(film_part)
    films = jnp.sum(films, axis=0).reshape(LAYERS, 1, GATES)
    films, cot_frames, cot_skip = tie(films, cot_frames, cot_skip)

    live = (jnp.arange(frames_in.shape[1], dtype=jnp.int32) < item_lengths[0]).astype(jnp.float32)[:, None]
    embed = step_embedding(diffusion_steps[0])[None, :]
    embed_pairs = embed.reshape(-1, 2).T
    frames, cond, cot, cot_last = frames_in[0], conditioning[0], cot_frames[0], cot_skip[0]
    if devices != PARTS:
        frame_whole_0 = regrouped(frame_whole_0, share)
    tanh_0, sig_0, step_row_0 = layer_gates(frame_whole_0, frames, cond, embed_pairs, live, 1)
    frames_1, skip = layer_post(frame_whole_0, tanh_0, sig_0, films[0], frames, jnp.zeros_like(frames), live)

    attention_pack = jnp.concatenate(
        [
            part
            for layer in range(LAYERS)
            for part in (film_proj[layer], jnp.concatenate([value_proj[layer], mixing_proj[layer]], axis=1))
        ],
        axis=0,
    )
    attention_pack, frame_whole_1, frames_1 = tie(attention_pack, frame_whole_1, frames_1)
    attention_whole = lax.all_gather(attention_pack, AXIS, axis=0, tiled=False)
    attention_whole = attention_whole.reshape(devices, LAYERS, 2, share, GATES)
    if devices != PARTS:
        attention_whole = jnp.transpose(attention_whole, (1, 2, 0, 3, 4)).reshape(1, LAYERS, 2, WIDTH, GATES)
        frame_whole_1 = regrouped(frame_whole_1, share)

    tanh_1, sig_1, step_row_1 = layer_gates(frame_whole_1, frames_1, cond, embed_pairs, live, 2)

    def by_device(grad):
        return grad.reshape(devices, -1, GATES)

    def by_share(grad):
        return grad.reshape(devices, share, -1)

    grad_pre_1, grad_film_1, grad_out = layer_back_gates(frame_whole_1, tanh_1, sig_1, films[1], cot, cot_last, live)
    sum_2 = RowSum([by_device(grad_out)], pairs)

    def weights_1(grad_pre):
        return layer_back_weights(frames_1, cond, step_row_1, live, grad_pre, 2), grad_pre

    (grad_conv, grad_cond), grad_pre_1 = beside([sum_2], weights_1, grad_pre_1)
    sum_1 = RowSum([by_device(grad_conv), by_device(grad_cond)], pairs)

    def post_1(tanh, sig, grad_pre):
        return layer_post(frame_whole_1, tanh, sig, films[1], frames_1, skip, live), grad_pre

    (frames, skip), grad_pre_1 = beside([sum_1], post_1, tanh_1, sig_1, grad_pre_1)
    sum_1.add(sum_2)
    sum_1.join()
    sum_1.halve()

    def frames_and_gates(grad_pre):
        grad_frames, step_sum = layer_back_frames(frame_whole_1, grad_pre, cot, live, 2)
        gates = layer_back_gates(frame_whole_0, tanh_0, sig_0, films[0], grad_frames, cot_last, live)
        return grad_frames, step_sum, *gates

    grad_frames, step_sum_1, grad_pre_0, grad_film_0, grad_out = beside([sum_1], frames_and_gates, grad_pre_1)
    sum_a = RowSum([by_device(grad_out)], pairs)

    def weights_0(grad_pre):
        return layer_back_weights(frames_in[0], cond, step_row_0, live, grad_pre, 1), grad_pre

    (grad_conv, grad_cond), grad_pre_0 = beside([sum_1, sum_a], weights_0, grad_pre_0)
    sum_1.join()
    sum_b = RowSum([by_device(grad_conv), by_device(grad_cond)], pairs)
    key_w = query_key[:, :, WIDTH:]

    def attention_1(grad_film):
        return attention_back(1, grad_film, attention_whole, key_w, probs, keys)

    grad_film_0, grad_film_1 = grad_film_0.reshape(1, GATES), grad_film_1.reshape(1, GATES)
    absorbed_1, query_1, row_1, mixed_1 = beside([sum_b, sum_1], attention_1, grad_film_1)
    sum_b.add(sum_a)
    sum_b.join()
    sum_b.halve()

    def attention_and_frames(grad_film, grad_pre):
        attention = attention_back(0, grad_film, attention_whole, key_w, probs, keys)
        return *attention, *layer_back_frames(frame_whole_0, grad_pre, grad_frames, live, 1)

    absorbed_0, query_0, row_0, mixed_0, grad_frames, step_sum_0 = beside(
        [sum_b, sum_1], attention_and_frames, grad_film_0, grad_pre_0
    )
    sum_d = RowSum([by_share(absorbed_0), by_share(absorbed_1)], pairs, far_first=True)
    sum_d.step()
    query_parts = jnp.stack([query_0, query_1]).reshape(devices, -1)
    (query_cut,) = beside([sum_d, sum_b], exchange, query_parts)
    query_cut = jnp.sum(query_cut, axis=0)
    sum_d.step()
    sum_b.join()
    parts = (row_0, row_1, mixed_0, mixed_1, grad_film_0, grad_film_1, step_sum_0, step_sum_1, query_cut)
    whole_rows = jnp.concatenate([part.reshape(-1) for part in parts])
    rows, own_embeds = beside([sum_d, sum_b], exchange, to_all(whole_rows, devices), by_column(embed, devices))
    while sum_d.at < len(pairs):
        sum_d.step()
    sum_d.join()
    query_start = whole_rows.size - query_cut.size
    query_grads = rows[:, query_start:].reshape(LAYERS, QUERIES, WIDTH)
    absorbed_sums = sum_d.result().reshape(LAYERS, share, HEADS * QUERIES)

    small = [(LAYERS, share, columns) for columns in (WIDTH, QUERIES, WIDTH, WIDTH, WIDTH, WIDTH, GATES)]
    *factored, square = pl.pallas_call(factor_kernel, out_shape=shapes_of(*small, (1, 1)))(
        rows[:, :query_start],
        jnp.moveaxis(pooled_cut.reshape(devices, LAYERS, HEADS * share), 1, 0),
        jnp.moveaxis(mean_cut, 1, 0),
        jnp.moveaxis(mixed_cut, 1, 0),
        own_embeds,
        absorbed_sums,
        jnp.stack([query_rows, query_grads]),
        query_seeds,
        query_proj,
    )
    frame_sums = (sum_b.result(), sum_1.result())
    squares = pl.pallas_call(square_kernel, out_shape=shapes_of((devices, 8, 128))[0])(square, *frame_sums)
    squares = lax.all_to_all(squares, AXIS, split_axis=0, concat_axis=0, tiled=True)
    frame_shapes = [(LAYERS, rows_of * share, GATES) for rows_of in (3, 1, 1)]
    outs = pl.pallas_call(clip_kernel, out_shape=shapes_of(*small, *frame_shapes))(squares, *frame_sums, *factored)
    step_grad, seeds_grad, query_grad, key_grad, value_grad, mixing_grad, film_grad, conv_grad, cond_grad, out_grad = outs
    return (
        frames[None],
        skip[None],
        grad_frames[None],
        step_grad,
        conv_grad,
        cond_grad,
        out_grad,
        seeds_grad,
        query_grad,
        key_grad,
        value_grad,
        mixing_grad,
        film_grad,
    )


def solution(mesh):
    devices = mesh.shape[AXIS]

    def run(*args):
        return on_device(*args, devices=devices)

    items, rows = P(AXIS, None, None), P(None, AXIS, None)
    return jax.shard_map(
        run,
        mesh=mesh,
        in_specs=(items, items, rows, P(AXIS), P(), P(None, AXIS), P(AXIS)) + (rows,) * 10 + (items, items),
        out_specs=(items,) * 3 + (rows,) * 10,
        check_vma=False,
    )
```

time: 727 us -> 610 us (0.84)
  matrix products: 218 us -> 12 us
  Pallas kernels: 0 us -> 195 us
  local copies, waits for them, and re-layouts: 164 us -> 75.8 us
  other arithmetic: 82.5 us -> 66.9 us
  blocking collectives: 0 us -> 13.1 us
  between operations: 24.4 us -> 16.7 us
    pallas_call x0 -> x15, Pallas kernels: none -> 195 us  [the longest x2 41.6 us: layer_gates(): kernel_call(functools.partial(gates_kernel, dilation), (3,), [fixed(count...]
    dot_general x25 -> x0, matrix products: 176 us -> none  [the longest x16 160 us: big_dot(): lax.dot_general(left, right, (((left_dim,), (right_dim,)), ((), ())), pre...]
    ppermute x29 -> x36, waiting for transfers between devices: 121 us -> 69.2 us  [shift(): return lax.ppermute(block, AXIS, perm)]
    all_to_all x6, waiting for transfers between devices: 12.4 us -> 43.3 us  [exchange(): lax.all_to_all(joined, AXIS, split_axis=0, concat_axis=0, tiled=True)]
    slice x17 -> x4, local copies, waits for them, and re-layouts: 31.7 us -> 1.11 us  [the longest x1 0.89 us: on_device(): rows[:, :query_start]]
    dot_general x14 -> x2, matrix products: 34.5 us -> 4.82 us  [small_dot(): lax.dot_general(left, right, (((left_dim,), (right_dim,)), ((), ())), pre...]
    all_gather x1, waiting for transfers between devices: 0.02 us -> 20.5 us  [on_device(): frame_whole_1 = lax.all_gather(frame_pack_1, AXIS, axis=0, tiled=False)]
    unnamed x198 -> x135, local copies, waits for them, and re-layouts: 45.4 us -> 27.3 us
  transfers between devices with their start and end apart: 40 -> 46, of which waited for: 17 -> 18; matrix products, arithmetic and copies ran while one was open for 60% -> 20% of each run, Pallas kernels for 0% -> 31%
where the time goes in v2:
time: 610 us; the launch traced here: 605 us
  Pallas kernels  195 us (32%)
  waiting for transfers between devices  155 us (25%)
  local copies, waits for them, and re-layouts  75.8 us (12%)
  starting transfers between devices  70.1 us (11%)
  other arithmetic  66.9 us (11%)
  between operations  16.7 us (3%)
  blocking collectives  13.1 us (2%)
  matrix products  12 us (2%)
    ppermute x36, waiting for transfers between devices, shift(): return lax.ppermute(block, AXIS, perm)  69.2 us
    all_to_all x6, waiting for transfers between devices, exchange(): lax.all_to_all(joined, AXIS, split_axis=0, concat_axis=0, tiled=True)  43.3 us
    ppermute x36, starting transfers between devices, shift(): return lax.ppermute(block, AXIS, perm)  41.7 us
    pallas_call x2, Pallas kernels, layer_gates(): kernel_call(functools.partial(gates_kernel, dilation), (3,), [fixed(count...  41.6 us
    pallas_call x2, Pallas kernels, layer_back_weights(): kernel_call(functools.partial(back_weights_kernel, dilation), (GATES // T...  41.2 us
    pallas_call x2, Pallas kernels, layer_back_frames(): kernel_call(functools.partial(back_frames_kernel, dilation), (2,), [fixed...  35.9 us
    unnamed x135, local copies, waits for them, and re-layouts  27.3 us
    pallas_call x2, Pallas kernels, layer_back_gates(): kernel_call(back_gates_kernel, (2,), [rows, rows, pl.BlockSpec((count //...  27.2 us
  transfers between devices with their start and end apart: 46, of which 18 were waited for; matrix products, arithmetic and copies ran while one was open for 20% of the time, Pallas kernels for 31%

profile of v2, /device:TPU:0, one launch (start us, length us, event | category | flops | bytes accessed | tf_op | source)
XLA Modules:
  0.0 604.9 jit_solution(9203113119954077935)
XLA Ops:
  10.8 2.6 copy.91
  15.5 3.0 collective-permute-start
  18.6 2.6 collective-permute-start.1
  22.5 2.5 collective-permute-done
  25.1 8.7 %collective-permute-done.1 = f32[32,1024]{1,0:T(8,128)S(1)} collective-permute-done((f32[32,1024]{1,0:T(8,128)S(1)}, f32[32,1024]{1,0:T(8,128)S(1)}, u32[]{:S(2)}, u32[]{:S(2)}) %collective-permute-start.1) | collective-permute-done | bytes 131104 | tf_op jit(solution)/shard_map/ppermute | solution.py:50
  37.5 7.7 %all-to-all-start = ((f32[32,32,512]{2,1,0:T(8,128)}), f32[32,32,512]{2,1,0:T(8,128)S(1)}, u32[]{:S(2)}, u32[]{:S(2)}) async-start(f32[32,32,512]{2,1,0:T(8,128)} %pad_maximum_fusion.9), calls=%async_computation | async-start | bytes 4194304 | tf_op jit(solution)/shard_map/all_to_all | solution.py:641
  50.1 39.1 %collective-permute-done.6 = f32[2,4,16,1024]{3,2,0,1:T(8,128)S(1)} collective-permute-done((f32[2,4,16,1024]{3,2,0,1:T(8,128)S(1)}, f32[2,4,16,1024]{3,2,0,1:T(8,128)S(1)}, u32[]{:S(2)}, u32[]{:S(2)}) %collective-permute-start.6) | collective-permute-done | bytes 524320 | tf_op jit(solution)/shard_map/ppermute | solution.py:50
  92.6 3.1 collective-permute-done.7
  95.7 2.4 select_bitcast_fusion.1
  99.1 2.1 copy-done.1
  102.8 2.9 copy.99
  105.7 21.4 %all-to-all-done = f32[32,32,512]{2,1,0:T(8,128)S(1)} async-done(((f32[32,32,512]{2,1,0:T(8,128)}), f32[32,32,512]{2,1,0:T(8,128)S(1)}, u32[]{:S(2)}, u32[]{:S(2)}) %all-to-all-start) | async-done | bytes 2097184 | tf_op jit(solution)/shard_map/all_to_all | solution.py:641
  127.5 3.2 fusion
  131.7 2.8 convolution_multiply_fusion
  134.5 3.7 select_reduce_fusion
  138.7 2.1 bitcast_reduce_fusion
  143.9 3.8 all-to-all-start.1
  148.5 7.4 %all-to-all-done.1 = f32[32,8,128]{2,1,0:T(8,128)S(1)} async-done(((f32[32,8,128]{2,1,0:T(8,128)}), f32[32,8,128]{2,1,0:T(8,128)S(1)}, u32[]{:S(2)}, u32[]{:S(2)}) %all-to-all-start.1) | async-done | bytes 131104 | tf_op jit(solution)/shard_map/all_to_all | solution.py:177
  158.3 2.6 all-to-all-start.2
  161.0 8.9 %all-to-all-done.2 = f32[32,8,128]{2,1,0:T(8,128)S(1)} async-done(((f32[32,8,128]{2,1,0:T(8,128)}), f32[32,8,128]{2,1,0:T(8,128)S(1)}, u32[]{:S(2)}, u32[]{:S(2)}) %all-to-all-start.2) | async-done | bytes 131104 | tf_op jit(solution)/shard_map/all_to_all | solution.py:177
  172.0 2.9 all-to-all-start.3
  177.8 7.7 %all-to-all-done.3 = f32[32,8,128]{2,1,0:T(8,128)S(1)} async-done(((f32[32,8,128]{2,1,0:T(8,128)}), f32[32,8,128]{2,1,0:T(8,128)S(1)}, u32[]{:S(2)}, u32[]{:S(2)}) %all-to-all-start.3) | async-done | bytes 131104 | tf_op jit(solution)/shard_map/all_to_all | solution.py:177
  187.7 3.4 all-to-all-start.4
  191.1 20.6 %shard_map.282 = (f32[1024,512]{1,0:T(8,128)}, f32[1024,512]{1,0:T(8,128)}, f32[1,512]{1,0:T(1,128)}) custom-call(f32[1024,512]{1,0:T(8,128)} %bitcast.467, f32[1024,512]{1,0:T(8,128)} %bitcast.521, f32[32,88,1024]{2,1,0:T(8,128)} %bitcast.437, f32[32,88,1024]{2,1,0:T(8,128)} %bitcast.438, f32[32,88,1024]{2,1,0:T(8,128)} %bitcast.439, ...), custom_call_target="tpu_custom_call" | custom-call | flops 12884901888 | bytes 16777216 | tf_op jit(solution)/shard_map/pallas_call | solution.py:425
  214.0 7.9 %shard_map.283 = (f32[1024,512]{1,0:T(8,128)}, f32[1024,512]{1,0:T(8,128)}) custom-call(f32[1024,512]{1,0:T(8,128)} %get-tuple-element.189.tanh, f32[1024,512]{1,0:T(8,128)} %get-tuple-element.190.sig, f32[2,512]{1,0:T(2,128)} %reshape_squeeze.16.film, f32[32,88,1024]{2,1,0:T(8,128)} %bitcast.440, f32[1024,512]{1,0:T(8,128)} %bitcast.468, ...), custom_call_target="tpu_custom_call" | custom-call | flops 3221225472 | bytes 16777216 | tf_op jit(solution)/shard_map/pallas_call | solution.py:456
  221.9 20.5 %all-gather.9.cloned.1.call-done = f32[2816,1024]{1,0:T(8,128)} async-done(((f32[88,1024]{1,0:T(8,128)}), f32[2816,1024]{1,0:T(8,128)}) %all-gather.9.cloned.1.call-update) | async-done | bytes 11534352 | tf_op jit(solution)/shard_map/all_gather | solution.py:674
  243.1 21.0 %shard_map.284 = (f32[1024,512]{1,0:T(8,128)}, f32[1024,512]{1,0:T(8,128)}, f32[1,512]{1,0:T(1,128)}) custom-call(f32[1024,512]{1,0:T(8,128)} %get-tuple-element.193.frames, f32[1024,512]{1,0:T(8,128)} %bitcast.522, f32[32,88,1024]{2,1,0:T(8,128)} %bitcast.443, f32[32,88,1024]{2,1,0:T(8,128)} %bitcast.444, f32[32,88,1024]{2,1,0:T(8,128)} %bitcast.445, ...), custom_call_target="tpu_custom_call" | custom-call | flops 12884901888 | bytes 16777216 | tf_op jit(solution)/shard_map/pallas_call | solution.py:425
  264.1 13.5 %shard_map.285 = (f32[1024,1024]{1,0:T(8,128)}, f32[2,512]{1,0:T(2,128)}, f32[512,1024]{1,0:T(8,128)}) custom-call(f32[1024,512]{1,0:T(8,128)} %bitcast.517, f32[1024,512]{1,0:T(8,128)} %bitcast.519, f32[1024,1]{1,0:T(8,128)} %fusion.35.live, f32[1024,512]{1,0:T(8,128)} %get-tuple-element.212.tanh, f32[1024,512]{1,0:T(8,128)} %get-tuple-element.213.sig, ...), custom_call_target="tpu_custom_call" | custom-call | flops 6442450944 | bytes 16777216 | tf_op jit(solution)/shard_map/pallas_call | solution.py:504
  277.6 2.8 dynamic-slice_bitcast_fusion.8
  280.6 20.5 %shard_map.286 = (f32[1536,1024]{1,0:T(8,128)}, f32[512,1024]{1,0:T(8,128)}) custom-call(f32[1024,512]{1,0:T(8,128)} %get-tuple-element.193.frames, f32[1024,512]{1,0:T(8,128)} %bitcast.523, f32[1,512]{1,0:T(1,128)} %get-tuple-element.200.step_row, f32[1024,1]{1,0:T(8,128)} %fusion.35.live, f32[1024,1024]{1,0:T(8,128)} %get-tuple-element.227.grad_pre), custom_call_target="tpu_custom_call" | custom-call | flops 12884901888 | bytes 16777216 | tf_op jit(solution)/shard_map/pallas_call | solution.py:543
  302.1 5.6 dynamic-slice_bitcast_fusion.2
  310.4 8.1 %shard_map.287 = (f32[1024,512]{1,0:T(8,128)}, f32[1024,512]{1,0:T(8,128)}) custom-call(f32[1024,512]{1,0:T(8,128)} %get-tuple-element.212.tanh, f32[1024,512]{1,0:T(8,128)} %get-tuple-element.213.sig, f32[2,512]{1,0:T(2,128)} %reshape_squeeze.17.film, f32[32,88,1024]{2,1,0:T(8,128)} %bitcast.447, f32[1024,512]{1,0:T(8,128)} %get-tuple-element.193.frames, ...), custom_call_target="tpu_custom_call" | custom-call | flops 3221225472 | bytes 16777216 | tf_op jit(solution)/shard_map/pallas_call | solution.py:456
  318.5 2.3 pad_maximum_fusion.7
  320.9 4.0 copy.119
  332.7 17.6 %shard_map.288 = (f32[1024,512]{1,0:T(8,128)}, f32[1,512]{1,0:T(1,128)}) custom-call(f32[1024,1024]{1,0:T(8,128)} %get-tuple-element.227.grad_pre, f32[32,88,1024]{2,1,0:T(8,128)} %bitcast.448, f32[1024,512]{1,0:T(8,128)} %bitcast.518, f32[1024,1]{1,0:T(8,128)} %fusion.35.live), custom_call_target="tpu_custom_call" | custom-call | flops 9663676416 | bytes 16777216 | tf_op jit(solution)/shard_map/pallas_call | solution.py:586
  350.3 13.7 %shard_map.289 = (f32[1024,1024]{1,0:T(8,128)}, f32[2,512]{1,0:T(2,128)}, f32[512,1024]{1,0:T(8,128)}) custom-call(f32[1024,512]{1,0:T(8,128)} %get-tuple-element.281.grad_frames, f32[1024,512]{1,0:T(8,128)} %bitcast.520, f32[1024,1]{1,0:T(8,128)} %fusion.35.live, f32[1024,512]{1,0:T(8,128)} %get-tuple-element.189.tanh, f32[1024,512]{1,0:T(8,128)} %get-tuple-element.190.sig, ...), custom_call_target="tpu_custom_call" | custom-call | flops 6442450944 | bytes 16777216 | tf_op jit(solution)/shard_map/pallas_call | solution.py:504
  364.1 2.6 fusion.32
  366.7 2.5 fusion.30
  372.2 20.7 %shard_map.290 = (f32[1536,1024]{1,0:T(8,128)}, f32[512,1024]{1,0:T(8,128)}) custom-call(f32[1024,512]{1,0:T(8,128)} %bitcast.469, f32[1024,512]{1,0:T(8,128)} %bitcast.524, f32[1,512]{1,0:T(1,128)} %get-tuple-element.242.step_row, f32[1024,1]{1,0:T(8,128)} %fusion.35.live, f32[1024,1024]{1,0:T(8,128)} %get-tuple-element.280.grad_pre), custom_call_target="tpu_custom_call" | custom-call | flops 12884901888 | bytes 16777216 | tf_op jit(solution)/shard_map/pallas_call | solution.py:543
  394.4 3.4 dynamic-slice_bitcast_fusion
  399.8 2.8 dynamic-slice_bitcast_fusion.5
  411.6 4.6 pad_maximum_fusion.3
  416.1 12.3 %shard_map.291 = (f32[512,256]{1,0:T(8,128)}, f32[32,512]{1,0:T(8,128)}, f32[1,512]{1,0:T(1,128)}, f32[1,512]{1,0:T(1,128)}) custom-call(f32[1,1024]{1,0:T(1,128)} %bitcast.503, f32[32,2,2,16,1024]{4,3,2,1,0:T(8,128)} %bitcast.424, f32[32,2,2,16,1024]{4,3,2,1,0:T(8,128)} %bitcast.425, f32[2,512,512]{2,1,0:T(8,128)} %slice.154.key_w, ...), custom_call_target="tpu_custom_call" | custom-call | flops 2013265920 | bytes 16777216 | tf_op jit(solution)/shard_map/pallas_call | solution.py:251
  430.7 3.2 pad_maximum_fusion.1
  435.2 2.4 copy-done.4
  442.4 18.3 %shard_map.293 = (f32[1024,512]{1,0:T(8,128)}, f32[1,512]{1,0:T(1,128)}) custom-call(f32[1024,1024]{1,0:T(8,128)} %get-tuple-element.280.grad_pre, f32[32,88,1024]{2,1,0:T(8,128)} %bitcast.442, f32[1024,512]{1,0:T(8,128)} %get-tuple-element.281.grad_frames, f32[1024,1]{1,0:T(8,128)} %fusion.35.live), custom_call_target="tpu_custom_call" | custom-call | flops 9663676416 | bytes 16777216 | tf_op jit(solution)/shard_map/pallas_call | solution.py:586
  460.7 12.2 %shard_map.292 = (f32[512,256]{1,0:T(8,128)}, f32[32,512]{1,0:T(8,128)}, f32[1,512]{1,0:T(1,128)}, f32[1,512]{1,0:T(1,128)}) custom-call(f32[1,1024]{1,0:T(1,128)} %bitcast.504, f32[32,2,2,16,1024]{4,3,2,1,0:T(8,128)} %bitcast.426, f32[32,2,2,16,1024]{4,3,2,1,0:T(8,128)} %bitcast.427, f32[2,512,512]{2,1,0:T(8,128)} %slice.154.key_w, ...), custom_call_target="tpu_custom_call" | custom-call | flops 2013265920 | bytes 16777216 | tf_op jit(solution)/shard_map/pallas_call | solution.py:251
  479.7 2.5 fusion.23
  482.2 2.3 fusion.25
  492.0 3.3 all-to-all-start.5
  501.2 4.4 all-to-all-done.5
  507.3 2.0 fusion.33
  509.3 2.4 fusion.21
  512.6 2.0 collective-permute-start.30
  524.5 4.4 all-to-all-start.6
  537.6 14.9 %all-to-all-done.6 = f32[32,56,128]{2,1,0:T(8,128)S(1)} async-done(((f32[32,56,128]{2,1,0:T(8,128)}), f32[32,56,128]{2,1,0:T(8,128)S(1)}, u32[]{:S(2)}, u32[]{:S(2)}) %all-to-all-start.6) | async-done | bytes 917536 | tf_op jit(solution)/shard_map/all_to_all | solution.py:177
  553.3 7.4 %collective-permute-done.32 = f32[2,80,1024]{2,1,0:T(8,128)} collective-permute-done((f32[2,80,1024]{2,1,0:T(8,128)}, f32[2,80,1024]{2,1,0:T(8,128)}, u32[]{:S(2)}, u32[]{:S(2)}) %collective-permute-start.32) | collective-permute-done | bytes 655392 | tf_op jit(solution)/shard_map/ppermute | solution.py:50
  561.9 2.5 collective-permute-start.35
  569.2 2.2 collective-permute-done.34
  572.1 3.5 shard_map.294
  575.5 3.6 collective-permute-done.35
  580.0 2.6 shard_map.295
  582.6 13.1 %all_to_all.40.squares = f32[32,8,128]{2,1,0:T(8,128)} all-to-all(f32[32,8,128]{2,1,0:T(8,128)} %shard_map.295), channel_id=1, replica_groups=mesh['items'=32] {'items'}, dimensions={0} | all-to-all | bytes 262144 | tf_op jit(solution)/shard_map/all_to_all | solution.py:803
  595.7 2.4 shard_map.296
  (332 shorter events, 123.2 us)
Async XLA Ops:
  7.2 135.6 %all-gather.7.cloned.1.call-start = ((), (), s32[]{:S(2)}) async-start(), calls=%async_computation.8 | async-start | bytes 11894784 | tf_op jit(solution)/shard_map/all_gather | solution.py:632
  15.5 9.5 %collective-permute-start = (f32[32,1024]{1,0:T(8,128)S(1)}, f32[32,1024]{1,0:T(8,128)S(1)}, u32[]{:S(2)}, u32[]{:S(2)}) collective-permute-start(f32[32,1024]{1,0:T(8,128)S(1)} %bitcast.477), channel_id=1, source_target_pairs={{0,8},{1,9},{2,10},{3,11},{4,12},{5,13},{6,14},{7,15},{8,16},{9,17... | collective-permute-start | bytes 393224 | tf_op jit(solution)/shard_map/ppermute | solution.py:50
  18.6 15.2 %collective-permute-start.1 = (f32[32,1024]{1,0:T(8,128)S(1)}, f32[32,1024]{1,0:T(8,128)S(1)}, u32[]{:S(2)}, u32[]{:S(2)}) collective-permute-start(f32[32,1024]{1,0:T(8,128)S(1)} %bitcast.478), channel_id=1, source_target_pairs={{0,16},{1,17},{2,18},{3,19},{4,20},{5,21},{6,22},{7,23},{8,24},{9,... | collective-permute-start | bytes 393224 | tf_op jit(solution)/shard_map/ppermute | solution.py:50
  21.2 12.7 %collective-permute-start.2 = (f32[32,1024]{1,0:T(8,128)S(1)}, f32[32,1024]{1,0:T(8,128)S(1)}, u32[]{:S(2)}, u32[]{:S(2)}) collective-permute-start(f32[32,1024]{1,0:T(8,128)S(1)} %bitcast.479), channel_id=1, source_target_pairs={{0,24},{1,25},{2,26},{3,27},{4,28},{5,29},{6,30},{7,31},{8,0},{9,1... | collective-permute-start | bytes 393224 | tf_op jit(solution)/shard_map/ppermute | solution.py:50
  33.9 11.6 %collective-permute-start.3 = (f32[4,16,1024]{2,1,0:T(8,128)S(1)}, f32[4,16,1024]{2,1,0:T(8,128)}, u32[]{:S(2)}, u32[]{:S(2)}) collective-permute-start(f32[4,16,1024]{2,1,0:T(8,128)S(1)} %get-tuple-element.377), channel_id=1, source_target_pairs={{0,2},{1,3},{2,0},{3,1},{4,6},{5,7},{6,4},{7,5},{8,10},{9,11},{10,... | collective-permute-start | bytes 786440 | tf_op jit(solution)/shard_map/ppermute | solution.py:50
  35.7 9.8 %collective-permute-start.5 = (f32[4,16,1024]{2,1,0:T(8,128)S(1)}, f32[4,16,1024]{2,1,0:T(8,128)}, u32[]{:S(2)}, u32[]{:S(2)}) collective-permute-start(f32[4,16,1024]{2,1,0:T(8,128)S(1)} %get-tuple-element.378), channel_id=1, source_target_pairs={{0,4},{1,5},{2,6},{3,7},{4,0},{5,1},{6,2},{7,3},{8,12},{9,13},{10,... | collective-permute-start | bytes 786440 | tf_op jit(solution)/shard_map/ppermute | solution.py:50
  37.5 89.6 %all-to-all-start = ((f32[32,32,512]{2,1,0:T(8,128)}), f32[32,32,512]{2,1,0:T(8,128)S(1)}, u32[]{:S(2)}, u32[]{:S(2)}) async-start(f32[32,32,512]{2,1,0:T(8,128)} %pad_maximum_fusion.9), calls=%async_computation | async-start | bytes 4194304 | tf_op jit(solution)/shard_map/all_to_all | solution.py:641
  45.2 197.2 %all-gather.9.cloned.1.call-start = ((), (), s32[]{:S(2)}) async-start(), calls=%async_computation.9 | async-start | bytes 11894784 | tf_op jit(solution)/shard_map/all_gather | solution.py:674
  46.8 42.4 %collective-permute-start.6 = (f32[2,4,16,1024]{3,2,0,1:T(8,128)S(1)}, f32[2,4,16,1024]{3,2,0,1:T(8,128)S(1)}, u32[]{:S(2)}, u32[]{:S(2)}) collective-permute-start(f32[2,4,16,1024]{3,2,0,1:T(8,128)S(1)} %pad_maximum_fusion.12), channel_id=1, source_target_pairs={{0,2},{1,3},{2,0},{3,1},{4,6},{5,7},{6,4},{7,5},{8,10},{9,11},{10,... | collective-permute-start | bytes 1572872 | tf_op jit(solution)/shard_map/ppermute | solution.py:50
  48.6 40.8 %collective-permute-start.4 = (f32[2,4,16,1024]{3,2,1,0:T(8,128)S(1)}, f32[2,4,16,1024]{3,2,1,0:T(8,128)S(1)}, u32[]{:S(2)}, u32[]{:S(2)}) collective-permute-start(f32[2,4,16,1024]{3,2,1,0:T(8,128)S(1)} %pad_maximum_fusion.11), channel_id=1, source_target_pairs={{0,4},{1,5},{2,6},{3,7},{4,0},{5,1},{6,2},{7,3},{8,12},{9,13},{10,... | collective-permute-start | bytes 1572872 | tf_op jit(solution)/shard_map/ppermute | solution.py:50
  91.2 4.5 collective-permute-start.7
  127.1 13.7 %copy-start = (f32[32,32,512]{2,1,0:T(8,128)}, f32[32,32,512]{2,1,0:T(8,128)S(1)}, u32[]{:S(2)}) copy-start(f32[32,32,512]{2,1,0:T(8,128)S(1)} %all-to-all-done) | copy-start | bytes 6291460
  130.8 7.4 %copy-start.25 = (f32[2,32,512]{2,1,0:T(8,128)}, f32[2,32,512]{2,1,0:T(8,128)S(1)}, u32[]{:S(2)}) copy-start(f32[2,32,512]{2,1,0:T(8,128)S(1)} %fusion) | copy-start | bytes 393220
  140.8 7.6 %copy-start.44 = (f32[2,16,512]{2,1,0:T(8,128)S(1)}, f32[2,16,512]{2,1,0:T(8,128)}, u32[]{:S(2)}) copy-start(f32[2,16,512]{2,1,0:T(8,128)} %param.33) | copy-start | bytes 196612
  140.8 7.7 %copy-start.45 = (f32[2,16,512]{2,1,0:T(8,128)S(1)}, f32[2,16,512]{2,1,0:T(8,128)}, u32[]{:S(2)}) copy-start(f32[2,16,512]{2,1,0:T(8,128)} %param.34) | copy-start | bytes 196612
  143.9 12.1 %all-to-all-start.1 = ((f32[32,8,128]{2,1,0:T(8,128)}), f32[32,8,128]{2,1,0:T(8,128)S(1)}, u32[]{:S(2)}, u32[]{:S(2)}) async-start(f32[32,8,128]{2,1,0:T(8,128)} %copy.102), calls=%async_computation.1 | async-start | bytes 262144 | tf_op jit(solution)/shard_map/all_to_all | solution.py:177
  148.4 12.6 %copy-start.38 = (f32[2,16,1024]{2,1,0:T(8,128)S(1)}, f32[2,16,1024]{2,1,0:T(8,128)}, u32[]{:S(2)}) copy-start(f32[2,16,1024]{2,1,0:T(8,128)} %param.35) | copy-start | bytes 393220
  158.3 11.6 %all-to-all-start.2 = ((f32[32,8,128]{2,1,0:T(8,128)}), f32[32,8,128]{2,1,0:T(8,128)S(1)}, u32[]{:S(2)}, u32[]{:S(2)}) async-start(f32[32,8,128]{2,1,0:T(8,128)} %copy.107), calls=%async_computation.2 | async-start | bytes 262144 | tf_op jit(solution)/shard_map/all_to_all | solution.py:177
  172.0 13.4 %all-to-all-start.3 = ((f32[32,8,128]{2,1,0:T(8,128)}), f32[32,8,128]{2,1,0:T(8,128)S(1)}, u32[]{:S(2)}, u32[]{:S(2)}) async-start(f32[32,8,128]{2,1,0:T(8,128)} %copy.111), calls=%async_computation.3 | async-start | bytes 262144 | tf_op jit(solution)/shard_map/all_to_all | solution.py:177
  187.7 24.0 %all-to-all-start.4 = ((f32[32,16,128]{2,1,0:T(8,128)}), f32[32,16,128]{2,1,0:T(8,128)S(1)}, u32[]{:S(2)}, u32[]{:S(2)}) async-start(f32[32,16,128]{2,1,0:T(8,128)} %reshape.296), calls=%async_computation.4 | async-start | bytes 524288 | tf_op jit(solution)/shard_map/all_to_all | solution.py:177
  191.0 225.1 %all-gather.11.cloned.1.call-start = ((), (), s32[]{:S(2)}) async-start(), calls=%async_computation.10 | async-start | bytes 8650752 | tf_op jit(solution)/shard_map/all_gather | solution.py:709
  280.3 20.8 %collective-permute-start.8 = (f32[2,2,2,2,16,1024]{5,4,3,2,1,0:T(8,128)S(1)}, f32[2,2,2,2,16,1024]{5,4,3,2,1,0:T(8,128)S(1)}, u32[]{:S(2)}, u32[]{:S(2)}) collective-permute-start(f32[2,2,2,2,16,1024]{5,4,3,2,1,0:T(8,128)S(1)} %get-tuple-element.199), channel_id=1, source_target_pairs={{0,1},{1,0},{2,3},{3,2},{4,5},{5,4},{6,7},{7,6},{8,9},{9,8},{10,11... | collective-permute-start | bytes 3145736 | tf_op jit(solution)/shard_map/ppermute | solution.py:50
  307.7 13.2 %collective-permute-start.9 = (f32[2,2,2,2,48,1024]{5,4,3,2,1,0:T(8,128)}, f32[2,2,2,2,48,1024]{5,4,3,2,1,0:T(8,128)}, u32[]{:S(2)}, u32[]{:S(2)}) collective-permute-start(f32[2,2,2,2,48,1024]{5,4,3,2,1,0:T(8,128)} %get-tuple-element.206), channel_id=1, source_target_pairs={{0,1},{1,0},{2,3},{3,2},{4,5},{5,4},{6,7},{7,6},{8,9},{9,8},{10,11... | collective-permute-start | bytes 9437192 | tf_op jit(solution)/shard_map/ppermute | solution.py:50
  309.5 11.3 %collective-permute-start.10 = (f32[2,2,2,2,16,1024]{5,4,3,2,1,0:T(8,128)}, f32[2,2,2,2,16,1024]{5,4,3,2,1,0:T(8,128)}, u32[]{:S(2)}, u32[]{:S(2)}) collective-permute-start(f32[2,2,2,2,16,1024]{5,4,3,2,1,0:T(8,128)} %get-tuple-element.211), channel_id=1, source_target_pairs={{0,1},{1,0},{2,3},{3,2},{4,5},{5,4},{6,7},{7,6},{8,9},{9,8},{10,11... | collective-permute-start | bytes 3145736 | tf_op jit(solution)/shard_map/ppermute | solution.py:50
  320.8 7.9 %copy-start.8 = (f32[2,2,2,2,40,1024]{5,4,3,2,1,0:T(8,128)}, f32[2,2,2,2,40,1024]{5,4,3,2,1,0:T(8,128)S(1)}, u32[]{:S(2)}) copy-start(f32[2,2,2,2,40,1024]{5,4,3,2,1,0:T(8,128)S(1)} %get-tuple-element.357) | copy-start | bytes 7864324
  325.0 39.0 %copy-start.2 = (f32[2,2,2,2,40,1024]{5,4,1,0,3,2:T(8,128)}, f32[2,2,2,2,40,1024]{5,4,1,0,3,2:T(8,128)S(1)}, u32[]{:S(2)}) copy-start(f32[2,2,2,2,40,1024]{5,4,1,0,3,2:T(8,128)S(1)} %slice.157) | copy-start | bytes 7864324
  330.7 33.3 %collective-permute-start.12 = (f32[2,2,2,40,1024]{4,3,1,0,2:T(8,128)}, f32[2,2,2,40,1024]{4,3,1,0,2:T(8,128)}, u32[]{:S(2)}, u32[]{:S(2)}) collective-permute-start(f32[2,2,2,40,1024]{4,3,1,0,2:T(8,128)} %fusion.6), channel_id=1, source_target_pairs={{0,2},{1,3},{2,0},{3,1},{4,6},{5,7},{6,4},{7,5},{8,10},{9,11},{10,... | collective-permute-start | bytes 3932168 | tf_op jit(solution)/shard_map/ppermute | solution.py:50
  332.1 31.9 %collective-permute-start.11 = (f32[2,2,2,40,1024]{4,3,1,0,2:T(8,128)}, f32[2,2,2,40,1024]{4,3,1,0,2:T(8,128)S(1)}, u32[]{:S(2)}, u32[]{:S(2)}) collective-permute-start(f32[2,2,2,40,1024]{4,3,1,0,2:T(8,128)} %fusion.7), channel_id=1, source_target_pairs={{0,4},{1,5},{2,6},{3,7},{4,0},{5,1},{6,2},{7,3},{8,12},{9,13},{10,... | collective-permute-start | bytes 3932168 | tf_op jit(solution)/shard_map/ppermute | solution.py:50
  370.2 22.7 %collective-permute-start.15 = (f32[2,2,2,2,16,1024]{5,4,3,2,1,0:T(8,128)S(1)}, f32[2,2,2,2,16,1024]{5,4,3,2,1,0:T(8,128)S(1)}, u32[]{:S(2)}, u32[]{:S(2)}) collective-permute-start(f32[2,2,2,2,16,1024]{5,4,3,2,1,0:T(8,128)S(1)} %get-tuple-element.241), channel_id=1, source_target_pairs={{0,1},{1,0},{2,3},{3,2},{4,5},{5,4},{6,7},{7,6},{8,9},{9,8},{10,11... | collective-permute-start | bytes 3145736 | tf_op jit(solution)/shard_map/ppermute | solution.py:50
  370.2 22.7 %collective-permute-start.14 = (f32[2,2,40,1024]{3,2,1,0:T(8,128)}, f32[2,2,40,1024]{3,2,1,0:T(8,128)S(1)}, u32[]{:S(2)}, u32[]{:S(2)}) collective-permute-start(f32[2,2,40,1024]{3,2,1,0:T(8,128)} %fusion.30), channel_id=1, source_target_pairs={{0,4},{1,5},{2,6},{3,7},{4,0},{5,1},{6,2},{7,3},{8,12},{9,13},{10,... | collective-permute-start | bytes 1966088 | tf_op jit(solution)/shard_map/ppermute | solution.py:50
  371.7 21.3 %collective-permute-start.13 = (f32[2,2,40,1024]{3,2,1,0:T(8,128)}, f32[2,2,40,1024]{3,2,1,0:T(8,128)S(1)}, u32[]{:S(2)}, u32[]{:S(2)}) collective-permute-start(f32[2,2,40,1024]{3,2,1,0:T(8,128)} %fusion.32), channel_id=1, source_target_pairs={{0,2},{1,3},{2,0},{3,1},{4,6},{5,7},{6,4},{7,5},{8,10},{9,11},{10,... | collective-permute-start | bytes 1966088 | tf_op jit(solution)/shard_map/ppermute | solution.py:50
  399.7 28.8 %collective-permute-start.16 = (f32[2,2,2,2,48,1024]{5,4,1,0,3,2:T(8,128)}, f32[2,2,2,2,48,1024]{5,4,1,0,3,2:T(8,128)}, u32[]{:S(2)}, u32[]{:S(2)}) collective-permute-start(f32[2,2,2,2,48,1024]{5,4,1,0,3,2:T(8,128)} %copy.131), channel_id=1, source_target_pairs={{0,1},{1,0},{2,3},{3,2},{4,5},{5,4},{6,7},{7,6},{8,9},{9,8},{10,11... | collective-permute-start | bytes 9437192 | tf_op jit(solution)/shard_map/ppermute | solution.py:50
  403.6 24.8 %collective-permute-start.17 = (f32[2,2,2,2,16,1024]{5,4,1,0,3,2:T(8,128)}, f32[2,2,2,2,16,1024]{5,4,1,0,3,2:T(8,128)}, u32[]{:S(2)}, u32[]{:S(2)}) collective-permute-start(f32[2,2,2,2,16,1024]{5,4,1,0,3,2:T(8,128)} %copy.133), channel_id=1, source_target_pairs={{0,1},{1,0},{2,3},{3,2},{4,5},{5,4},{6,7},{7,6},{8,9},{9,8},{10,11... | collective-permute-start | bytes 3145736 | tf_op jit(solution)/shard_map/ppermute | solution.py:50
  408.7 19.7 %collective-permute-start.18 = (f32[2,80,1024]{2,1,0:T(8,128)}, f32[2,80,1024]{2,1,0:T(8,128)}, u32[]{:S(2)}, u32[]{:S(2)}) collective-permute-start(f32[2,80,1024]{2,1,0:T(8,128)} %fusion.18), channel_id=1, source_target_pairs={{0,8},{1,9},{2,10},{3,11},{4,12},{5,13},{6,14},{7,15},{8,0},{9,1},... | collective-permute-start | bytes 1966088 | tf_op jit(solution)/shard_map/ppermute | solution.py:50
  416.1 12.3 %copy-start.11 = (f32[2,2,40,1024]{3,2,1,0:T(8,128)S(1)}, f32[2,2,40,1024]{3,2,1,0:T(8,128)}, u32[]{:S(2)}) copy-start(f32[2,2,40,1024]{3,2,1,0:T(8,128)} %copy-done.10) | copy-start | bytes 1966084
  416.1 12.4 %copy-start.13 = (f32[2,2,40,1024]{3,2,1,0:T(8,128)S(1)}, f32[2,2,40,1024]{3,2,1,0:T(8,128)}, u32[]{:S(2)}) copy-start(f32[2,2,40,1024]{3,2,1,0:T(8,128)} %copy-done.12) | copy-start | bytes 1966084
  438.9 35.6 %collective-permute-start.21 = (f32[80,1024]{1,0:T(8,128)S(1)}, f32[80,1024]{1,0:T(8,128)S(1)}, u32[]{:S(2)}, u32[]{:S(2)}) collective-permute-start(f32[80,1024]{1,0:T(8,128)S(1)} %dynamic-slice_bitcast_fusion.13), channel_id=1, source_target_pairs={{0,16},{1,17},{2,18},{3,19},{4,20},{5,21},{6,22},{7,23},{8,24},{9,... | collective-permute-start | bytes 983048 | tf_op jit(solution)/shard_map/ppermute | solution.py:50
  440.2 34.3 %collective-permute-start.20 = (f32[2,2,2,40,1024]{4,3,1,0,2:T(8,128)}, f32[2,2,2,40,1024]{4,3,1,0,2:T(8,128)}, u32[]{:S(2)}, u32[]{:S(2)}) collective-permute-start(f32[2,2,2,40,1024]{4,3,1,0,2:T(8,128)} %fusion.4), channel_id=1, source_target_pairs={{0,2},{1,3},{2,0},{3,1},{4,6},{5,7},{6,4},{7,5},{8,10},{9,11},{10,... | collective-permute-start | bytes 3932168 | tf_op jit(solution)/shard_map/ppermute | solution.py:50
  441.7 32.8 %collective-permute-start.19 = (f32[2,2,2,40,1024]{4,3,1,0,2:T(8,128)}, f32[2,2,2,40,1024]{4,3,1,0,2:T(8,128)}, u32[]{:S(2)}, u32[]{:S(2)}) collective-permute-start(f32[2,2,2,40,1024]{4,3,1,0,2:T(8,128)} %fusion.5), channel_id=1, source_target_pairs={{0,4},{1,5},{2,6},{3,7},{4,0},{5,1},{6,2},{7,3},{8,12},{9,13},{10,... | collective-permute-start | bytes 3932168 | tf_op jit(solution)/shard_map/ppermute | solution.py:50
  442.3 30.6 %collective-permute-start.24 = (f32[2,2,2,2,16,256]{5,4,3,2,1,0:T(8,128)S(1)}, f32[2,2,2,2,16,256]{5,4,3,2,1,0:T(8,128)}, u32[]{:S(2)}, u32[]{:S(2)}) collective-permute-start(f32[2,2,2,2,16,256]{5,4,3,2,1,0:T(8,128)S(1)} %dynamic-slice_bitcast_fusion.14), channel_id=1, source_target_pairs={{0,1},{1,0},{2,3},{3,2},{4,5},{5,4},{6,7},{7,6},{8,9},{9,8},{10,11... | collective-permute-start | bytes 786440 | tf_op jit(solution)/shard_map/ppermute | solution.py:50
  460.7 17.7 %copy-start.54 = (f32[1,512]{1,0:T(1,128)S(1)}, f32[1,512]{1,0:T(1,128)}, u32[]{:S(2)}) copy-start(f32[1,512]{1,0:T(1,128)} %get-tuple-element.301) | copy-start | bytes 6148
  475.6 8.8 %collective-permute-start.22 = (f32[2,2,2,2,16,256]{5,4,3,2,1,0:T(8,128)S(1)}, f32[2,2,2,2,16,256]{5,4,3,2,1,0:T(8,128)}, u32[]{:S(2)}, u32[]{:S(2)}) collective-permute-start(f32[2,2,2,2,16,256]{5,4,3,2,1,0:T(8,128)S(1)} %dynamic-slice_bitcast_fusion.15), channel_id=1, source_target_pairs={{0,1},{1,0},{2,3},{3,2},{4,5},{5,4},{6,7},{7,6},{8,9},{9,8},{10,11... | collective-permute-start | bytes 786440 | tf_op jit(solution)/shard_map/ppermute | solution.py:50
  482.2 7.3 %copy-start.53 = (f32[1,512]{1,0:T(1,128)S(1)}, f32[1,512]{1,0:T(1,128)}, u32[]{:S(2)}) copy-start(f32[1,512]{1,0:T(1,128)} %get-tuple-element.303) | copy-start | bytes 6148
  482.2 8.6 %copy-start.52 = (f32[1,4,2,128]{3,1,2,0:T(4,128)S(1)}, f32[1,4,2,128]{3,1,2,0:T(4,128)}, u32[]{:S(2)}) copy-start(f32[1,4,2,128]{3,1,2,0:T(4,128)} %copy.180) | copy-start | bytes 12292
  486.1 20.4 %collective-permute-start.27 = (f32[2,2,40,1024]{3,2,1,0:T(8,128)}, f32[2,2,40,1024]{3,2,1,0:T(8,128)}, u32[]{:S(2)}, u32[]{:S(2)}) collective-permute-start(f32[2,2,40,1024]{3,2,1,0:T(8,128)} %fusion.23), channel_id=1, source_target_pairs={{0,4},{1,5},{2,6},{3,7},{4,0},{5,1},{6,2},{7,3},{8,12},{9,13},{10,... | collective-permute-start | bytes 1966088 | tf_op jit(solution)/shard_map/ppermute | solution.py:50
  487.5 19.0 %collective-permute-start.26 = (f32[2,2,40,1024]{3,2,1,0:T(8,128)}, f32[2,2,40,1024]{3,2,1,0:T(8,128)S(1)}, u32[]{:S(2)}, u32[]{:S(2)}) collective-permute-start(f32[2,2,40,1024]{3,2,1,0:T(8,128)} %fusion.25), channel_id=1, source_target_pairs={{0,2},{1,3},{2,0},{3,1},{4,6},{5,7},{6,4},{7,5},{8,10},{9,11},{10,... | collective-permute-start | bytes 1966088 | tf_op jit(solution)/shard_map/ppermute | solution.py:50
  492.0 13.6 %all-to-all-start.5 = ((f32[32,8,128]{2,1,0:T(8,128)}), f32[32,8,128]{2,1,0:T(8,128)S(1)}, u32[]{:S(2)}, u32[]{:S(2)}) async-start(f32[32,8,128]{2,1,0:T(8,128)} %bitcast.492), calls=%async_computation.5 | async-start | bytes 262144 | tf_op jit(solution)/shard_map/all_to_all | solution.py:177
  496.5 9.0 %collective-permute-start.25 = (f32[2,2,2,16,256]{4,3,2,1,0:T(8,128)}, f32[2,2,2,16,256]{4,3,2,1,0:T(8,128)}, u32[]{:S(2)}, u32[]{:S(2)}) collective-permute-start(f32[2,2,2,16,256]{4,3,2,1,0:T(8,128)} %bitcast_add_fusion.11), channel_id=1, source_target_pairs={{0,8},{1,9},{2,10},{3,11},{4,12},{5,13},{6,14},{7,15},{8,0},{9,1},... | collective-permute-start | bytes 393224 | tf_op jit(solution)/shard_map/ppermute | solution.py:50
  498.3 8.2 %collective-permute-start.23 = (f32[2,2,2,16,256]{4,3,2,1,0:T(8,128)}, f32[2,2,2,16,256]{4,3,2,1,0:T(8,128)}, u32[]{:S(2)}, u32[]{:S(2)}) collective-permute-start(f32[2,2,2,16,256]{4,3,2,1,0:T(8,128)} %bitcast_add_fusion.12), channel_id=1, source_target_pairs={{0,8},{1,9},{2,10},{3,11},{4,12},{5,13},{6,14},{7,15},{8,0},{9,1},... | collective-permute-start | bytes 393224 | tf_op jit(solution)/shard_map/ppermute | solution.py:50
  512.6 7.2 %collective-permute-start.30 = (f32[2,2,16,256]{3,2,1,0:T(8,128)S(1)}, f32[2,2,16,256]{3,2,1,0:T(8,128)S(1)}, u32[]{:S(2)}, u32[]{:S(2)}) collective-permute-start(f32[2,2,16,256]{3,2,1,0:T(8,128)S(1)} %bitcast_add_fusion.13), channel_id=1, source_target_pairs={{0,16},{1,17},{2,18},{3,19},{4,20},{5,21},{6,22},{7,23},{8,24},{9,... | collective-permute-start | bytes 196616 | tf_op jit(solution)/shard_map/ppermute | solution.py:50
  515.5 6.1 %collective-permute-start.28 = (f32[2,2,16,256]{3,2,1,0:T(8,128)S(1)}, f32[2,2,16,256]{3,2,1,0:T(8,128)S(1)}, u32[]{:S(2)}, u32[]{:S(2)}) collective-permute-start(f32[2,2,16,256]{3,2,1,0:T(8,128)S(1)} %bitcast_add_fusion.17), channel_id=1, source_target_pairs={{0,16},{1,17},{2,18},{3,19},{4,20},{5,21},{6,22},{7,23},{8,24},{9,... | collective-permute-start | bytes 196616 | tf_op jit(solution)/shard_map/ppermute | solution.py:50
  523.4 7.6 %copy-start.24 = (f32[32,256]{0,1:T(8,128)S(1)}, f32[32,256]{0,1:T(8,128)}, u32[]{:S(2)}) copy-start(f32[32,256]{0,1:T(8,128)} %copy-done.23) | copy-start | bytes 98308
  523.4 8.2 %copy-start.41 = (f32[32,2,16]{2,1,0:T(2,128)S(1)}, f32[32,2,16]{2,1,0:T(2,128)}, u32[]{:S(2)}) copy-start(f32[32,2,16]{2,1,0:T(2,128)} %copy-done.40) | copy-start | bytes 12292
  523.4 8.9 %copy-start.43 = (f32[32,2,16]{2,1,0:T(2,128)S(1)}, f32[32,2,16]{2,1,0:T(2,128)}, u32[]{:S(2)}) copy-start(f32[32,2,16]{2,1,0:T(2,128)} %copy-done.42) | copy-start | bytes 12292
  523.4 12.4 %copy-start.18 = (f32[2,80,1024]{2,1,0:T(8,128)S(1)}, f32[2,80,1024]{2,1,0:T(8,128)}, u32[]{:S(2)}) copy-start(f32[2,80,1024]{2,1,0:T(8,128)} %copy-done.17) | copy-start | bytes 1966084
  524.5 27.9 %all-to-all-start.6 = ((f32[32,56,128]{2,1,0:T(8,128)}), f32[32,56,128]{2,1,0:T(8,128)S(1)}, u32[]{:S(2)}, u32[]{:S(2)}) async-start(f32[32,56,128]{2,1,0:T(8,128)} %bitcast.219), calls=%async_computation.6 | async-start | bytes 1835008 | tf_op jit(solution)/shard_map/all_to_all | solution.py:177
  529.0 31.7 %collective-permute-start.32 = (f32[2,80,1024]{2,1,0:T(8,128)}, f32[2,80,1024]{2,1,0:T(8,128)}, u32[]{:S(2)}, u32[]{:S(2)}) collective-permute-start(f32[2,80,1024]{2,1,0:T(8,128)} %fusion.13), channel_id=1, source_target_pairs={{0,8},{1,9},{2,10},{3,11},{4,12},{5,13},{6,14},{7,15},{8,0},{9,1},... | collective-permute-start | bytes 1966088 | tf_op jit(solution)/shard_map/ppermute | solution.py:50
  532.9 27.9 %copy-start.14 = (f32[2,2,40,1024]{3,2,1,0:T(8,128)S(1)}, f32[2,2,40,1024]{3,2,1,0:T(8,128)}, u32[]{:S(2)}) copy-start(f32[2,2,40,1024]{3,2,1,0:T(8,128)} %fusion.21) | copy-start | bytes 1966084
  532.9 20.4 %collective-permute-start.31 = (f32[2,16,256]{2,1,0:T(8,128)S(1)}, f32[2,16,256]{2,1,0:T(8,128)S(1)}, u32[]{:S(2)}, u32[]{:S(2)}) collective-permute-start(f32[2,16,256]{2,1,0:T(8,128)S(1)} %dynamic-slice_bitcast_fusion.16), channel_id=1, source_target_pairs={{0,2},{1,3},{2,0},{3,1},{4,6},{5,7},{6,4},{7,5},{8,10},{9,11},{10,... | collective-permute-start | bytes 98312 | tf_op jit(solution)/shard_map/ppermute | solution.py:50
  534.3 19.0 %collective-permute-start.29 = (f32[2,16,256]{2,1,0:T(8,128)S(1)}, f32[2,16,256]{2,1,0:T(8,128)S(1)}, u32[]{:S(2)}, u32[]{:S(2)}) collective-permute-start(f32[2,16,256]{2,1,0:T(8,128)S(1)} %dynamic-slice_bitcast_fusion.17), channel_id=1, source_target_pairs={{0,4},{1,5},{2,6},{3,7},{4,0},{5,1},{6,2},{7,3},{8,12},{9,13},{10,... | collective-permute-start | bytes 98312 | tf_op jit(solution)/shard_map/ppermute | solution.py:50
  552.7 13.4 %copy-start.26 = (f32[2,32,512]{2,1,0:T(8,128)S(1)}, f32[2,32,512]{2,1,0:T(8,128)}, u32[]{:S(2)}) copy-start(f32[2,32,512]{2,1,0:T(8,128)} %copy-done.25) | copy-start | bytes 393220
  561.9 17.2 %collective-permute-start.35 = (f32[80,1024]{1,0:T(8,128)S(1)}, f32[80,1024]{1,0:T(8,128)S(1)}, u32[]{:S(2)}, u32[]{:S(2)}) collective-permute-start(f32[80,1024]{1,0:T(8,128)S(1)} %dynamic-slice_bitcast_fusion.12), channel_id=1, source_target_pairs={{0,16},{1,17},{2,18},{3,19},{4,20},{5,21},{6,22},{7,23},{8,24},{9,... | collective-permute-start | bytes 983048 | tf_op jit(solution)/shard_map/ppermute | solution.py:50
  564.5 4.7 collective-permute-start.33
  567.7 3.7 collective-permute-start.34
  (40 other events, 107.4 us)
Sparse Core Ops, SparseCore 0:
  11.4 131.2 all-gather.6
  145.6 96.8 all-gather.8
  245.3 75.8 all-gather.10

commit v3 on v2

--- a/solution.py
+++ b/solution.py
@@ -108,6 +108,8 @@
 
 
 class RowSum:
+    parts = None
+
     def __init__(self, arrays, pairs, far_first=False):
         count = len(pairs)
         self.pairs, self.at, bits = pairs, 0, list(range(count))
@@ -119,12 +121,33 @@
         self.left = [list(bits) for _ in arrays]
         self.state = [[array.reshape((2,) * count + array.shape[1:])] for array in arrays]
 
-    def add(self, other):
-        self.state, self.orders, self.left = (
-            self.state + other.state,
-            self.orders + other.orders,
-            self.left + other.left,
+    @classmethod
+    def of_parts(cls, top_stays, low_stays, top_goes, low_goes, pairs):
+        if PARTS == 2 ** len(pairs):
+            sums = cls([top_goes, low_goes], pairs[:-1])
+            sums.parts, sums.pairs = (top_stays, low_stays), pairs
+            count = len(pairs)
+            sums.orders = [[count - 1, count - 3, count - 2, 1, 0], [count - 1, count - 2, count - 3, 1, 0]]
+            sums.left = [order[1:] for order in sums.orders]
+            return sums
+        halves = (
+            [jnp.stack([half[place] for place in places]) for half in pair]
+            for pair, places in zip(((top_stays, top_goes), (low_stays, low_goes)), PLACES)
         )
+        whole = jnp.concatenate([jnp.stack(pair, axis=1) for pair in halves], axis=2).reshape(PARTS, -1, GATES)
+        cuts = jnp.split(whole, [CONV_ROWS, CONV_ROWS + PART_ROWS], axis=1)
+        sums = cls([jnp.concatenate([cut.reshape(2 ** len(pairs), -1, GATES) for cut in cuts], axis=1)], pairs)
+        sums.halve()
+        return sums
+
+    def core(self, *gates):
+        if self.parts is None:
+            return self.step(*gates)
+        goes, gates = tie([terms[0] for terms in self.state], gates)
+        stays = [part.reshape(term.shape) for part, term in zip(self.parts, goes)]
+        self.state = [[part, self.pairs[-1].shift(term, 1)] for part, term in zip(stays, goes)]
+        self.at = 1
+        return gates
 
     def join(self):
         parts = self.state if self.at == 1 else [[sum(terms)] for terms in self.state]
@@ -135,6 +158,9 @@
         (terms,) = self.state
         half = terms[0].shape[-2] // 2
         self.state = [[term[..., :half, :] for term in terms], [term[..., half:, :] for term in terms]]
+        ((*order,),) = self.orders
+        self.orders = [order, order[:1] + order[2:0:-1] + order[3:]]
+        self.left = [list(self.left[0]), list(self.left[0])]
 
     def step(self, *gates):
         for k, terms in enumerate(self.state):
@@ -155,7 +181,7 @@
 
 def beside(sums, work, *inputs):
     for rows in sums:
-        inputs = rows.step(*inputs)
+        inputs = rows.core(*inputs) if rows.at == 0 else rows.step(*inputs)
     out = work(*inputs)
     came, out = tie([[terms[-1] for terms in rows.state] for rows in sums], out)
     for rows, last in zip(sums, came):
@@ -187,7 +213,7 @@
 
 
 def regrouped(whole, share):
-    sizes, start, pieces = (3 * share, share, share, share // 2), 0, []
+    sizes, start, pieces = (3 * share, share, share), 0, []
     for size in sizes:
         pieces.append(whole[:, start : start + size].reshape(PARTS, -1, GATES))
         start += size
@@ -209,6 +235,10 @@
     return lax.dot_general(
         left, right, (((left_dim,), (right_dim,)), ((), ())), precision=HIGHEST, preferred_element_type=jnp.float32
     )
+
+
+def split_dot(left, right, left_dim=1, right_dim=0):
+    return three_dots(halves_of(left), halves_of(right), left_dim, right_dim)
 
 
 def head_of(shape, dim, per_head):
@@ -221,21 +251,21 @@
     film = film_w[...].reshape(WIDTH, GATES)
     value = value_mixing[..., :WIDTH].reshape(WIDTH, WIDTH)
     mixing = value_mixing[..., WIDTH:].reshape(WIDTH, WIDTH)
-    grad_mixed = exact_dot(jnp.broadcast_to(grad_film[...], (8, GATES)), film, 1, 1)
-    grad_row = exact_dot(grad_mixed * (1.0 / QUERIES), mixing, 1, 1)
+    grad_mixed = split_dot(jnp.broadcast_to(grad_film[...], (16, GATES)), film, 1, 1)
+    grad_row = split_dot(grad_mixed * (1.0 / QUERIES), mixing, 1, 1)
     mixed_out[...] = grad_mixed[:1]
     row_out[...] = grad_row[:1]
-    own = head_of((HEADS, WIDTH), 1, HEAD_DIM) == head_of((HEADS, WIDTH), 0, 1)
-    grad_pooled = exact_dot(jnp.where(own, grad_row, 0.0), value, 1, 1)
-    grad_probs = exact_dot(grad_pooled, keys[...], 1, 1)
+    own = head_of((16, WIDTH), 1, HEAD_DIM) == head_of((16, WIDTH), 0, 1)
+    grad_pooled = split_dot(jnp.where(own, grad_row, 0.0), value, 1, 1)
+    grad_probs = split_dot(grad_pooled, keys[...], 1, 1)
     prob = probs[0]
-    weighted = prob * grad_probs[:, None, :]
+    weighted = prob * grad_probs[:HEADS][:, None, :]
     row_terms = jnp.sum(weighted, axis=2, keepdims=True)
     grad_scores = (weighted - prob * row_terms) * (1.0 / math.sqrt(HEAD_DIM))
     grad_scores = grad_scores.reshape(HEADS * QUERIES, -1)
-    grad_absorbed = exact_dot(grad_scores, keys[...])
+    grad_absorbed = split_dot(grad_scores, keys[...])
     absorbed_out[...] = grad_absorbed.T
-    grad_query = exact_dot(grad_absorbed, key_w[0])
+    grad_query = split_dot(grad_absorbed, key_w[0])
     shape = grad_query.shape
     grad_query = jnp.where(head_of(shape, 1, HEAD_DIM) == head_of(shape, 0, QUERIES), grad_query, 0.0)
     query_out[...] = jnp.sum(grad_query.reshape(HEADS, QUERIES, WIDTH), axis=0)
@@ -267,16 +297,18 @@
 
 
 def factor_kernel(
-    rows, pooled, means, mixeds, embeds, absorbed, query_rows, seeds, query_w,
+    rows, step_rows, pooled, means, mixeds, embeds, absorbed, query_rows, seeds, query_w,
     step_out, seeds_out, query_out, key_out, value_out, mixing_out, film_out, square_out,
 ):
     share = embeds.shape[1]
     at = {}
     start = 0
-    for name, size in (("row", WIDTH), ("mixed", WIDTH), ("film", GATES), ("step", WIDTH)):
+    for name, size in (("row", WIDTH), ("mixed", WIDTH), ("film", GATES)):
         for layer in range(LAYERS):
             at[name, layer] = rows[:, start : start + size]
             start += size
+    for layer in range(LAYERS):
+        at["step", layer] = step_rows[:, layer * WIDTH : (layer + 1) * WIDTH]
     square = jnp.zeros((1, 1), jnp.float32)
     own = head_of((HEADS, share, WIDTH), 2, HEAD_DIM) == head_of((HEADS, share, WIDTH), 0, 1)
     near = head_of((HEADS * QUERIES, WIDTH), 1, HEAD_DIM) == head_of((HEADS * QUERIES, WIDTH), 0, QUERIES)
@@ -329,7 +361,11 @@
 
 HALF = jnp.bfloat16
 PARTS = 32
-CONV_ROWS, PART_ROWS, STEP_ROWS = 3 * WIDTH // PARTS, WIDTH // PARTS, WIDTH // PARTS // 2
+PLACES = (
+    [(pair // 2 % 2) * 8 + pair % 2 * 4 + pair // 4 % 2 * 2 + pair // 8 for pair in range(PARTS // 2)],
+    [pair % 2 * 8 + (pair // 2 % 2) * 4 + pair // 4 % 2 * 2 + pair // 8 for pair in range(PARTS // 2)],
+)
+CONV_ROWS, PART_ROWS = 3 * WIDTH // PARTS, WIDTH // PARTS
 TILE = 256
 
 
@@ -354,6 +390,11 @@
     count = rows.shape[0]
     place = lax.broadcasted_iota(jnp.int32, rows.shape, 0) - steps
     return jnp.where((place >= 0) & (place < count), pltpu.roll(rows, steps % count, 0), 0.0)
+
+
+def shape_of(*sizes):
+    dtype = jnp.float32 if isinstance(sizes[-1], int) else sizes[-1]
+    return jax.ShapeDtypeStruct(tuple(size for size in sizes if isinstance(size, int)), dtype)
 
 
 def kernel_call(kernel, grid, in_specs, out_specs, out_shapes, scratch, macs):
@@ -362,7 +403,7 @@
         grid=grid,
         in_specs=in_specs,
         out_specs=out_specs,
-        out_shape=[jax.ShapeDtypeStruct(shape, jnp.float32) for shape in out_shapes],
+        out_shape=[shape_of(*shape) for shape in out_shapes],
         scratch_shapes=scratch,
         compiler_params=pltpu.CompilerParams(vmem_limit_bytes=60 * 2**20),
         cost_estimate=pl.CostEstimate(flops=6 * macs, bytes_accessed=16 * 2**20, transcendentals=0),
@@ -382,15 +423,8 @@
 OUT_SPEC = part_rows(PART_ROWS, 4)
 
 
-def gates_kernel(dilation, frames, cond, conv_w, cond_w, step_w, embed, live, tanh, sig, step_row, total):
+def gates_kernel(dilation, frames, cond, conv_w, cond_w, step_row, live, tanh, sig, total):
     k = pl.program_id(0)
-
-    @pl.when(k == 0)
-    def _():
-        pairs = step_w[...].reshape(-1, GATES)
-        row = exact_dot(jnp.broadcast_to(embed[:1], (8, embed.shape[1])), pairs[:, :WIDTH])
-        row = row + exact_dot(jnp.broadcast_to(embed[1:], (8, embed.shape[1])), pairs[:, WIDTH:])
-        step_row[...] = row[:1]
 
     def add(left, right, first):
         for start in range(0, GATES, TILE):
@@ -420,18 +454,17 @@
             sig[:, start : start + TILE] = jax.nn.sigmoid(total[:, WIDTH + start : WIDTH + start + TILE] + part)
 
 
-def layer_gates(whole, frames, cond, embed, live, dilation):
+def layer_gates(whole, frames, cond, step_row, live, dilation):
     count = frames.shape[0]
     return kernel_call(
         functools.partial(gates_kernel, dilation),
         (3,),
-        [fixed(count, WIDTH)] * 2
-        + [CONV_SPEC, COND_SPEC, part_rows(STEP_ROWS, 10), fixed(2, WIDTH // 2), fixed(count, 1)],
-        [fixed(count, WIDTH)] * 2 + [fixed(1, WIDTH)],
-        [(count, WIDTH)] * 2 + [(1, WIDTH)],
+        [fixed(count, WIDTH)] * 2 + [CONV_SPEC, COND_SPEC, fixed(1, WIDTH), fixed(count, 1)],
+        [fixed(count, WIDTH)] * 2,
+        [(count, WIDTH)] * 2,
         [pltpu.VMEM((count, GATES), jnp.float32)],
         4 * count * WIDTH * GATES,
-    )(frames, cond, whole, whole, whole, embed, live)
+    )(frames, cond, whole, whole, step_row, live)
 
 
 def post_kernel(tanh, sig, film, out_w, frames, skip, live, frames_next, skip_next, high, low):
@@ -464,7 +497,9 @@
     )(tanh, sig, film.reshape(2, WIDTH), whole, frames, skip, live)
 
 
-def back_gates_kernel(grad_frames, grad_skip, live, tanh, sig, film, out_w, grad_pre, grad_film, grad_out, high, low):
+def back_gates_kernel(
+    grad_frames, grad_skip, live, tanh, sig, film, out_w, pre_high, pre_low, grad_film, grad_out, high, low
+):
     k = pl.program_id(0)
 
     @pl.when(k == 0)
@@ -482,8 +517,8 @@
         grad_film[0:1, cut] += jnp.sum(grad_mod * gate, axis=0, keepdims=True)
         grad_film[1:2, cut] += jnp.sum(grad_mod, axis=0, keepdims=True)
         grad_gate = grad_mod * (1.0 + film[:1, cut])
-        grad_pre[:, cut] = grad_gate * (s * (1.0 - t * t))
-        grad_pre[:, far] = grad_gate * (gate * (1.0 - s))
+        pre_high[:, cut], pre_low[:, cut] = halves_of(grad_gate * (s * (1.0 - t * t)))
+        pre_high[:, far], pre_low[:, far] = halves_of(grad_gate * (gate * (1.0 - s)))
     modulated = tanh[...] * sig[...] * (1.0 + film[:1]) + film[1:]
     modulated = halves_of(modulated.T)
 
@@ -505,14 +540,17 @@
         back_gates_kernel,
         (2,),
         [rows, rows, pl.BlockSpec((count // 2, 1), lambda k: (k, 0)), rows, rows, fixed(2, WIDTH), OUT_SPEC],
-        [pl.BlockSpec((count // 2, GATES), lambda k: (k, 0)), fixed(2, WIDTH), fixed(WIDTH, GATES)],
-        [(count, GATES), (2, WIDTH), (WIDTH, GATES)],
+        [pl.BlockSpec((count // 2, GATES), lambda k: (k, 0))] * 2 + [fixed(2, WIDTH), fixed(WIDTH, GATES)],
+        [(count, GATES, HALF)] * 2 + [(2, WIDTH), (WIDTH, GATES)],
         [pltpu.VMEM((WIDTH, GATES), HALF)] * 2,
         2 * count * WIDTH * GATES,
     )(grad_frames, grad_skip, live, tanh, sig, film.reshape(2, WIDTH), whole)
 
 
-def back_weights_kernel(dilation, frames, cond, step_row, live, grad_pre, grad_conv, grad_cond, high, low):
+def back_weights_kernel(
+    dilation, core, frames, cond, step_row, live, pre_high, pre_low, grad_out,
+    top_stays, low_stays, top_goes, low_goes, high, low, conv_rows, cond_rows,
+):
     @pl.when(pl.program_id(0) == 0)
     def _():
         hidden = ((frames[...] + step_row[...]) * live[...]).T
@@ -528,39 +566,51 @@
         cut = slice(3 * WIDTH, 4 * WIDTH)
         high[cut, :], low[cut, :] = halves_of(cond[...].T)
 
-    grad = halves_of(grad_pre[...])
+    grad = (pre_high[...], pre_low[...])
     for start in range(0, 4 * WIDTH, 2 * TILE):
         cut = slice(start, start + 2 * TILE)
         part = three_dots((high[cut, :], low[cut, :]), grad, 1, 0)
         if start < 3 * WIDTH:
-            grad_conv[cut, :] = part
+            conv_rows[cut, :] = part
         else:
-            grad_cond[start - 3 * WIDTH : start - 3 * WIDTH + 2 * TILE, :] = part
-
-
-def layer_back_weights(frames, cond, step_row, live, grad_pre, dilation):
+            cond_rows[start - 3 * WIDTH : start - 3 * WIDTH + 2 * TILE, :] = part
+    half = top_goes.shape[1]
+    rest = CONV_ROWS - half
+    for top_out, low_out, parity in ((top_stays, low_stays, core[0]), (top_goes, low_goes, 1 - core[0])):
+        for pair in range(PARTS // 2):
+            part = 2 * pair + parity
+            rows = pl.multiple_of(part * CONV_ROWS, 8)
+            top_out[PLACES[0][pair]] = conv_rows[pl.ds(rows, half), :]
+            place = PLACES[1][pair]
+            low_out[place, :rest, :] = conv_rows[pl.ds(rows + half, rest), :]
+            rows = pl.multiple_of(part * PART_ROWS, 8)
+            low_out[place, rest : rest + PART_ROWS, :] = cond_rows[pl.ds(rows, PART_ROWS), :]
+            low_out[place, rest + PART_ROWS :, :] = grad_out[pl.ds(rows, PART_ROWS), :]
+
+
+def layer_back_weights(core, frames, cond, step_row, live, grad_pre, grad_out, dilation):
     count = frames.shape[0]
+    part = (PARTS // 2, (CONV_ROWS + 2 * PART_ROWS) // 2)
+    columns = pl.BlockSpec(part + (TILE,), lambda k: (0, 0, k))
     return kernel_call(
         functools.partial(back_weights_kernel, dilation),
         (GATES // TILE,),
-        [fixed(count, WIDTH)] * 2
-        + [fixed(1, WIDTH), fixed(count, 1), pl.BlockSpec((count, TILE), lambda k: (0, k))],
-        [pl.BlockSpec((3 * WIDTH, TILE), lambda k: (0, k)), pl.BlockSpec((WIDTH, TILE), lambda k: (0, k))],
-        [(3 * WIDTH, GATES), (WIDTH, GATES)],
-        [pltpu.VMEM((4 * WIDTH, count), HALF)] * 2,
+        [pl.BlockSpec(memory_space=pltpu.SMEM)]
+        + [fixed(count, WIDTH)] * 2
+        + [fixed(1, WIDTH), fixed(count, 1)]
+        + [pl.BlockSpec((rows, TILE), lambda k: (0, k)) for rows in (count, count, WIDTH)],
+        [columns] * 4,
+        [part + (GATES,)] * 4,
+        [pltpu.VMEM((4 * WIDTH, count), HALF)] * 2
+        + [pltpu.VMEM((rows, TILE), jnp.float32) for rows in (3 * WIDTH, WIDTH)],
         4 * count * WIDTH * GATES,
-    )(frames, cond, step_row, live, grad_pre)
-
-
-def back_frames_kernel(dilation, grad_pre, conv_w, grad_frames, live, grad_next, step_sum, high, low, total):
+    )(core, frames, cond, step_row, live, *grad_pre, grad_out)
+
+
+def back_frames_kernel(dilation, pre_high, pre_low, conv_w, grad_frames, live, grad_next, step_sum, total):
     k = pl.program_id(0)
     middle = WIDTH // 2
-
-    @pl.when(k == 0)
-    def _():
-        high[...], low[...] = halves_of(grad_pre[...])
-
-    grad, weight = (high[...], low[...]), halves_of(conv_w[...].reshape(-1, GATES))
+    grad, weight = (pre_high[...], pre_low[...]), halves_of(conv_w[...].reshape(-1, GATES))
 
     def taps(start):
         return three_dots(grad, tile_of(weight, start, 0), 1, 1)
@@ -582,16 +632,16 @@
 
 
 def layer_back_frames(whole, grad_pre, grad_frames, live, dilation):
-    count = grad_pre.shape[0]
+    count = grad_pre[0].shape[0]
     return kernel_call(
         functools.partial(back_frames_kernel, dilation),
         (2,),
-        [fixed(count, GATES), CONV_SPEC, fixed(count, WIDTH), fixed(count, 1)],
+        [fixed(count, GATES)] * 2 + [CONV_SPEC, fixed(count, WIDTH), fixed(count, 1)],
         [fixed(count, WIDTH), fixed(1, WIDTH)],
         [(count, WIDTH), (1, WIDTH)],
-        [pltpu.VMEM((count, GATES), HALF)] * 2 + [pltpu.VMEM((count, WIDTH), jnp.float32)],
+        [pltpu.VMEM((count, WIDTH), jnp.float32)],
         3 * count * WIDTH * GATES,
-    )(grad_pre, whole, grad_frames, live)
+    )(*grad_pre, whole, grad_frames, live)
 
 
 def on_device(
@@ -619,21 +669,22 @@
     rings, pairs = rings_of(devices), pairs_of(devices)
     share = step_proj.shape[1]
     key_count = prompt.shape[1]
-    extra_rows = -(-(key_count + LAYERS * share * QUERIES) // WIDTH)
+    extra_size = key_count + LAYERS * share * QUERIES
+    extra_rows = -(-(extra_size + 1) // WIDTH)
     key_rows = -(-(key_count + extra_rows) // 8) * 8
     me = lax.axis_index(AXIS)
 
     frame_packs = [
-        jnp.concatenate(
-            [conv_weight[layer], cond_proj[layer], out_proj[layer], step_proj[layer].reshape(-1, GATES)], axis=0
-        )
-        for layer in range(LAYERS)
+        jnp.concatenate([conv_weight[layer], cond_proj[layer], out_proj[layer]], axis=0) for layer in range(LAYERS)
     ]
     frame_whole_0 = lax.all_gather(frame_packs[0], AXIS, axis=0, tiled=False)
 
-    extra = jnp.concatenate(
-        [key_mask.astype(jnp.float32), to_all(query_seeds, prompt.shape[0])], axis=1
-    )
+    extra = (
+        key_mask.astype(jnp.float32),
+        to_all(query_seeds, devices),
+        to_all(diffusion_steps.astype(jnp.float32), devices),
+    )
+    extra = jnp.concatenate(extra, axis=1)
     extra = jnp.pad(extra, ((0, 0), (0, (key_rows - key_count) * WIDTH - extra.shape[1])))
     sent = jnp.concatenate([prompt, extra.reshape(prompt.shape[0], -1, WIDTH)], axis=1)
     query_key = jnp.concatenate([query_proj, key_proj], axis=2).reshape(LAYERS * share, GATES)
@@ -650,10 +701,14 @@
         & (key_place < lax.dynamic_index_in_dim(prompt_lengths, me, 0, keepdims=False))
         & ((masked_in == 1.0) | (key_place == 0))
     ).reshape(-1)
-    seeds = extra[:, key_count : key_count + LAYERS * share * QUERIES]
+    seeds = extra[:, key_count:extra_size]
     seeds = jnp.moveaxis(seeds.reshape(devices, LAYERS, share, QUERIES), 1, 0)
     seeds = seeds.reshape(LAYERS, WIDTH, QUERIES)
     keys = keys.reshape(-1, WIDTH)
+
+    embeds = jax.vmap(step_embedding)(extra[:, extra_size])
+    own_embeds = lax.dynamic_slice_in_dim(embeds, me * share, share, 1)
+    step_part = jnp.einsum("bw,lwx->blx", own_embeds, step_proj, precision=HIGHEST)
 
     query_key = gather_rows(query_key, rings).reshape(devices, LAYERS, share, GATES)
     query_key = jnp.moveaxis(query_key, 1, 0).reshape(LAYERS, WIDTH, GATES)
@@ -673,7 +728,8 @@
     frame_pack_1, frame_whole_0, pooled_keys = tie(frame_packs[1], frame_whole_0, pooled_keys)
     frame_whole_1 = lax.all_gather(frame_pack_1, AXIS, axis=0, tiled=False)
 
-    (pooled_cut,) = exchange(by_column(pooled_keys, devices))
+    pooled_cut, step_rows = exchange(by_column(pooled_keys, devices), step_part)
+    step_rows = jnp.sum(step_rows, axis=0).reshape(LAYERS, 1, WIDTH)
     pooled_cut = pooled_cut.reshape(devices, LAYERS, HEADS, share)
     pooled_cut, frame_whole_0, frames_in, conditioning = tie(pooled_cut, frame_whole_0, frames_in, conditioning)
     value_heads = value_proj.reshape(LAYERS, share, HEADS, HEAD_DIM)
@@ -689,12 +745,10 @@
     films, cot_frames, cot_skip = tie(films, cot_frames, cot_skip)
 
     live = (jnp.arange(frames_in.shape[1], dtype=jnp.int32) < item_lengths[0]).astype(jnp.float32)[:, None]
-    embed = step_embedding(diffusion_steps[0])[None, :]
-    embed_pairs = embed.reshape(-1, 2).T
     frames, cond, cot, cot_last = frames_in[0], conditioning[0], cot_frames[0], cot_skip[0]
     if devices != PARTS:
         frame_whole_0 = regrouped(frame_whole_0, share)
-    tanh_0, sig_0, step_row_0 = layer_gates(frame_whole_0, frames, cond, embed_pairs, live, 1)
+    tanh_0, sig_0 = layer_gates(frame_whole_0, frames, cond, step_rows[0], live, 1)
     frames_1, skip = layer_post(frame_whole_0, tanh_0, sig_0, films[0], frames, jnp.zeros_like(frames), live)
 
     attention_pack = jnp.concatenate(
@@ -712,7 +766,7 @@
         attention_whole = jnp.transpose(attention_whole, (1, 2, 0, 3, 4)).reshape(1, LAYERS, 2, WIDTH, GATES)
         frame_whole_1 = regrouped(frame_whole_1, share)
 
-    tanh_1, sig_1, step_row_1 = layer_gates(frame_whole_1, frames_1, cond, embed_pairs, live, 2)
+    tanh_1, sig_1 = layer_gates(frame_whole_1, frames_1, cond, step_rows[1], live, 2)
 
     def by_device(grad):
         return grad.reshape(devices, -1, GATES)
@@ -720,37 +774,29 @@
     def by_share(grad):
         return grad.reshape(devices, share, -1)
 
-    grad_pre_1, grad_film_1, grad_out = layer_back_gates(frame_whole_1, tanh_1, sig_1, films[1], cot, cot_last, live)
-    sum_2 = RowSum([by_device(grad_out)], pairs)
-
-    def weights_1(grad_pre):
-        return layer_back_weights(frames_1, cond, step_row_1, live, grad_pre, 2), grad_pre
-
-    (grad_conv, grad_cond), grad_pre_1 = beside([sum_2], weights_1, grad_pre_1)
-    sum_1 = RowSum([by_device(grad_conv), by_device(grad_cond)], pairs)
+    core = (me % 2 if devices == PARTS else jnp.zeros_like(me)).astype(jnp.int32).reshape(1)
+    *grad_pre_1, grad_film_1, grad_out = layer_back_gates(frame_whole_1, tanh_1, sig_1, films[1], cot, cot_last, live)
+    parts = layer_back_weights(core, frames_1, cond, step_rows[1], live, grad_pre_1, grad_out, 2)
+    sum_1 = RowSum.of_parts(*parts, pairs)
 
     def post_1(tanh, sig, grad_pre):
         return layer_post(frame_whole_1, tanh, sig, films[1], frames_1, skip, live), grad_pre
 
     (frames, skip), grad_pre_1 = beside([sum_1], post_1, tanh_1, sig_1, grad_pre_1)
-    sum_1.add(sum_2)
-    sum_1.join()
-    sum_1.halve()
 
     def frames_and_gates(grad_pre):
         grad_frames, step_sum = layer_back_frames(frame_whole_1, grad_pre, cot, live, 2)
         gates = layer_back_gates(frame_whole_0, tanh_0, sig_0, films[0], grad_frames, cot_last, live)
         return grad_frames, step_sum, *gates
 
-    grad_frames, step_sum_1, grad_pre_0, grad_film_0, grad_out = beside([sum_1], frames_and_gates, grad_pre_1)
-    sum_a = RowSum([by_device(grad_out)], pairs)
+    grad_frames, step_sum_1, *grad_pre_0, grad_film_0, grad_out = beside([sum_1], frames_and_gates, grad_pre_1)
 
     def weights_0(grad_pre):
-        return layer_back_weights(frames_in[0], cond, step_row_0, live, grad_pre, 1), grad_pre
-
-    (grad_conv, grad_cond), grad_pre_0 = beside([sum_1, sum_a], weights_0, grad_pre_0)
+        return layer_back_weights(core, frames_in[0], cond, step_rows[0], live, grad_pre, grad_out, 1), grad_pre
+
+    parts, grad_pre_0 = beside([sum_1], weights_0, grad_pre_0)
     sum_1.join()
-    sum_b = RowSum([by_device(grad_conv), by_device(grad_cond)], pairs)
+    sum_b = RowSum.of_parts(*parts, pairs)
     key_w = query_key[:, :, WIDTH:]
 
     def attention_1(grad_film):
@@ -758,9 +804,6 @@
 
     grad_film_0, grad_film_1 = grad_film_0.reshape(1, GATES), grad_film_1.reshape(1, GATES)
     absorbed_1, query_1, row_1, mixed_1 = beside([sum_b, sum_1], attention_1, grad_film_1)
-    sum_b.add(sum_a)
-    sum_b.join()
-    sum_b.halve()
 
     def attention_and_frames(grad_film, grad_pre):
         attention = attention_back(0, grad_film, attention_whole, key_w, probs, keys)
@@ -772,23 +815,25 @@
     sum_d = RowSum([by_share(absorbed_0), by_share(absorbed_1)], pairs, far_first=True)
     sum_d.step()
     query_parts = jnp.stack([query_0, query_1]).reshape(devices, -1)
-    (query_cut,) = beside([sum_d, sum_b], exchange, query_parts)
-    query_cut = jnp.sum(query_cut, axis=0)
-    sum_d.step()
+    first_rows = jnp.concatenate(
+        [part.reshape(-1) for part in (row_0, row_1, mixed_0, mixed_1, grad_film_0, grad_film_1)]
+    )
+    query_cut, first_rows = beside([sum_d, sum_b], exchange, query_parts, to_all(first_rows, devices))
+    (query_cut,) = sum_d.step(jnp.sum(query_cut, axis=0))
     sum_b.join()
-    parts = (row_0, row_1, mixed_0, mixed_1, grad_film_0, grad_film_1, step_sum_0, step_sum_1, query_cut)
-    whole_rows = jnp.concatenate([part.reshape(-1) for part in parts])
-    rows, own_embeds = beside([sum_d, sum_b], exchange, to_all(whole_rows, devices), by_column(embed, devices))
+    last_rows = jnp.concatenate([part.reshape(-1) for part in (step_sum_0, step_sum_1, query_cut)])
+    (last_rows,) = beside([sum_b], exchange, to_all(last_rows, devices))
+    (sum_d.state,) = sum_b.step(sum_d.state)
     while sum_d.at < len(pairs):
         sum_d.step()
     sum_d.join()
-    query_start = whole_rows.size - query_cut.size
-    query_grads = rows[:, query_start:].reshape(LAYERS, QUERIES, WIDTH)
+    query_grads = last_rows[:, LAYERS * WIDTH :].reshape(LAYERS, QUERIES, WIDTH)
     absorbed_sums = sum_d.result().reshape(LAYERS, share, HEADS * QUERIES)
 
     small = [(LAYERS, share, columns) for columns in (WIDTH, QUERIES, WIDTH, WIDTH, WIDTH, WIDTH, GATES)]
     *factored, square = pl.pallas_call(factor_kernel, out_shape=shapes_of(*small, (1, 1)))(
-        rows[:, :query_start],
+        first_rows,
+        last_rows[:, : LAYERS * WIDTH],
         jnp.moveaxis(pooled_cut.reshape(devices, LAYERS, HEADS * share), 1, 0),
         jnp.moveaxis(mean_cut, 1, 0),
         jnp.moveaxis(mixed_cut, 1, 0),

time: 610 us -> 547 us (0.90)
  local copies, waits for them, and re-layouts: 75.8 us -> 42.3 us
  other arithmetic: 66.9 us -> 52.4 us
    unnamed x135 -> x90, local copies, waits for them, and re-layouts: 27.3 us -> 14.4 us
    concatenate x5 -> x1, other arithmetic: 12.4 us -> 0.62 us  [join(): self.state = [[jnp.concatenate(terms, axis=axis) for terms in zip(*parts)]]]
    all_gather x1, waiting for transfers between devices: 20.5 us -> 8.76 us  [on_device(): frame_whole_1 = lax.all_gather(frame_pack_1, AXIS, axis=0, tiled=False)]
    squeeze x14, local copies, waits for them, and re-layouts: 18.4 us -> 6.85 us  [pick(): lax.dynamic_index_in_dim(term, place, dim, keepdims=False)]
    pallas_call x2, Pallas kernels: 24.5 us -> 17.1 us  [attention_back(): kernel_call(attention_back_kernel, (1,), [fixed(1, GATES), pl.BlockSpec((...]
    optimization_barrier x3 -> x0, local copies, waits for them, and re-layouts: 6.91 us -> none  [tie(): return jax.tree.unflatten(tree, lax.optimization_barrier(leaves))]
    ppermute x36 -> x34, starting transfers between devices: 41.7 us -> 37.7 us  [shift(): return lax.ppermute(block, AXIS, perm)]
    ppermute x36 -> x34, waiting for transfers between devices: 69.2 us -> 68.9 us  [shift(): return lax.ppermute(block, AXIS, perm)]
  transfers between devices with their start and end apart: 46 -> 44, of which waited for: 18 -> 20; matrix products, arithmetic and copies ran while one was open for 20% -> 16% of each run, Pallas kernels for 31% -> 34%
where the time goes in v3:
time: 547 us; the launch traced here: 541 us
  Pallas kernels  190 us (35%)
  waiting for transfers between devices  151 us (28%)
  starting transfers between devices  65.6 us (12%)
  other arithmetic  52.4 us (10%)
  local copies, waits for them, and re-layouts  42.3 us (8%)
  between operations  16.5 us (3%)
  matrix products  12.2 us (2%)
  blocking collectives  11.5 us (2%)
    ppermute x34, waiting for transfers between devices, shift(): return lax.ppermute(block, AXIS, perm)  68.9 us
    all_to_all x6, waiting for transfers between devices, exchange(): lax.all_to_all(joined, AXIS, split_axis=0, concat_axis=0, tiled=True)  48.3 us
    pallas_call x2, Pallas kernels, layer_back_weights(): kernel_call(functools.partial(back_weights_kernel, dilation), (GATES // T...  43.1 us
    pallas_call x2, Pallas kernels, layer_gates(): kernel_call(functools.partial(gates_kernel, dilation), (3,), [fixed(count...  41.3 us
    ppermute x34, starting transfers between devices, shift(): return lax.ppermute(block, AXIS, perm)  37.7 us
    pallas_call x2, Pallas kernels, layer_back_frames(): kernel_call(functools.partial(back_frames_kernel, dilation), (2,), [fixed...  35.8 us
    pallas_call x2, Pallas kernels, layer_back_gates(): kernel_call(back_gates_kernel, (2,), [rows, rows, pl.BlockSpec((count //...  28.2 us
    add x12, other arithmetic, hop(): sum(pick(1 - ring.digit))  25.4 us
  transfers between devices with their start and end apart: 44, of which 20 were waited for; matrix products, arithmetic and copies ran while one was open for 16% of the time, Pallas kernels for 34%

profile of v3, /device:TPU:0, one launch (start us, length us, event | category | flops | bytes accessed | tf_op | source)
XLA Modules:
  0.0 541.3 jit_solution(11195818435878487109)
XLA Ops:
  10.1 2.6 copy.95
  15.5 3.0 collective-permute-start
  18.5 2.6 collective-permute-start.1
  22.4 2.5 collective-permute-done
  25.0 8.4 %collective-permute-done.1 = f32[32,1024]{1,0:T(8,128)S(1)} collective-permute-done((f32[32,1024]{1,0:T(8,128)S(1)}, f32[32,1024]{1,0:T(8,128)S(1)}, u32[]{:S(2)}, u32[]{:S(2)}) %collective-permute-start.1) | collective-permute-done | bytes 131104 | tf_op jit(solution)/shard_map/ppermute | solution.py:50
  36.8 7.4 %all-to-all-start = ((f32[32,32,512]{2,1,0:T(8,128)}), f32[32,32,512]{2,1,0:T(8,128)S(1)}, u32[]{:S(2)}, u32[]{:S(2)}) async-start(f32[32,32,512]{2,1,0:T(8,128)} %pad_maximum_fusion.1), calls=%async_computation | async-start | bytes 4194304 | tf_op jit(solution)/shard_map/all_to_all | solution.py:692
  45.5 1.8 collective-permute-start.6
  48.9 38.3 %collective-permute-done.6 = f32[2,4,16,1024]{3,2,0,1:T(8,128)S(1)} collective-permute-done((f32[2,4,16,1024]{3,2,0,1:T(8,128)S(1)}, f32[2,4,16,1024]{3,2,0,1:T(8,128)S(1)}, u32[]{:S(2)}, u32[]{:S(2)}) %collective-permute-start.6) | collective-permute-done | bytes 524320 | tf_op jit(solution)/shard_map/ppermute | solution.py:50
  90.6 3.2 collective-permute-done.7
  93.7 2.8 select_bitcast_fusion.1
  97.6 2.0 copy-done.3
  101.2 3.4 copy.103
  104.5 24.8 %all-to-all-done = f32[32,32,512]{2,1,0:T(8,128)S(1)} async-done(((f32[32,32,512]{2,1,0:T(8,128)}), f32[32,32,512]{2,1,0:T(8,128)S(1)}, u32[]{:S(2)}, u32[]{:S(2)}) %all-to-all-start) | async-done | bytes 2097184 | tf_op jit(solution)/shard_map/all_to_all | solution.py:692
  129.8 3.2 fusion
  133.9 2.8 convolution_multiply_fusion
  136.7 3.7 select_reduce_fusion
  140.9 2.1 bitcast_reduce_fusion
  146.0 3.3 all-to-all-start.1
  149.5 12.9 %all-to-all-done.1 = f32[32,16,128]{2,1,0:T(8,128)S(1)} async-done(((f32[32,16,128]{2,1,0:T(8,128)}), f32[32,16,128]{2,1,0:T(8,128)S(1)}, u32[]{:S(2)}, u32[]{:S(2)}) %all-to-all-start.1) | async-done | bytes 262176 | tf_op jit(solution)/shard_map/all_to_all | solution.py:203
  164.8 3.7 all-to-all-start.2
  170.7 6.1 %all-to-all-done.2 = f32[32,8,128]{2,1,0:T(8,128)S(1)} async-done(((f32[32,8,128]{2,1,0:T(8,128)}), f32[32,8,128]{2,1,0:T(8,128)S(1)}, u32[]{:S(2)}, u32[]{:S(2)}) %all-to-all-start.2) | async-done | bytes 131104 | tf_op jit(solution)/shard_map/all_to_all | solution.py:203
  178.8 2.6 all-to-all-start.3
  182.0 9.1 %all-to-all-done.3 = f32[32,8,128]{2,1,0:T(8,128)S(1)} async-done(((f32[32,8,128]{2,1,0:T(8,128)}), f32[32,8,128]{2,1,0:T(8,128)S(1)}, u32[]{:S(2)}, u32[]{:S(2)}) %all-to-all-start.3) | async-done | bytes 131104 | tf_op jit(solution)/shard_map/all_to_all | solution.py:203
  192.7 4.0 all-to-all-start.4
  196.7 21.3 %shard_map.282 = (f32[1024,512]{1,0:T(8,128)}, f32[1024,512]{1,0:T(8,128)}) custom-call(f32[1024,512]{1,0:T(8,128)} %bitcast.366, f32[1024,512]{1,0:T(8,128)} %bitcast.430, f32[32,80,1024]{2,1,0:T(8,128)} %bitcast.333, f32[32,80,1024]{2,1,0:T(8,128)} %bitcast.334, f32[1,512]{1,0:T(1,128)} %bitcast.416, f32[1024,1]{1,0:T(8,128)} %fusion.18.live), custom_call_target="tpu_custom_call" | custom-call | flops 12884901888 | bytes 16777216 | tf_op jit(solution)/shard_map/pallas_call | solution.py:459
  220.3 8.0 %shard_map.283 = (f32[1024,512]{1,0:T(8,128)}, f32[1024,512]{1,0:T(8,128)}) custom-call(f32[1024,512]{1,0:T(8,128)} %get-tuple-element.198.tanh, f32[1024,512]{1,0:T(8,128)} %get-tuple-element.199.sig, f32[2,512]{1,0:T(2,128)} %reshape_squeeze.8.film, f32[32,80,1024]{2,1,0:T(8,128)} %bitcast.335, f32[1024,512]{1,0:T(8,128)} %bitcast.367, ...), custom_call_target="tpu_custom_call" | custom-call | flops 3221225472 | bytes 16777216 | tf_op jit(solution)/shard_map/pallas_call | solution.py:489
  228.2 8.8 %all-gather.9.cloned.1.call-done = f32[2560,1024]{1,0:T(8,128)} async-done(((f32[80,1024]{1,0:T(8,128)}), f32[2560,1024]{1,0:T(8,128)}) %all-gather.9.cloned.1.call-update) | async-done | bytes 10485776 | tf_op jit(solution)/shard_map/all_gather | solution.py:729
  237.6 20.0 %shard_map.284 = (f32[1024,512]{1,0:T(8,128)}, f32[1024,512]{1,0:T(8,128)}) custom-call(f32[1024,512]{1,0:T(8,128)} %get-tuple-element.203.frames, f32[1024,512]{1,0:T(8,128)} %bitcast.431, f32[32,80,1024]{2,1,0:T(8,128)} %bitcast.338, f32[32,80,1024]{2,1,0:T(8,128)} %bitcast.339, f32[1,512]{1,0:T(1,128)} %bitcast.418, f32[1024,1]{1,0:T(8,128)} %fusion.18.live), custom_call_target="tpu_custom_call" | custom-call | flops 12884901888 | bytes 16777216 | tf_op jit(solution)/shard_map/pallas_call | solution.py:459
  257.6 14.2 %shard_map.285 = (bf16[1024,1024]{1,0:T(8,128)(2,1)}, bf16[1024,1024]{1,0:T(8,128)(2,1)}, f32[2,512]{1,0:T(2,128)}, f32[512,1024]{1,0:T(8,128)}) custom-call(f32[1024,512]{1,0:T(8,128)} %bitcast.426, f32[1024,512]{1,0:T(8,128)} %bitcast.428, f32[1024,1]{1,0:T(8,128)} %fusion.18.live, f32[1024,512]{1,0:T(8,128)} %get-tuple-element.216.tanh, ...), custom_call_target="tpu_custom_call" | custom-call | flops 6442450944 | bytes 16777216 | tf_op jit(solution)/shard_map/pallas_call | solution.py:539
  271.8 21.6 %shard_map.286 = (f32[16,40,1024]{2,1,0:T(8,128)}, f32[16,40,1024]{2,1,0:T(8,128)}, f32[16,40,1024]{2,1,0:T(8,128)}, f32[16,40,1024]{2,1,0:T(8,128)}) custom-call(s32[1]{0:T(128)} %bitcast.core, f32[1024,512]{1,0:T(8,128)} %get-tuple-element.203.frames, f32[1024,512]{1,0:T(8,128)} %bitcast.432, f32[1,512]{1,0:T(1,128)} %bitcast.419, f32[1024,1]{1,0:T(8,128)} %fusion.18.live, ...), custom_call_target="tpu_custom_call" | custom-call | flops 12884901888 | bytes 16777216 | tf_op jit(solution)/shard_map/pallas_call | solution.py:595
  294.5 8.1 %shard_map.287 = (f32[1024,512]{1,0:T(8,128)}, f32[1024,512]{1,0:T(8,128)}) custom-call(f32[1024,512]{1,0:T(8,128)} %get-tuple-element.216.tanh, f32[1024,512]{1,0:T(8,128)} %get-tuple-element.217.sig, f32[2,512]{1,0:T(2,128)} %reshape_squeeze.9.film, f32[32,80,1024]{2,1,0:T(8,128)} %bitcast.341, f32[1024,512]{1,0:T(8,128)} %get-tuple-element.203.frames, ...), custom_call_target="tpu_custom_call" | custom-call | flops 3221225472 | bytes 16777216 | tf_op jit(solution)/shard_map/pallas_call | solution.py:489
  302.6 2.9 add_bitcast_fusion.3
  305.5 2.7 add_bitcast_fusion.2
  309.1 1.7 collective-permute-start.10
  310.8 18.0 %shard_map.288 = (f32[1024,512]{1,0:T(8,128)}, f32[1,512]{1,0:T(1,128)}) custom-call(bf16[1024,1024]{1,0:T(8,128)(2,1)} %get-tuple-element.235.pre_high, bf16[1024,1024]{1,0:T(8,128)(2,1)} %get-tuple-element.236.pre_low, f32[32,80,1024]{2,1,0:T(8,128)} %bitcast.342, f32[1024,512]{1,0:T(8,128)} %bitcast.427, f32[1024,1]{1,0:T(8,128)} %fusion.18.live), custom_call_target="tpu_custom_call" | custom-call | flops 9663676416 | bytes 16777216 | tf_op jit(solution)/shard_map/pallas_call | solution.py:636
  328.8 14.0 %shard_map.289 = (bf16[1024,1024]{1,0:T(8,128)(2,1)}, bf16[1024,1024]{1,0:T(8,128)(2,1)}, f32[2,512]{1,0:T(2,128)}, f32[512,1024]{1,0:T(8,128)}) custom-call(f32[1024,512]{1,0:T(8,128)} %get-tuple-element.297.grad_frames, f32[1024,512]{1,0:T(8,128)} %bitcast.429, f32[1024,1]{1,0:T(8,128)} %fusion.18.live, f32[1024,512]{1,0:T(8,128)} %get-tuple-element.198.tanh, ...), custom_call_target="tpu_custom_call" | custom-call | flops 6442450944 | bytes 16777216 | tf_op jit(solution)/shard_map/pallas_call | solution.py:539
  342.8 2.1 bitcast_add_fusion.7
  347.9 21.6 %shard_map.290 = (f32[16,40,1024]{2,1,0:T(8,128)}, f32[16,40,1024]{2,1,0:T(8,128)}, f32[16,40,1024]{2,1,0:T(8,128)}, f32[16,40,1024]{2,1,0:T(8,128)}) custom-call(s32[1]{0:T(128)} %bitcast.core, f32[1024,512]{1,0:T(8,128)} %bitcast.368, f32[1024,512]{1,0:T(8,128)} %bitcast.433, f32[1,512]{1,0:T(1,128)} %bitcast.417, f32[1024,1]{1,0:T(8,128)} %fusion.18.live, ...), custom_call_target="tpu_custom_call" | custom-call | flops 12884901888 | bytes 16777216 | tf_op jit(solution)/shard_map/pallas_call | solution.py:595
  370.0 1.7 fusion.16
  377.8 8.5 %shard_map.291 = (f32[512,256]{1,0:T(8,128)}, f32[32,512]{1,0:T(8,128)}, f32[1,512]{1,0:T(1,128)}, f32[1,512]{1,0:T(1,128)}) custom-call(f32[1,1024]{1,0:T(1,128)} %bitcast.404, f32[32,2,2,16,1024]{4,3,2,1,0:T(8,128)} %bitcast.320, f32[32,2,2,16,1024]{4,3,2,1,0:T(8,128)} %bitcast.321, f32[2,512,512]{2,1,0:T(8,128)} %slice.134.key_w, ...), custom_call_target="tpu_custom_call" | custom-call | flops 2013265920 | bytes 16777216 | tf_op jit(solution)/shard_map/pallas_call | solution.py:281
  386.3 3.8 collective-permute-done.16
  390.1 3.0 add_bitcast_fusion.1
  393.1 2.6 add_bitcast_fusion
  400.6 17.9 %shard_map.293 = (f32[1024,512]{1,0:T(8,128)}, f32[1,512]{1,0:T(1,128)}) custom-call(bf16[1024,1024]{1,0:T(8,128)(2,1)} %get-tuple-element.295.pre_high, bf16[1024,1024]{1,0:T(8,128)(2,1)} %get-tuple-element.296.pre_low, f32[32,80,1024]{2,1,0:T(8,128)} %bitcast.337, f32[1024,512]{1,0:T(8,128)} %get-tuple-element.297.grad_frames, f32[1024,1]{1,0:T(8,128)} %fusion.18.live), custom_call_target="tpu_custom_call" | custom-call | flops 9663676416 | bytes 16777216 | tf_op jit(solution)/shard_map/pallas_call | solution.py:636
  418.5 8.6 %shard_map.292 = (f32[512,256]{1,0:T(8,128)}, f32[32,512]{1,0:T(8,128)}, f32[1,512]{1,0:T(1,128)}, f32[1,512]{1,0:T(1,128)}) custom-call(f32[1,1024]{1,0:T(1,128)} %bitcast.405, f32[32,2,2,16,1024]{4,3,2,1,0:T(8,128)} %bitcast.322, f32[32,2,2,16,1024]{4,3,2,1,0:T(8,128)} %bitcast.323, f32[2,512,512]{2,1,0:T(8,128)} %slice.134.key_w, ...), custom_call_target="tpu_custom_call" | custom-call | flops 2013265920 | bytes 16777216 | tf_op jit(solution)/shard_map/pallas_call | solution.py:281
  432.8 2.3 bitcast_add_fusion.2
  435.1 2.5 bitcast_add_fusion.3
  437.6 1.6 bitcast_add_fusion.11
  440.3 3.3 all-to-all-start.5
  443.6 1.9 collective-permute-start.25
  452.6 8.9 %all-to-all-done.5 = f32[32,40,128]{2,1,0:T(8,128)S(1)} async-done(((f32[32,40,128]{2,1,0:T(8,128)}), f32[32,40,128]{2,1,0:T(8,128)S(1)}, u32[]{:S(2)}, u32[]{:S(2)}) %all-to-all-start.5) | async-done | bytes 655392 | tf_op jit(solution)/shard_map/all_to_all | solution.py:203
  462.7 5.0 collective-permute-done.25
  470.2 1.7 fusion.14
  471.9 1.9 fusion.15
  476.3 3.6 all-to-all-start.6
  482.3 2.7 collective-permute-start.28
  487.0 11.3 %all-to-all-done.6 = f32[32,16,128]{2,1,0:T(8,128)S(1)} async-done(((f32[32,16,128]{2,1,0:T(8,128)}), f32[32,16,128]{2,1,0:T(8,128)S(1)}, u32[]{:S(2)}, u32[]{:S(2)}) %all-to-all-start.6) | async-done | bytes 262176 | tf_op jit(solution)/shard_map/all_to_all | solution.py:203
  504.9 1.8 collective-permute-start.30
  508.7 1.8 collective-permute-done.32
  511.2 3.5 shard_map.294
  514.7 2.7 collective-permute-done.33
  518.1 2.6 shard_map.295
  520.7 11.5 %all_to_all.40.squares = f32[32,8,128]{2,1,0:T(8,128)} all-to-all(f32[32,8,128]{2,1,0:T(8,128)} %shard_map.295), channel_id=1, replica_groups=mesh['items'=32] {'items'}, dimensions={0} | all-to-all | bytes 262144 | tf_op jit(solution)/shard_map/all_to_all | solution.py:848
  532.2 2.4 shard_map.296
  (277 shorter events, 85.0 us)
Async XLA Ops:
  7.2 137.5 %copy-start = (f32[2,16,512]{2,1,0:T(8,128)S(1)}, f32[2,16,512]{2,1,0:T(8,128)}, u32[]{:S(2)}) copy-start(f32[2,16,512]{2,1,0:T(8,128)} %param.26) | copy-start | bytes 196612
  7.2 136.9 %all-gather.7.cloned.1.call-start = ((), (), s32[]{:S(2)}) async-start(), calls=%async_computation.8 | async-start | bytes 10813440 | tf_op jit(solution)/shard_map/all_gather | solution.py:680
  15.5 9.5 %collective-permute-start = (f32[32,1024]{1,0:T(8,128)S(1)}, f32[32,1024]{1,0:T(8,128)S(1)}, u32[]{:S(2)}, u32[]{:S(2)}) collective-permute-start(f32[32,1024]{1,0:T(8,128)S(1)} %bitcast.384), channel_id=1, source_target_pairs={{0,8},{1,9},{2,10},{3,11},{4,12},{5,13},{6,14},{7,15},{8,16},{9,17... | collective-permute-start | bytes 393224 | tf_op jit(solution)/shard_map/ppermute | solution.py:50
  18.5 14.9 %collective-permute-start.1 = (f32[32,1024]{1,0:T(8,128)S(1)}, f32[32,1024]{1,0:T(8,128)S(1)}, u32[]{:S(2)}, u32[]{:S(2)}) collective-permute-start(f32[32,1024]{1,0:T(8,128)S(1)} %bitcast.385), channel_id=1, source_target_pairs={{0,16},{1,17},{2,18},{3,19},{4,20},{5,21},{6,22},{7,23},{8,24},{9,... | collective-permute-start | bytes 393224 | tf_op jit(solution)/shard_map/ppermute | solution.py:50
  21.1 12.6 %collective-permute-start.2 = (f32[32,1024]{1,0:T(8,128)S(1)}, f32[32,1024]{1,0:T(8,128)S(1)}, u32[]{:S(2)}, u32[]{:S(2)}) collective-permute-start(f32[32,1024]{1,0:T(8,128)S(1)} %bitcast.386), channel_id=1, source_target_pairs={{0,24},{1,25},{2,26},{3,27},{4,28},{5,29},{6,30},{7,31},{8,0},{9,1... | collective-permute-start | bytes 393224 | tf_op jit(solution)/shard_map/ppermute | solution.py:50
  33.8 10.6 %collective-permute-start.3 = (f32[4,16,1024]{2,1,0:T(8,128)S(1)}, f32[4,16,1024]{2,1,0:T(8,128)}, u32[]{:S(2)}, u32[]{:S(2)}) collective-permute-start(f32[4,16,1024]{2,1,0:T(8,128)S(1)} %get-tuple-element.383), channel_id=1, source_target_pairs={{0,2},{1,3},{2,0},{3,1},{4,6},{5,7},{6,4},{7,5},{8,10},{9,11},{10,... | collective-permute-start | bytes 786440 | tf_op jit(solution)/shard_map/ppermute | solution.py:50
  35.2 9.1 %collective-permute-start.5 = (f32[4,16,1024]{2,1,0:T(8,128)S(1)}, f32[4,16,1024]{2,1,0:T(8,128)}, u32[]{:S(2)}, u32[]{:S(2)}) collective-permute-start(f32[4,16,1024]{2,1,0:T(8,128)S(1)} %get-tuple-element.384), channel_id=1, source_target_pairs={{0,4},{1,5},{2,6},{3,7},{4,0},{5,1},{6,2},{7,3},{8,12},{9,13},{10,... | collective-permute-start | bytes 786440 | tf_op jit(solution)/shard_map/ppermute | solution.py:50
  36.8 92.5 %all-to-all-start = ((f32[32,32,512]{2,1,0:T(8,128)}), f32[32,32,512]{2,1,0:T(8,128)S(1)}, u32[]{:S(2)}, u32[]{:S(2)}) async-start(f32[32,32,512]{2,1,0:T(8,128)} %pad_maximum_fusion.1), calls=%async_computation | async-start | bytes 4194304 | tf_op jit(solution)/shard_map/all_to_all | solution.py:692
  44.2 192.8 %all-gather.9.cloned.1.call-start = ((), (), s32[]{:S(2)}) async-start(), calls=%async_computation.9 | async-start | bytes 10813440 | tf_op jit(solution)/shard_map/all_gather | solution.py:729
  45.5 41.8 %collective-permute-start.6 = (f32[2,4,16,1024]{3,2,0,1:T(8,128)S(1)}, f32[2,4,16,1024]{3,2,0,1:T(8,128)S(1)}, u32[]{:S(2)}, u32[]{:S(2)}) collective-permute-start(f32[2,4,16,1024]{3,2,0,1:T(8,128)S(1)} %pad_maximum_fusion.4), channel_id=1, source_target_pairs={{0,2},{1,3},{2,0},{3,1},{4,6},{5,7},{6,4},{7,5},{8,10},{9,11},{10,... | collective-permute-start | bytes 1572872 | tf_op jit(solution)/shard_map/ppermute | solution.py:50
  47.4 40.1 %collective-permute-start.4 = (f32[2,4,16,1024]{3,2,1,0:T(8,128)S(1)}, f32[2,4,16,1024]{3,2,1,0:T(8,128)S(1)}, u32[]{:S(2)}, u32[]{:S(2)}) collective-permute-start(f32[2,4,16,1024]{3,2,1,0:T(8,128)S(1)} %pad_maximum_fusion.3), channel_id=1, source_target_pairs={{0,4},{1,5},{2,6},{3,7},{4,0},{5,1},{6,2},{7,3},{8,12},{9,13},{10,... | collective-permute-start | bytes 1572872 | tf_op jit(solution)/shard_map/ppermute | solution.py:50
  89.2 4.5 collective-permute-start.7
  129.3 13.7 %copy-start.2 = (f32[32,32,512]{2,1,0:T(8,128)}, f32[32,32,512]{2,1,0:T(8,128)S(1)}, u32[]{:S(2)}) copy-start(f32[32,32,512]{2,1,0:T(8,128)S(1)} %all-to-all-done) | copy-start | bytes 6291460
  133.0 7.4 %copy-start.12 = (f32[2,32,512]{2,1,0:T(8,128)}, f32[2,32,512]{2,1,0:T(8,128)S(1)}, u32[]{:S(2)}) copy-start(f32[2,32,512]{2,1,0:T(8,128)S(1)} %fusion) | copy-start | bytes 393220
  144.1 5.3 copy-start.18
  144.1 5.4 copy-start.19
  144.7 17.9 %copy-start.21 = (f32[32,16]{1,0:T(8,128)}, f32[32,16]{1,0:T(8,128)S(1)}, u32[]{:S(2)}) copy-start(f32[32,16]{1,0:T(8,128)S(1)} %fusion.34.embeds) | copy-start | bytes 6148
  146.0 16.4 %all-to-all-start.1 = ((f32[32,16,128]{2,1,0:T(8,128)}), f32[32,16,128]{2,1,0:T(8,128)S(1)}, u32[]{:S(2)}, u32[]{:S(2)}) async-start(f32[32,16,128]{2,1,0:T(8,128)} %bitcast.163), calls=%async_computation.1 | async-start | bytes 524288 | tf_op jit(solution)/shard_map/all_to_all | solution.py:203
  149.5 19.0 %copy-start.15 = (f32[2,16,1024]{2,1,0:T(8,128)S(1)}, f32[2,16,1024]{2,1,0:T(8,128)}, u32[]{:S(2)}) copy-start(f32[2,16,1024]{2,1,0:T(8,128)} %param.35) | copy-start | bytes 393220
  164.8 12.0 %all-to-all-start.2 = ((f32[32,8,128]{2,1,0:T(8,128)}), f32[32,8,128]{2,1,0:T(8,128)S(1)}, u32[]{:S(2)}, u32[]{:S(2)}) async-start(f32[32,8,128]{2,1,0:T(8,128)} %copy.112), calls=%async_computation.2 | async-start | bytes 262144 | tf_op jit(solution)/shard_map/all_to_all | solution.py:203
  178.8 12.3 %all-to-all-start.3 = ((f32[32,8,128]{2,1,0:T(8,128)}), f32[32,8,128]{2,1,0:T(8,128)S(1)}, u32[]{:S(2)}, u32[]{:S(2)}) async-start(f32[32,8,128]{2,1,0:T(8,128)} %copy.116), calls=%async_computation.3 | async-start | bytes 262144 | tf_op jit(solution)/shard_map/all_to_all | solution.py:203
  192.7 25.3 %all-to-all-start.4 = ((f32[32,16,128]{2,1,0:T(8,128)}), f32[32,16,128]{2,1,0:T(8,128)S(1)}, u32[]{:S(2)}, u32[]{:S(2)}) async-start(f32[32,16,128]{2,1,0:T(8,128)} %reshape.334), calls=%async_computation.4 | async-start | bytes 524288 | tf_op jit(solution)/shard_map/all_to_all | solution.py:203
  196.7 181.1 %all-gather.11.cloned.1.call-start = ((), (), s32[]{:S(2)}) async-start(), calls=%async_computation.10 | async-start | bytes 8650752 | tf_op jit(solution)/shard_map/all_gather | solution.py:763
  271.8 22.1 %copy-start.27 = (f32[2,512]{1,0:T(2,128)S(1)}, f32[2,512]{1,0:T(2,128)}, u32[]{:S(2)}) copy-start(f32[2,512]{1,0:T(2,128)} %get-tuple-element.261) | copy-start | bytes 12292
  293.4 9.2 %collective-permute-start.8 = (f32[2,2,2,2,40,1024]{5,4,3,2,1,0:T(8,128)}, f32[2,2,2,2,40,1024]{5,4,3,2,1,0:T(8,128)}, u32[]{:S(2)}, u32[]{:S(2)}) collective-permute-start(f32[2,2,2,2,40,1024]{5,4,3,2,1,0:T(8,128)} %bitcast.425), channel_id=1, source_target_pairs={{0,1},{1,0},{2,3},{3,2},{4,5},{5,4},{6,7},{7,6},{8,9},{9,8},{10,11... | collective-permute-start | bytes 7864328 | tf_op jit(solution)/shard_map/ppermute | solution.py:50
  293.6 9.0 %collective-permute-start.9 = (f32[2,2,2,2,40,1024]{5,4,3,2,1,0:T(8,128)}, f32[2,2,2,2,40,1024]{5,4,3,2,1,0:T(8,128)}, u32[]{:S(2)}, u32[]{:S(2)}) collective-permute-start(f32[2,2,2,2,40,1024]{5,4,3,2,1,0:T(8,128)} %bitcast.424), channel_id=1, source_target_pairs={{0,1},{1,0},{2,3},{3,2},{4,5},{5,4},{6,7},{7,6},{8,9},{9,8},{10,11... | collective-permute-start | bytes 7864328 | tf_op jit(solution)/shard_map/ppermute | solution.py:50
  294.5 8.1 %copy-start.8 = (f32[16,40,1024]{2,1,0:T(8,128)S(1)}, f32[16,40,1024]{2,1,0:T(8,128)}, u32[]{:S(2)}) copy-start(f32[16,40,1024]{2,1,0:T(8,128)} %get-tuple-element.225) | copy-start | bytes 7864324
  308.2 34.6 %collective-permute-start.11 = (f32[2,2,2,40,1024]{4,3,2,1,0:T(8,128)}, f32[2,2,2,40,1024]{4,3,2,1,0:T(8,128)}, u32[]{:S(2)}, u32[]{:S(2)}) collective-permute-start(f32[2,2,2,40,1024]{4,3,2,1,0:T(8,128)} %add_bitcast_fusion.2), channel_id=1, source_target_pairs={{0,2},{1,3},{2,0},{3,1},{4,6},{5,7},{6,4},{7,5},{8,10},{9,11},{10,... | collective-permute-start | bytes 3932168 | tf_op jit(solution)/shard_map/ppermute | solution.py:50
  309.1 33.7 %collective-permute-start.10 = (f32[2,2,2,40,1024]{4,3,2,1,0:T(8,128)}, f32[2,2,2,40,1024]{4,3,2,1,0:T(8,128)S(1)}, u32[]{:S(2)}, u32[]{:S(2)}) collective-permute-start(f32[2,2,2,40,1024]{4,3,2,1,0:T(8,128)} %add_bitcast_fusion.3), channel_id=1, source_target_pairs={{0,4},{1,5},{2,6},{3,7},{4,0},{5,1},{6,2},{7,3},{8,12},{9,13},{10,... | collective-permute-start | bytes 3932168 | tf_op jit(solution)/shard_map/ppermute | solution.py:50
  346.5 22.9 %collective-permute-start.13 = (f32[2,2,40,1024]{3,2,1,0:T(8,128)S(1)}, f32[2,2,40,1024]{3,2,1,0:T(8,128)S(1)}, u32[]{:S(2)}, u32[]{:S(2)}) collective-permute-start(f32[2,2,40,1024]{3,2,1,0:T(8,128)S(1)} %bitcast_add_fusion.6), channel_id=1, source_target_pairs={{0,4},{1,5},{2,6},{3,7},{4,0},{5,1},{6,2},{7,3},{8,12},{9,13},{10,... | collective-permute-start | bytes 1966088 | tf_op jit(solution)/shard_map/ppermute | solution.py:50
  347.0 22.5 %collective-permute-start.12 = (f32[2,2,40,1024]{3,2,1,0:T(8,128)}, f32[2,2,40,1024]{3,2,1,0:T(8,128)S(1)}, u32[]{:S(2)}, u32[]{:S(2)}) collective-permute-start(f32[2,2,40,1024]{3,2,1,0:T(8,128)} %bitcast_add_fusion.7), channel_id=1, source_target_pairs={{0,2},{1,3},{2,0},{3,1},{4,6},{5,7},{6,4},{7,5},{8,10},{9,11},{10,... | collective-permute-start | bytes 1966088 | tf_op jit(solution)/shard_map/ppermute | solution.py:50
  369.5 20.6 %collective-permute-start.14 = (f32[2,2,2,2,40,1024]{5,4,3,2,1,0:T(8,128)}, f32[2,2,2,2,40,1024]{5,4,3,2,1,0:T(8,128)}, u32[]{:S(2)}, u32[]{:S(2)}) collective-permute-start(f32[2,2,2,2,40,1024]{5,4,3,2,1,0:T(8,128)} %bitcast.423), channel_id=1, source_target_pairs={{0,1},{1,0},{2,3},{3,2},{4,5},{5,4},{6,7},{7,6},{8,9},{9,8},{10,11... | collective-permute-start | bytes 7864328 | tf_op jit(solution)/shard_map/ppermute | solution.py:50
  369.6 20.5 %collective-permute-start.15 = (f32[2,2,2,2,40,1024]{5,4,3,2,1,0:T(8,128)}, f32[2,2,2,2,40,1024]{5,4,3,2,1,0:T(8,128)}, u32[]{:S(2)}, u32[]{:S(2)}) collective-permute-start(f32[2,2,2,2,40,1024]{5,4,3,2,1,0:T(8,128)} %bitcast.422), channel_id=1, source_target_pairs={{0,1},{1,0},{2,3},{3,2},{4,5},{5,4},{6,7},{7,6},{8,9},{9,8},{10,11... | collective-permute-start | bytes 7864328 | tf_op jit(solution)/shard_map/ppermute | solution.py:50
  373.3 16.8 %collective-permute-start.16 = (f32[2,80,1024]{2,1,0:T(8,128)S(1)}, f32[2,80,1024]{2,1,0:T(8,128)S(1)}, u32[]{:S(2)}, u32[]{:S(2)}) collective-permute-start(f32[2,80,1024]{2,1,0:T(8,128)S(1)} %fusion.13), channel_id=1, source_target_pairs={{0,8},{1,9},{2,10},{3,11},{4,12},{5,13},{6,14},{7,15},{8,0},{9,1},... | collective-permute-start | bytes 1966088 | tf_op jit(solution)/shard_map/ppermute | solution.py:50
  386.3 6.9 %copy-start.6 = (f32[16,40,1024]{2,1,0:T(8,128)S(1)}, f32[16,40,1024]{2,1,0:T(8,128)}, u32[]{:S(2)}) copy-start(f32[16,40,1024]{2,1,0:T(8,128)} %get-tuple-element.279) | copy-start | bytes 7864324
  396.7 32.1 %collective-permute-start.19 = (f32[80,1024]{1,0:T(8,128)S(1)}, f32[80,1024]{1,0:T(8,128)S(1)}, u32[]{:S(2)}, u32[]{:S(2)}) collective-permute-start(f32[80,1024]{1,0:T(8,128)S(1)} %dynamic-slice_bitcast_fusion.1), channel_id=1, source_target_pairs={{0,16},{1,17},{2,18},{3,19},{4,20},{5,21},{6,22},{7,23},{8,24},{9,... | collective-permute-start | bytes 983048 | tf_op jit(solution)/shard_map/ppermute | solution.py:50
  398.0 30.7 %collective-permute-start.18 = (f32[2,2,2,40,1024]{4,3,2,1,0:T(8,128)}, f32[2,2,2,40,1024]{4,3,2,1,0:T(8,128)}, u32[]{:S(2)}, u32[]{:S(2)}) collective-permute-start(f32[2,2,2,40,1024]{4,3,2,1,0:T(8,128)} %add_bitcast_fusion), channel_id=1, source_target_pairs={{0,2},{1,3},{2,0},{3,1},{4,6},{5,7},{6,4},{7,5},{8,10},{9,11},{10,... | collective-permute-start | bytes 3932168 | tf_op jit(solution)/shard_map/ppermute | solution.py:50
  399.3 29.7 %collective-permute-start.17 = (f32[2,2,2,40,1024]{4,3,2,1,0:T(8,128)}, f32[2,2,2,40,1024]{4,3,2,1,0:T(8,128)}, u32[]{:S(2)}, u32[]{:S(2)}) collective-permute-start(f32[2,2,2,40,1024]{4,3,2,1,0:T(8,128)} %add_bitcast_fusion.1), channel_id=1, source_target_pairs={{0,4},{1,5},{2,6},{3,7},{4,0},{5,1},{6,2},{7,3},{8,12},{9,13},{10,... | collective-permute-start | bytes 3932168 | tf_op jit(solution)/shard_map/ppermute | solution.py:50
  400.6 26.6 %collective-permute-start.22 = (f32[2,2,2,2,16,256]{5,4,3,2,1,0:T(8,128)}, f32[2,2,2,2,16,256]{5,4,3,2,1,0:T(8,128)}, u32[]{:S(2)}, u32[]{:S(2)}) collective-permute-start(f32[2,2,2,2,16,256]{5,4,3,2,1,0:T(8,128)} %dynamic-slice_bitcast_fusion.2), channel_id=1, source_target_pairs={{0,1},{1,0},{2,3},{3,2},{4,5},{5,4},{6,7},{7,6},{8,9},{9,8},{10,11... | collective-permute-start | bytes 786440 | tf_op jit(solution)/shard_map/ppermute | solution.py:50
  418.5 12.7 %copy-start.31 = (f32[1,512]{1,0:T(1,128)S(1)}, f32[1,512]{1,0:T(1,128)}, u32[]{:S(2)}) copy-start(f32[1,512]{1,0:T(1,128)} %get-tuple-element.305) | copy-start | bytes 6148
  418.5 13.4 %copy-start.30 = (f32[1,512]{1,0:T(1,128)S(1)}, f32[1,512]{1,0:T(1,128)}, u32[]{:S(2)}) copy-start(f32[1,512]{1,0:T(1,128)} %get-tuple-element.307) | copy-start | bytes 6148
  418.5 13.4 %copy-start.29 = (f32[1,4,2,128]{3,1,2,0:T(4,128)S(1)}, f32[1,4,2,128]{3,1,2,0:T(4,128)}, u32[]{:S(2)}) copy-start(f32[1,4,2,128]{3,1,2,0:T(4,128)} %copy.130) | copy-start | bytes 12292
  418.5 13.4 %copy-start.24 = (f32[32,512]{1,0:T(8,128)S(1)}, f32[32,512]{1,0:T(8,128)}, u32[]{:S(2)}) copy-start(f32[32,512]{1,0:T(8,128)} %get-tuple-element.303) | copy-start | bytes 196612
  418.5 14.2 %copy-start.28 = (f32[1,4,2,128]{3,1,2,0:T(4,128)S(1)}, f32[1,4,2,128]{3,1,2,0:T(4,128)}, u32[]{:S(2)}) copy-start(f32[1,4,2,128]{3,1,2,0:T(4,128)} %copy.131) | copy-start | bytes 12292
  418.5 14.3 %copy-start.7 = (f32[16,40,1024]{2,1,0:T(8,128)S(1)}, f32[16,40,1024]{2,1,0:T(8,128)}, u32[]{:S(2)}) copy-start(f32[16,40,1024]{2,1,0:T(8,128)} %get-tuple-element.279) | copy-start | bytes 7864324
  429.9 7.7 %collective-permute-start.20 = (f32[2,2,2,2,16,256]{5,4,3,2,1,0:T(8,128)S(1)}, f32[2,2,2,2,16,256]{5,4,3,2,1,0:T(8,128)}, u32[]{:S(2)}, u32[]{:S(2)}) collective-permute-start(f32[2,2,2,2,16,256]{5,4,3,2,1,0:T(8,128)S(1)} %dynamic-slice_bitcast_fusion.3), channel_id=1, source_target_pairs={{0,1},{1,0},{2,3},{3,2},{4,5},{5,4},{6,7},{7,6},{8,9},{9,8},{10,11... | collective-permute-start | bytes 786440 | tf_op jit(solution)/shard_map/ppermute | solution.py:50
  440.3 21.2 %all-to-all-start.5 = ((f32[32,40,128]{2,1,0:T(8,128)}), f32[32,40,128]{2,1,0:T(8,128)S(1)}, u32[]{:S(2)}, u32[]{:S(2)}) async-start(f32[32,40,128]{2,1,0:T(8,128)} %bitcast.358), calls=%async_computation.5 | async-start | bytes 1310720 | tf_op jit(solution)/shard_map/all_to_all | solution.py:203
  443.6 24.1 %collective-permute-start.25 = (f32[2,2,40,1024]{3,2,1,0:T(8,128)}, f32[2,2,40,1024]{3,2,1,0:T(8,128)}, u32[]{:S(2)}, u32[]{:S(2)}) collective-permute-start(f32[2,2,40,1024]{3,2,1,0:T(8,128)} %bitcast_add_fusion.2), channel_id=1, source_target_pairs={{0,4},{1,5},{2,6},{3,7},{4,0},{5,1},{6,2},{7,3},{8,12},{9,13},{10,... | collective-permute-start | bytes 1966088 | tf_op jit(solution)/shard_map/ppermute | solution.py:50
  445.5 22.1 %collective-permute-start.24 = (f32[2,2,40,1024]{3,2,1,0:T(8,128)}, f32[2,2,40,1024]{3,2,1,0:T(8,128)}, u32[]{:S(2)}, u32[]{:S(2)}) collective-permute-start(f32[2,2,40,1024]{3,2,1,0:T(8,128)} %bitcast_add_fusion.3), channel_id=1, source_target_pairs={{0,2},{1,3},{2,0},{3,1},{4,6},{5,7},{6,4},{7,5},{8,10},{9,11},{10,... | collective-permute-start | bytes 1966088 | tf_op jit(solution)/shard_map/ppermute | solution.py:50
  448.9 13.6 %collective-permute-start.23 = (f32[2,2,2,16,256]{4,3,2,1,0:T(8,128)}, f32[2,2,2,16,256]{4,3,2,1,0:T(8,128)}, u32[]{:S(2)}, u32[]{:S(2)}) collective-permute-start(f32[2,2,2,16,256]{4,3,2,1,0:T(8,128)} %bitcast_add_fusion.10), channel_id=1, source_target_pairs={{0,8},{1,9},{2,10},{3,11},{4,12},{5,13},{6,14},{7,15},{8,0},{9,1},... | collective-permute-start | bytes 393224 | tf_op jit(solution)/shard_map/ppermute | solution.py:50
  450.4 12.3 %collective-permute-start.21 = (f32[2,2,2,16,256]{4,3,2,1,0:T(8,128)}, f32[2,2,2,16,256]{4,3,2,1,0:T(8,128)}, u32[]{:S(2)}, u32[]{:S(2)}) collective-permute-start(f32[2,2,2,16,256]{4,3,2,1,0:T(8,128)} %bitcast_add_fusion.11), channel_id=1, source_target_pairs={{0,8},{1,9},{2,10},{3,11},{4,12},{5,13},{6,14},{7,15},{8,0},{9,1},... | collective-permute-start | bytes 393224 | tf_op jit(solution)/shard_map/ppermute | solution.py:50
  473.8 6.1 %copy-start.11 = (f32[2,80,1024]{2,1,0:T(8,128)S(1)}, f32[2,80,1024]{2,1,0:T(8,128)}, u32[]{:S(2)}) copy-start(f32[2,80,1024]{2,1,0:T(8,128)} %copy-done.10) | copy-start | bytes 1966084
  473.8 6.1 %copy-start.17 = (f32[80,1024]{1,0:T(8,128)S(1)}, f32[80,1024]{1,0:T(8,128)}, u32[]{:S(2)}) copy-start(f32[80,1024]{1,0:T(8,128)} %copy-done.16) | copy-start | bytes 983044
  473.8 8.5 %copy-start.25 = (f32[2,2,16,256]{3,2,1,0:T(8,128)S(1)}, f32[2,2,16,256]{3,2,1,0:T(8,128)}, u32[]{:S(2)}) copy-start(f32[2,2,16,256]{3,2,1,0:T(8,128)} %bitcast_add_fusion.14) | copy-start | bytes 196612
  473.9 24.4 %collective-permute-start.26 = (f32[2,80,1024]{2,1,0:T(8,128)S(1)}, f32[2,80,1024]{2,1,0:T(8,128)}, u32[]{:S(2)}, u32[]{:S(2)}) collective-permute-start(f32[2,80,1024]{2,1,0:T(8,128)S(1)} %fusion.8), channel_id=1, source_target_pairs={{0,8},{1,9},{2,10},{3,11},{4,12},{5,13},{6,14},{7,15},{8,0},{9,1},... | collective-permute-start | bytes 1966088 | tf_op jit(solution)/shard_map/ppermute | solution.py:50
  476.3 22.0 %all-to-all-start.6 = ((f32[32,16,128]{2,1,0:T(8,128)}), f32[32,16,128]{2,1,0:T(8,128)S(1)}, u32[]{:S(2)}, u32[]{:S(2)}) async-start(f32[32,16,128]{2,1,0:T(8,128)} %bitcast.181), calls=%async_computation.6 | async-start | bytes 524288 | tf_op jit(solution)/shard_map/all_to_all | solution.py:203
  482.3 17.3 %collective-permute-start.28 = (f32[2,2,16,256]{3,2,1,0:T(8,128)S(1)}, f32[2,2,16,256]{3,2,1,0:T(8,128)S(1)}, u32[]{:S(2)}, u32[]{:S(2)}) collective-permute-start(f32[2,2,16,256]{3,2,1,0:T(8,128)S(1)} %copy-done.25), channel_id=1, source_target_pairs={{0,16},{1,17},{2,18},{3,19},{4,20},{5,21},{6,22},{7,23},{8,24},{9,... | collective-permute-start | bytes 196616 | tf_op jit(solution)/shard_map/ppermute | solution.py:50
  485.0 14.6 %collective-permute-start.27 = (f32[2,2,16,256]{3,2,1,0:T(8,128)S(1)}, f32[2,2,16,256]{3,2,1,0:T(8,128)S(1)}, u32[]{:S(2)}, u32[]{:S(2)}) collective-permute-start(f32[2,2,16,256]{3,2,1,0:T(8,128)S(1)} %bitcast_add_fusion.12), channel_id=1, source_target_pairs={{0,16},{1,17},{2,18},{3,19},{4,20},{5,21},{6,22},{7,23},{8,24},{9,... | collective-permute-start | bytes 196616 | tf_op jit(solution)/shard_map/ppermute | solution.py:50
  499.6 17.7 %collective-permute-start.33 = (f32[80,1024]{1,0:T(8,128)S(1)}, f32[80,1024]{1,0:T(8,128)S(1)}, u32[]{:S(2)}, u32[]{:S(2)}) collective-permute-start(f32[80,1024]{1,0:T(8,128)S(1)} %dynamic-slice_bitcast_fusion), channel_id=1, source_target_pairs={{0,16},{1,17},{2,18},{3,19},{4,20},{5,21},{6,22},{7,23},{8,24},{9,... | collective-permute-start | bytes 983048 | tf_op jit(solution)/shard_map/ppermute | solution.py:50
  500.9 4.0 collective-permute-start.29
  502.5 4.2 collective-permute-start.31
  504.9 3.8 collective-permute-start.30
  506.8 3.8 collective-permute-start.32
  511.2 23.4 %copy-start.1 = (f32[2,16,512]{2,1,0:T(8,128)S(1)}, f32[2,16,512]{2,1,0:T(8,128)}, u32[]{:S(2)}) copy-start(f32[2,16,512]{2,1,0:T(8,128)} %param.26) | copy-start | bytes 196612
  (16 other events, 43.7 us)
Sparse Core Ops, SparseCore 0:
  11.4 125.9 all-gather.6
  144.3 92.6 all-gather.8
  239.8 76.0 all-gather.10

commit v4 on v3

--- a/solution.py
+++ b/solution.py
@@ -397,7 +397,7 @@
     return jax.ShapeDtypeStruct(tuple(size for size in sizes if isinstance(size, int)), dtype)
 
 
-def kernel_call(kernel, grid, in_specs, out_specs, out_shapes, scratch, macs):
+def kernel_call(kernel, grid, in_specs, out_specs, out_shapes, scratch, macs, mebibytes=52):
     return pl.pallas_call(
         kernel,
         grid=grid,
@@ -405,8 +405,8 @@
         out_specs=out_specs,
         out_shape=[shape_of(*shape) for shape in out_shapes],
         scratch_shapes=scratch,
-        compiler_params=pltpu.CompilerParams(vmem_limit_bytes=60 * 2**20),
-        cost_estimate=pl.CostEstimate(flops=6 * macs, bytes_accessed=16 * 2**20, transcendentals=0),
+        compiler_params=pltpu.CompilerParams(vmem_limit_bytes=mebibytes * 2**20),
+        cost_estimate=pl.CostEstimate(flops=1 * macs, bytes_accessed=16 * 2**20, transcendentals=0),
     )
 
 

time: 547 us -> 540 us (0.987)
  local copies, waits for them, and re-layouts: 42.3 us -> 31.1 us
  waiting for transfers between devices: 151 us -> 159 us
    unnamed x90 -> x64, local copies, waits for them, and re-layouts: 14.4 us -> 7.81 us
  transfers between devices with their start and end apart: 44 -> 44, of which waited for: 20 -> 20; matrix products, arithmetic and copies ran while one was open for 16% -> 14% of each run, Pallas kernels for 34% -> 34%
where the time goes in v4:
time: 540 us; the launch traced here: 534 us
  Pallas kernels  188 us (35%)
  waiting for transfers between devices  159 us (29%)
  starting transfers between devices  65.6 us (12%)
  other arithmetic  50.9 us (9%)
  local copies, waits for them, and re-layouts  31.1 us (6%)
  between operations  16.7 us (3%)
  matrix products  12.2 us (2%)
  blocking collectives  11.5 us (2%)
    ppermute x34, waiting for transfers between devices, shift(): return lax.ppermute(block, AXIS, perm)  73.6 us
    all_to_all x6, waiting for transfers between devices, exchange(): lax.all_to_all(joined, AXIS, split_axis=0, concat_axis=0, tiled=True)  50.8 us
    pallas_call x2, Pallas kernels, layer_back_weights(): kernel_call(functools.partial(back_weights_kernel, dilation), (GATES // T...  43.1 us
    pallas_call x2, Pallas kernels, layer_gates(): kernel_call(functools.partial(gates_kernel, dilation), (3,), [fixed(count...  41.1 us
    ppermute x34, starting transfers between devices, shift(): return lax.ppermute(block, AXIS, perm)  37.7 us
    pallas_call x2, Pallas kernels, layer_back_frames(): kernel_call(functools.partial(back_frames_kernel, dilation), (2,), [fixed...  35.8 us
    pallas_call x2, Pallas kernels, layer_back_gates(): kernel_call(back_gates_kernel, (2,), [rows, rows, pl.BlockSpec((count //...  27.8 us
    all_to_all x1, waiting for transfers between devices, on_device(): keys = lax.all_to_all(sent, AXIS, split_axis=0, concat_axis=0, tiled=True)  25 us
  transfers between devices with their start and end apart: 44, of which 20 were waited for; matrix products, arithmetic and copies ran while one was open for 14% of the time, Pallas kernels for 34%

profile of v4, /device:TPU:0, one launch (start us, length us, event | category | flops | bytes accessed | tf_op | source)
XLA Modules:
  0.0 534.5 jit_solution(9348829776005484144)
XLA Ops:
  10.1 2.6 copy.95
  13.8 1.6 pad_maximum_fusion.1
  15.5 3.0 collective-permute-start
  18.5 2.6 collective-permute-start.1
  22.4 2.5 collective-permute-done
  25.0 8.4 %collective-permute-done.1 = f32[32,1024]{1,0:T(8,128)S(1)} collective-permute-done((f32[32,1024]{1,0:T(8,128)S(1)}, f32[32,1024]{1,0:T(8,128)S(1)}, u32[]{:S(2)}, u32[]{:S(2)}) %collective-permute-start.1) | collective-permute-done | bytes 131104 | tf_op jit(solution)/shard_map/ppermute | solution.py:50
  36.8 7.4 %all-to-all-start = ((f32[32,32,512]{2,1,0:T(8,128)}), f32[32,32,512]{2,1,0:T(8,128)S(1)}, u32[]{:S(2)}, u32[]{:S(2)}) async-start(f32[32,32,512]{2,1,0:T(8,128)} %pad_maximum_fusion.1), calls=%async_computation | async-start | bytes 4194304 | tf_op jit(solution)/shard_map/all_to_all | solution.py:692
  45.5 1.8 collective-permute-start.6
  48.9 38.3 %collective-permute-done.6 = f32[2,4,16,1024]{3,2,0,1:T(8,128)S(1)} collective-permute-done((f32[2,4,16,1024]{3,2,0,1:T(8,128)S(1)}, f32[2,4,16,1024]{3,2,0,1:T(8,128)S(1)}, u32[]{:S(2)}, u32[]{:S(2)}) %collective-permute-start.6) | collective-permute-done | bytes 524320 | tf_op jit(solution)/shard_map/ppermute | solution.py:50
  90.6 3.1 collective-permute-done.7
  93.7 2.8 select_bitcast_fusion.1
  97.6 2.0 copy-done.3
  101.2 3.1 copy.103
  104.3 25.0 %all-to-all-done = f32[32,32,512]{2,1,0:T(8,128)S(1)} async-done(((f32[32,32,512]{2,1,0:T(8,128)}), f32[32,32,512]{2,1,0:T(8,128)S(1)}, u32[]{:S(2)}, u32[]{:S(2)}) %all-to-all-start) | async-done | bytes 2097184 | tf_op jit(solution)/shard_map/all_to_all | solution.py:692
  129.8 3.1 fusion
  133.9 2.8 convolution_multiply_fusion
  136.7 3.7 select_reduce_fusion
  140.9 2.1 bitcast_reduce_fusion
  146.0 3.3 all-to-all-start.1
  149.5 12.9 %all-to-all-done.1 = f32[32,16,128]{2,1,0:T(8,128)S(1)} async-done(((f32[32,16,128]{2,1,0:T(8,128)}), f32[32,16,128]{2,1,0:T(8,128)S(1)}, u32[]{:S(2)}, u32[]{:S(2)}) %all-to-all-start.1) | async-done | bytes 262176 | tf_op jit(solution)/shard_map/all_to_all | solution.py:203
  164.8 3.9 all-to-all-start.2
  168.7 8.3 %all-to-all-done.2 = f32[32,8,128]{2,1,0:T(8,128)S(1)} async-done(((f32[32,8,128]{2,1,0:T(8,128)}), f32[32,8,128]{2,1,0:T(8,128)S(1)}, u32[]{:S(2)}, u32[]{:S(2)}) %all-to-all-start.2) | async-done | bytes 131104 | tf_op jit(solution)/shard_map/all_to_all | solution.py:203
  179.0 2.6 all-to-all-start.3
  183.0 8.7 %all-to-all-done.3 = f32[32,8,128]{2,1,0:T(8,128)S(1)} async-done(((f32[32,8,128]{2,1,0:T(8,128)}), f32[32,8,128]{2,1,0:T(8,128)S(1)}, u32[]{:S(2)}, u32[]{:S(2)}) %all-to-all-start.3) | async-done | bytes 131104 | tf_op jit(solution)/shard_map/all_to_all | solution.py:203
  193.3 3.5 all-to-all-start.4
  196.9 21.2 %shard_map.282 = (f32[1024,512]{1,0:T(8,128)}, f32[1024,512]{1,0:T(8,128)}) custom-call(f32[1024,512]{1,0:T(8,128)} %bitcast.370, f32[1024,512]{1,0:T(8,128)} %bitcast.364, f32[32,80,1024]{2,1,0:T(8,128)} %bitcast.346, f32[32,80,1024]{2,1,0:T(8,128)} %bitcast.347, f32[1,512]{1,0:T(1,128)S(1)} %bitcast.330, f32[1024,1]{1,0:T(8,128)S(1)} %fusion.18.live), custom_call_target="tpu_custom_call" | custom-call | flops 2147483648 | bytes 16777216 | tf_op jit(solution)/shard_map/pallas_call | solution.py:459
  219.8 7.8 %shard_map.283 = (f32[1024,512]{1,0:T(8,128)}, f32[1024,512]{1,0:T(8,128)}) custom-call(f32[1024,512]{1,0:T(8,128)} %get-tuple-element.198.tanh, f32[1024,512]{1,0:T(8,128)} %get-tuple-element.199.sig, f32[2,512]{1,0:T(2,128)S(1)} %reshape_squeeze.8.film, f32[32,80,1024]{2,1,0:T(8,128)} %bitcast.348, f32[1024,512]{1,0:T(8,128)} %bitcast.371, ...), custom_call_target="tpu_custom_call" | custom-call | flops 536870912 | bytes 16777216 | tf_op jit(solution)/shard_map/pallas_call | solution.py:489
  227.6 9.5 %all-gather.9.cloned.1.call-done = f32[2560,1024]{1,0:T(8,128)} async-done(((f32[80,1024]{1,0:T(8,128)}), f32[2560,1024]{1,0:T(8,128)}) %all-gather.9.cloned.1.call-update) | async-done | bytes 10485776 | tf_op jit(solution)/shard_map/all_gather | solution.py:729
  237.1 19.9 %shard_map.284 = (f32[1024,512]{1,0:T(8,128)}, f32[1024,512]{1,0:T(8,128)}) custom-call(f32[1024,512]{1,0:T(8,128)} %get-tuple-element.203.frames, f32[1024,512]{1,0:T(8,128)} %bitcast.365, f32[32,80,1024]{2,1,0:T(8,128)} %bitcast.351, f32[32,80,1024]{2,1,0:T(8,128)} %bitcast.352, f32[1,512]{1,0:T(1,128)S(1)} %bitcast.332, f32[1024,1]{1,0:T(8,128)S(1)} %fusion.18.live), custom_call_target="tpu_custom_call" | custom-call | flops 2147483648 | bytes 16777216 | tf_op jit(solution)/shard_map/pallas_call | solution.py:459
  257.0 13.9 %shard_map.285 = (bf16[1024,1024]{1,0:T(8,128)(2,1)}, bf16[1024,1024]{1,0:T(8,128)(2,1)}, f32[2,512]{1,0:T(2,128)S(1)}, f32[512,1024]{1,0:T(8,128)}) custom-call(f32[1024,512]{1,0:T(8,128)} %bitcast.377, f32[1024,512]{1,0:T(8,128)} %bitcast.379, f32[1024,1]{1,0:T(8,128)S(1)} %fusion.18.live, f32[1024,512]{1,0:T(8,128)} %get-tuple-element.216.tanh, ...), custom_call_target="tpu_custom_call" | custom-call | flops 1073741824 | bytes 16777216 | tf_op jit(solution)/shard_map/pallas_call | solution.py:539
  270.9 21.5 %shard_map.286 = (f32[16,40,1024]{2,1,0:T(8,128)}, f32[16,40,1024]{2,1,0:T(8,128)}, f32[16,40,1024]{2,1,0:T(8,128)}, f32[16,40,1024]{2,1,0:T(8,128)}) custom-call(s32[1]{0:T(128)} %bitcast.core, f32[1024,512]{1,0:T(8,128)} %get-tuple-element.203.frames, f32[1024,512]{1,0:T(8,128)} %bitcast.366, f32[1,512]{1,0:T(1,128)S(1)} %bitcast.333, ...), custom_call_target="tpu_custom_call" | custom-call | flops 2147483648 | bytes 16777216 | tf_op jit(solution)/shard_map/pallas_call | solution.py:595
  292.9 8.0 %shard_map.287 = (f32[1024,512]{1,0:T(8,128)}, f32[1024,512]{1,0:T(8,128)}) custom-call(f32[1024,512]{1,0:T(8,128)} %get-tuple-element.216.tanh, f32[1024,512]{1,0:T(8,128)} %get-tuple-element.217.sig, f32[2,512]{1,0:T(2,128)S(1)} %reshape_squeeze.9.film, f32[32,80,1024]{2,1,0:T(8,128)} %bitcast.354, f32[1024,512]{1,0:T(8,128)} %get-tuple-element.203.frames, ...), custom_call_target="tpu_custom_call" | custom-call | flops 536870912 | bytes 16777216 | tf_op jit(solution)/shard_map/pallas_call | solution.py:489
  301.5 2.8 add_bitcast_fusion.3
  304.4 2.7 add_bitcast_fusion.2
  309.7 18.1 %shard_map.288 = (f32[1024,512]{1,0:T(8,128)}, f32[1,512]{1,0:T(1,128)S(1)}) custom-call(bf16[1024,1024]{1,0:T(8,128)(2,1)} %get-tuple-element.235.pre_high, bf16[1024,1024]{1,0:T(8,128)(2,1)} %get-tuple-element.236.pre_low, f32[32,80,1024]{2,1,0:T(8,128)} %bitcast.355, f32[1024,512]{1,0:T(8,128)} %bitcast.378, f32[1024,1]{1,0:T(8,128)S(1)} %fusion.18.live), custom_call_target="tpu_custom_call" | custom-call | flops 1610612736 | bytes 16777216 | tf_op jit(solution)/shard_map/pallas_call | solution.py:636
  327.8 13.8 %shard_map.289 = (bf16[1024,1024]{1,0:T(8,128)(2,1)}, bf16[1024,1024]{1,0:T(8,128)(2,1)}, f32[2,512]{1,0:T(2,128)S(1)}, f32[512,1024]{1,0:T(8,128)}) custom-call(f32[1024,512]{1,0:T(8,128)} %get-tuple-element.297.grad_frames, f32[1024,512]{1,0:T(8,128)} %bitcast.380, f32[1024,1]{1,0:T(8,128)S(1)} %fusion.18.live, f32[1024,512]{1,0:T(8,128)} %get-tuple-element.198.tanh, ...), custom_call_target="tpu_custom_call" | custom-call | flops 1073741824 | bytes 16777216 | tf_op jit(solution)/shard_map/pallas_call | solution.py:539
  346.2 21.6 %shard_map.290 = (f32[16,40,1024]{2,1,0:T(8,128)}, f32[16,40,1024]{2,1,0:T(8,128)}, f32[16,40,1024]{2,1,0:T(8,128)}, f32[16,40,1024]{2,1,0:T(8,128)}) custom-call(s32[1]{0:T(128)} %bitcast.core, f32[1024,512]{1,0:T(8,128)} %bitcast.372, f32[1024,512]{1,0:T(8,128)} %bitcast.367, f32[1,512]{1,0:T(1,128)S(1)} %bitcast.331, f32[1024,1]{1,0:T(8,128)S(1)} %fusion.18.live, ...), custom_call_target="tpu_custom_call" | custom-call | flops 2147483648 | bytes 16777216 | tf_op jit(solution)/shard_map/pallas_call | solution.py:595
  368.4 1.7 fusion.16
  370.1 1.7 fusion.17
  372.6 7.9 %shard_map.291 = (f32[512,256]{1,0:T(8,128)S(1)}, f32[32,512]{1,0:T(8,128)S(1)}, f32[1,512]{1,0:T(1,128)S(1)}, f32[1,512]{1,0:T(1,128)S(1)}) custom-call(f32[1,1024]{1,0:T(1,128)S(1)} %bitcast.335, f32[32,2,2,16,1024]{4,3,2,1,0:T(8,128)} %bitcast.356, f32[32,2,2,16,1024]{4,3,2,1,0:T(8,128)} %bitcast.357, f32[2,512,512]{2,1,0:T(8,128)} %slice.134.key_w, ...), custom_call_target="tpu_custom_call" | custom-call | flops 335544320 | bytes 16777216 | tf_op jit(solution)/shard_map/pallas_call | solution.py:281
  380.5 8.2 %collective-permute-done.16 = f32[2,80,1024]{2,1,0:T(8,128)} collective-permute-done((f32[2,80,1024]{2,1,0:T(8,128)S(1)}, f32[2,80,1024]{2,1,0:T(8,128)}, u32[]{:S(2)}, u32[]{:S(2)}) %collective-permute-start.16) | collective-permute-done | bytes 655392 | tf_op jit(solution)/shard_map/ppermute | solution.py:50
  388.8 2.6 add_bitcast_fusion.1
  391.4 2.7 add_bitcast_fusion
  399.3 7.8 %shard_map.292 = (f32[512,256]{1,0:T(8,128)S(1)}, f32[32,512]{1,0:T(8,128)S(1)}, f32[1,512]{1,0:T(1,128)S(1)}, f32[1,512]{1,0:T(1,128)S(1)}) custom-call(f32[1,1024]{1,0:T(1,128)S(1)} %bitcast.334, f32[32,2,2,16,1024]{4,3,2,1,0:T(8,128)} %bitcast.358, f32[32,2,2,16,1024]{4,3,2,1,0:T(8,128)} %bitcast.359, f32[2,512,512]{2,1,0:T(8,128)} %slice.134.key_w, ...), custom_call_target="tpu_custom_call" | custom-call | flops 335544320 | bytes 16777216 | tf_op jit(solution)/shard_map/pallas_call | solution.py:281
  407.0 17.7 %shard_map.293 = (f32[1024,512]{1,0:T(8,128)}, f32[1,512]{1,0:T(1,128)S(1)}) custom-call(bf16[1024,1024]{1,0:T(8,128)(2,1)} %get-tuple-element.295.pre_high, bf16[1024,1024]{1,0:T(8,128)(2,1)} %get-tuple-element.296.pre_low, f32[32,80,1024]{2,1,0:T(8,128)} %bitcast.350, f32[1024,512]{1,0:T(8,128)} %get-tuple-element.297.grad_frames, f32[1024,1]{1,0:T(8,128)S(1)} %fusion.18.live), custom_call_target="tpu_custom_call" | custom-call | flops 1610612736 | bytes 16777216 | tf_op jit(solution)/shard_map/pallas_call | solution.py:636
  426.8 2.5 bitcast_add_fusion.2
  429.3 2.5 bitcast_add_fusion.3
  432.9 3.1 all-to-all-start.5
  436.0 1.8 collective-permute-start.25
  444.1 9.8 %all-to-all-done.5 = f32[32,40,128]{2,1,0:T(8,128)S(1)} async-done(((f32[32,40,128]{2,1,0:T(8,128)}), f32[32,40,128]{2,1,0:T(8,128)S(1)}, u32[]{:S(2)}, u32[]{:S(2)}) %all-to-all-start.5) | async-done | bytes 655392 | tf_op jit(solution)/shard_map/all_to_all | solution.py:203
  455.1 4.9 collective-permute-done.25
  461.9 1.9 fusion.14
  463.8 1.9 fusion.15
  468.9 3.9 all-to-all-start.6
  472.9 1.7 bitcast_add_fusion.8.refs_1_.sums_1
  475.5 2.8 collective-permute-start.28
  480.1 11.0 %all-to-all-done.6 = f32[32,16,128]{2,1,0:T(8,128)S(1)} async-done(((f32[32,16,128]{2,1,0:T(8,128)}), f32[32,16,128]{2,1,0:T(8,128)S(1)}, u32[]{:S(2)}, u32[]{:S(2)}) %all-to-all-start.6) | async-done | bytes 262176 | tf_op jit(solution)/shard_map/all_to_all | solution.py:203
  497.8 1.8 collective-permute-start.30
  501.6 1.8 collective-permute-done.32
  504.1 3.5 shard_map.294
  507.6 2.6 collective-permute-done.33
  511.0 2.6 shard_map.295
  513.6 11.5 %all_to_all.40.squares = f32[32,8,128]{2,1,0:T(8,128)} all-to-all(f32[32,8,128]{2,1,0:T(8,128)} %shard_map.295), channel_id=1, replica_groups=mesh['items'=32] {'items'}, dimensions={0} | all-to-all | bytes 262144 | tf_op jit(solution)/shard_map/all_to_all | solution.py:848
  525.1 2.4 shard_map.296
  (251 shorter events, 73.3 us)
Async XLA Ops:
  7.2 137.4 %copy-start = (f32[2,16,512]{2,1,0:T(8,128)S(1)}, f32[2,16,512]{2,1,0:T(8,128)}, u32[]{:S(2)}) copy-start(f32[2,16,512]{2,1,0:T(8,128)} %param.26) | copy-start | bytes 196612
  7.2 136.9 %all-gather.7.cloned.1.call-start = ((), (), s32[]{:S(2)}) async-start(), calls=%async_computation.8 | async-start | bytes 10813440 | tf_op jit(solution)/shard_map/all_gather | solution.py:680
  10.0 2.7 copy-start.18
  10.0 3.4 copy-start.20
  10.0 3.8 copy-start.14
  10.0 3.8 copy-start.19
  15.5 9.5 %collective-permute-start = (f32[32,1024]{1,0:T(8,128)S(1)}, f32[32,1024]{1,0:T(8,128)S(1)}, u32[]{:S(2)}, u32[]{:S(2)}) collective-permute-start(f32[32,1024]{1,0:T(8,128)S(1)} %bitcast.418), channel_id=1, source_target_pairs={{0,8},{1,9},{2,10},{3,11},{4,12},{5,13},{6,14},{7,15},{8,16},{9,17... | collective-permute-start | bytes 393224 | tf_op jit(solution)/shard_map/ppermute | solution.py:50
  18.5 14.9 %collective-permute-start.1 = (f32[32,1024]{1,0:T(8,128)S(1)}, f32[32,1024]{1,0:T(8,128)S(1)}, u32[]{:S(2)}, u32[]{:S(2)}) collective-permute-start(f32[32,1024]{1,0:T(8,128)S(1)} %bitcast.419), channel_id=1, source_target_pairs={{0,16},{1,17},{2,18},{3,19},{4,20},{5,21},{6,22},{7,23},{8,24},{9,... | collective-permute-start | bytes 393224 | tf_op jit(solution)/shard_map/ppermute | solution.py:50
  21.1 12.6 %collective-permute-start.2 = (f32[32,1024]{1,0:T(8,128)S(1)}, f32[32,1024]{1,0:T(8,128)S(1)}, u32[]{:S(2)}, u32[]{:S(2)}) collective-permute-start(f32[32,1024]{1,0:T(8,128)S(1)} %bitcast.420), channel_id=1, source_target_pairs={{0,24},{1,25},{2,26},{3,27},{4,28},{5,29},{6,30},{7,31},{8,0},{9,1... | collective-permute-start | bytes 393224 | tf_op jit(solution)/shard_map/ppermute | solution.py:50
  33.8 10.6 %collective-permute-start.3 = (f32[4,16,1024]{2,1,0:T(8,128)S(1)}, f32[4,16,1024]{2,1,0:T(8,128)}, u32[]{:S(2)}, u32[]{:S(2)}) collective-permute-start(f32[4,16,1024]{2,1,0:T(8,128)S(1)} %get-tuple-element.383), channel_id=1, source_target_pairs={{0,2},{1,3},{2,0},{3,1},{4,6},{5,7},{6,4},{7,5},{8,10},{9,11},{10,... | collective-permute-start | bytes 786440 | tf_op jit(solution)/shard_map/ppermute | solution.py:50
  35.2 9.1 %collective-permute-start.5 = (f32[4,16,1024]{2,1,0:T(8,128)S(1)}, f32[4,16,1024]{2,1,0:T(8,128)}, u32[]{:S(2)}, u32[]{:S(2)}) collective-permute-start(f32[4,16,1024]{2,1,0:T(8,128)S(1)} %get-tuple-element.384), channel_id=1, source_target_pairs={{0,4},{1,5},{2,6},{3,7},{4,0},{5,1},{6,2},{7,3},{8,12},{9,13},{10,... | collective-permute-start | bytes 786440 | tf_op jit(solution)/shard_map/ppermute | solution.py:50
  36.8 92.5 %all-to-all-start = ((f32[32,32,512]{2,1,0:T(8,128)}), f32[32,32,512]{2,1,0:T(8,128)S(1)}, u32[]{:S(2)}, u32[]{:S(2)}) async-start(f32[32,32,512]{2,1,0:T(8,128)} %pad_maximum_fusion.1), calls=%async_computation | async-start | bytes 4194304 | tf_op jit(solution)/shard_map/all_to_all | solution.py:692
  44.2 192.9 %all-gather.9.cloned.1.call-start = ((), (), s32[]{:S(2)}) async-start(), calls=%async_computation.9 | async-start | bytes 10813440 | tf_op jit(solution)/shard_map/all_gather | solution.py:729
  45.5 41.8 %collective-permute-start.6 = (f32[2,4,16,1024]{3,2,0,1:T(8,128)S(1)}, f32[2,4,16,1024]{3,2,0,1:T(8,128)S(1)}, u32[]{:S(2)}, u32[]{:S(2)}) collective-permute-start(f32[2,4,16,1024]{3,2,0,1:T(8,128)S(1)} %pad_maximum_fusion.4), channel_id=1, source_target_pairs={{0,2},{1,3},{2,0},{3,1},{4,6},{5,7},{6,4},{7,5},{8,10},{9,11},{10,... | collective-permute-start | bytes 1572872 | tf_op jit(solution)/shard_map/ppermute | solution.py:50
  47.4 40.1 %collective-permute-start.4 = (f32[2,4,16,1024]{3,2,1,0:T(8,128)S(1)}, f32[2,4,16,1024]{3,2,1,0:T(8,128)S(1)}, u32[]{:S(2)}, u32[]{:S(2)}) collective-permute-start(f32[2,4,16,1024]{3,2,1,0:T(8,128)S(1)} %pad_maximum_fusion.3), channel_id=1, source_target_pairs={{0,4},{1,5},{2,6},{3,7},{4,0},{5,1},{6,2},{7,3},{8,12},{9,13},{10,... | collective-permute-start | bytes 1572872 | tf_op jit(solution)/shard_map/ppermute | solution.py:50
  89.2 4.5 collective-permute-start.7
  97.6 2.0 copy-start.3
  129.3 13.7 %copy-start.2 = (f32[32,32,512]{2,1,0:T(8,128)}, f32[32,32,512]{2,1,0:T(8,128)S(1)}, u32[]{:S(2)}) copy-start(f32[32,32,512]{2,1,0:T(8,128)S(1)} %all-to-all-done) | copy-start | bytes 6291460
  129.7 3.3 copy-start.21
  144.1 5.3 copy-start.12
  144.6 18.6 %copy-start.16 = (f32[32,16]{1,0:T(8,128)}, f32[32,16]{1,0:T(8,128)S(1)}, u32[]{:S(2)}) copy-start(f32[32,16]{1,0:T(8,128)S(1)} %fusion.34.embeds) | copy-start | bytes 6148
  146.0 16.4 %all-to-all-start.1 = ((f32[32,16,128]{2,1,0:T(8,128)}), f32[32,16,128]{2,1,0:T(8,128)S(1)}, u32[]{:S(2)}, u32[]{:S(2)}) async-start(f32[32,16,128]{2,1,0:T(8,128)} %bitcast.163), calls=%async_computation.1 | async-start | bytes 524288 | tf_op jit(solution)/shard_map/all_to_all | solution.py:203
  149.4 19.4 %copy-start.13 = (f32[2,16,512]{2,1,0:T(8,128)S(1)}, f32[2,16,512]{2,1,0:T(8,128)}, u32[]{:S(2)}) copy-start(f32[2,16,512]{2,1,0:T(8,128)} %param.34) | copy-start | bytes 196612
  164.0 17.6 %copy-start.10 = (f32[2,16,1024]{2,1,0:T(8,128)S(1)}, f32[2,16,1024]{2,1,0:T(8,128)}, u32[]{:S(2)}) copy-start(f32[2,16,1024]{2,1,0:T(8,128)} %param.35) | copy-start | bytes 393220
  164.8 12.2 %all-to-all-start.2 = ((f32[32,8,128]{2,1,0:T(8,128)}), f32[32,8,128]{2,1,0:T(8,128)S(1)}, u32[]{:S(2)}, u32[]{:S(2)}) async-start(f32[32,8,128]{2,1,0:T(8,128)} %copy.112), calls=%async_computation.2 | async-start | bytes 262144 | tf_op jit(solution)/shard_map/all_to_all | solution.py:203
  179.0 12.7 %all-to-all-start.3 = ((f32[32,8,128]{2,1,0:T(8,128)}), f32[32,8,128]{2,1,0:T(8,128)S(1)}, u32[]{:S(2)}, u32[]{:S(2)}) async-start(f32[32,8,128]{2,1,0:T(8,128)} %copy.116), calls=%async_computation.3 | async-start | bytes 262144 | tf_op jit(solution)/shard_map/all_to_all | solution.py:203
  193.3 24.8 %all-to-all-start.4 = ((f32[32,16,128]{2,1,0:T(8,128)}), f32[32,16,128]{2,1,0:T(8,128)S(1)}, u32[]{:S(2)}, u32[]{:S(2)}) async-start(f32[32,16,128]{2,1,0:T(8,128)} %reshape.334), calls=%async_computation.4 | async-start | bytes 524288 | tf_op jit(solution)/shard_map/all_to_all | solution.py:203
  196.8 175.8 %all-gather.11.cloned.1.call-start = ((), (), s32[]{:S(2)}) async-start(), calls=%async_computation.10 | async-start | bytes 8650752 | tf_op jit(solution)/shard_map/all_gather | solution.py:763
  292.4 8.5 %collective-permute-start.8 = (f32[2,2,2,2,40,1024]{5,4,3,2,1,0:T(8,128)}, f32[2,2,2,2,40,1024]{5,4,3,2,1,0:T(8,128)}, u32[]{:S(2)}, u32[]{:S(2)}) collective-permute-start(f32[2,2,2,2,40,1024]{5,4,3,2,1,0:T(8,128)} %bitcast.433), channel_id=1, source_target_pairs={{0,1},{1,0},{2,3},{3,2},{4,5},{5,4},{6,7},{7,6},{8,9},{9,8},{10,11... | collective-permute-start | bytes 7864328 | tf_op jit(solution)/shard_map/ppermute | solution.py:50
  292.7 8.9 %collective-permute-start.9 = (f32[2,2,2,2,40,1024]{5,4,3,2,1,0:T(8,128)}, f32[2,2,2,2,40,1024]{5,4,3,2,1,0:T(8,128)}, u32[]{:S(2)}, u32[]{:S(2)}) collective-permute-start(f32[2,2,2,2,40,1024]{5,4,3,2,1,0:T(8,128)} %bitcast.432), channel_id=1, source_target_pairs={{0,1},{1,0},{2,3},{3,2},{4,5},{5,4},{6,7},{7,6},{8,9},{9,8},{10,11... | collective-permute-start | bytes 7864328 | tf_op jit(solution)/shard_map/ppermute | solution.py:50
  292.9 8.6 %copy-start.8 = (f32[16,40,1024]{2,1,0:T(8,128)S(1)}, f32[16,40,1024]{2,1,0:T(8,128)}, u32[]{:S(2)}) copy-start(f32[16,40,1024]{2,1,0:T(8,128)} %get-tuple-element.225) | copy-start | bytes 7864324
  300.9 3.4 copy-start.9
  307.1 34.5 %collective-permute-start.11 = (f32[2,2,2,40,1024]{4,3,2,1,0:T(8,128)}, f32[2,2,2,40,1024]{4,3,2,1,0:T(8,128)}, u32[]{:S(2)}, u32[]{:S(2)}) collective-permute-start(f32[2,2,2,40,1024]{4,3,2,1,0:T(8,128)} %add_bitcast_fusion.2), channel_id=1, source_target_pairs={{0,2},{1,3},{2,0},{3,1},{4,6},{5,7},{6,4},{7,5},{8,10},{9,11},{10,... | collective-permute-start | bytes 3932168 | tf_op jit(solution)/shard_map/ppermute | solution.py:50
  308.2 33.4 %collective-permute-start.10 = (f32[2,2,2,40,1024]{4,3,2,1,0:T(8,128)}, f32[2,2,2,40,1024]{4,3,2,1,0:T(8,128)}, u32[]{:S(2)}, u32[]{:S(2)}) collective-permute-start(f32[2,2,2,40,1024]{4,3,2,1,0:T(8,128)} %add_bitcast_fusion.3), channel_id=1, source_target_pairs={{0,4},{1,5},{2,6},{3,7},{4,0},{5,1},{6,2},{7,3},{8,12},{9,13},{10,... | collective-permute-start | bytes 3932168 | tf_op jit(solution)/shard_map/ppermute | solution.py:50
  344.7 23.1 %collective-permute-start.13 = (f32[2,2,40,1024]{3,2,1,0:T(8,128)S(1)}, f32[2,2,40,1024]{3,2,1,0:T(8,128)S(1)}, u32[]{:S(2)}, u32[]{:S(2)}) collective-permute-start(f32[2,2,40,1024]{3,2,1,0:T(8,128)S(1)} %bitcast_add_fusion.6), channel_id=1, source_target_pairs={{0,4},{1,5},{2,6},{3,7},{4,0},{5,1},{6,2},{7,3},{8,12},{9,13},{10,... | collective-permute-start | bytes 1966088 | tf_op jit(solution)/shard_map/ppermute | solution.py:50
  345.2 22.6 %collective-permute-start.12 = (f32[2,2,40,1024]{3,2,1,0:T(8,128)S(1)}, f32[2,2,40,1024]{3,2,1,0:T(8,128)S(1)}, u32[]{:S(2)}, u32[]{:S(2)}) collective-permute-start(f32[2,2,40,1024]{3,2,1,0:T(8,128)S(1)} %bitcast_add_fusion.7), channel_id=1, source_target_pairs={{0,2},{1,3},{2,0},{3,1},{4,6},{5,7},{6,4},{7,5},{8,10},{9,11},{10,... | collective-permute-start | bytes 1966088 | tf_op jit(solution)/shard_map/ppermute | solution.py:50
  367.8 20.9 %collective-permute-start.14 = (f32[2,2,2,2,40,1024]{5,4,3,2,1,0:T(8,128)}, f32[2,2,2,2,40,1024]{5,4,3,2,1,0:T(8,128)}, u32[]{:S(2)}, u32[]{:S(2)}) collective-permute-start(f32[2,2,2,2,40,1024]{5,4,3,2,1,0:T(8,128)} %bitcast.431), channel_id=1, source_target_pairs={{0,1},{1,0},{2,3},{3,2},{4,5},{5,4},{6,7},{7,6},{8,9},{9,8},{10,11... | collective-permute-start | bytes 7864328 | tf_op jit(solution)/shard_map/ppermute | solution.py:50
  367.9 20.8 %collective-permute-start.15 = (f32[2,2,2,2,40,1024]{5,4,3,2,1,0:T(8,128)}, f32[2,2,2,2,40,1024]{5,4,3,2,1,0:T(8,128)}, u32[]{:S(2)}, u32[]{:S(2)}) collective-permute-start(f32[2,2,2,2,40,1024]{5,4,3,2,1,0:T(8,128)} %bitcast.430), channel_id=1, source_target_pairs={{0,1},{1,0},{2,3},{3,2},{4,5},{5,4},{6,7},{7,6},{8,9},{9,8},{10,11... | collective-permute-start | bytes 7864328 | tf_op jit(solution)/shard_map/ppermute | solution.py:50
  371.9 16.9 %collective-permute-start.16 = (f32[2,80,1024]{2,1,0:T(8,128)S(1)}, f32[2,80,1024]{2,1,0:T(8,128)}, u32[]{:S(2)}, u32[]{:S(2)}) collective-permute-start(f32[2,80,1024]{2,1,0:T(8,128)S(1)} %fusion.13), channel_id=1, source_target_pairs={{0,8},{1,9},{2,10},{3,11},{4,12},{5,13},{6,14},{7,15},{8,0},{9,1},... | collective-permute-start | bytes 1966088 | tf_op jit(solution)/shard_map/ppermute | solution.py:50
  372.6 16.2 %copy-start.6 = (f32[16,40,1024]{2,1,0:T(8,128)S(1)}, f32[16,40,1024]{2,1,0:T(8,128)}, u32[]{:S(2)}) copy-start(f32[16,40,1024]{2,1,0:T(8,128)} %get-tuple-element.258) | copy-start | bytes 7864324
  380.5 10.9 %copy-start.7 = (f32[16,40,1024]{2,1,0:T(8,128)S(1)}, f32[16,40,1024]{2,1,0:T(8,128)}, u32[]{:S(2)}) copy-start(f32[16,40,1024]{2,1,0:T(8,128)} %get-tuple-element.279) | copy-start | bytes 7864324
  394.1 32.2 %collective-permute-start.18 = (f32[2,2,2,40,1024]{4,3,2,1,0:T(8,128)}, f32[2,2,2,40,1024]{4,3,2,1,0:T(8,128)}, u32[]{:S(2)}, u32[]{:S(2)}) collective-permute-start(f32[2,2,2,40,1024]{4,3,2,1,0:T(8,128)} %add_bitcast_fusion), channel_id=1, source_target_pairs={{0,2},{1,3},{2,0},{3,1},{4,6},{5,7},{6,4},{7,5},{8,10},{9,11},{10,... | collective-permute-start | bytes 3932168 | tf_op jit(solution)/shard_map/ppermute | solution.py:50
  395.1 31.2 %collective-permute-start.17 = (f32[2,2,2,40,1024]{4,3,2,1,0:T(8,128)}, f32[2,2,2,40,1024]{4,3,2,1,0:T(8,128)}, u32[]{:S(2)}, u32[]{:S(2)}) collective-permute-start(f32[2,2,2,40,1024]{4,3,2,1,0:T(8,128)} %add_bitcast_fusion.1), channel_id=1, source_target_pairs={{0,4},{1,5},{2,6},{3,7},{4,0},{5,1},{6,2},{7,3},{8,12},{9,13},{10,... | collective-permute-start | bytes 3932168 | tf_op jit(solution)/shard_map/ppermute | solution.py:50
  397.4 27.3 %collective-permute-start.22 = (f32[2,2,2,2,16,256]{5,4,3,2,1,0:T(8,128)}, f32[2,2,2,2,16,256]{5,4,3,2,1,0:T(8,128)}, u32[]{:S(2)}, u32[]{:S(2)}) collective-permute-start(f32[2,2,2,2,16,256]{5,4,3,2,1,0:T(8,128)} %dynamic-slice_bitcast_fusion.2), channel_id=1, source_target_pairs={{0,1},{1,0},{2,3},{3,2},{4,5},{5,4},{6,7},{7,6},{8,9},{9,8},{10,11... | collective-permute-start | bytes 786440 | tf_op jit(solution)/shard_map/ppermute | solution.py:50
  398.6 27.7 %collective-permute-start.19 = (f32[80,1024]{1,0:T(8,128)S(1)}, f32[80,1024]{1,0:T(8,128)S(1)}, u32[]{:S(2)}, u32[]{:S(2)}) collective-permute-start(f32[80,1024]{1,0:T(8,128)S(1)} %dynamic-slice_bitcast_fusion.1), channel_id=1, source_target_pairs={{0,16},{1,17},{2,18},{3,19},{4,20},{5,21},{6,22},{7,23},{8,24},{9,... | collective-permute-start | bytes 983048 | tf_op jit(solution)/shard_map/ppermute | solution.py:50
  426.3 5.4 %copy-start.11 = (f32[80,1024]{1,0:T(8,128)}, f32[80,1024]{1,0:T(8,128)S(1)}, u32[]{:S(2)}) copy-start(f32[80,1024]{1,0:T(8,128)S(1)} %collective-permute-done.19) | copy-start | bytes 983044
  426.4 5.4 %collective-permute-start.20 = (f32[2,2,2,2,16,256]{5,4,3,2,1,0:T(8,128)S(1)}, f32[2,2,2,2,16,256]{5,4,3,2,1,0:T(8,128)S(1)}, u32[]{:S(2)}, u32[]{:S(2)}) collective-permute-start(f32[2,2,2,2,16,256]{5,4,3,2,1,0:T(8,128)S(1)} %dynamic-slice_bitcast_fusion.3), channel_id=1, source_target_pairs={{0,1},{1,0},{2,3},{3,2},{4,5},{5,4},{6,7},{7,6},{8,9},{9,8},{10,11... | collective-permute-start | bytes 786440 | tf_op jit(solution)/shard_map/ppermute | solution.py:50
  431.7 28.3 %copy-start.15 = (f32[2,2,2,2,16,256]{5,4,3,2,1,0:T(8,128)}, f32[2,2,2,2,16,256]{5,4,3,2,1,0:T(8,128)S(1)}, u32[]{:S(2)}) copy-start(f32[2,2,2,2,16,256]{5,4,3,2,1,0:T(8,128)S(1)} %collective-permute-done.20) | copy-start | bytes 786436
  431.8 9.4 %copy-start.17 = (f32[2,2,2,16,256]{4,3,2,1,0:T(8,128)S(1)}, f32[2,2,2,16,256]{4,3,2,1,0:T(8,128)}, u32[]{:S(2)}) copy-start(f32[2,2,2,16,256]{4,3,2,1,0:T(8,128)} %bitcast_add_fusion.10) | copy-start | bytes 393220
  432.9 21.1 %all-to-all-start.5 = ((f32[32,40,128]{2,1,0:T(8,128)}), f32[32,40,128]{2,1,0:T(8,128)S(1)}, u32[]{:S(2)}, u32[]{:S(2)}) async-start(f32[32,40,128]{2,1,0:T(8,128)} %bitcast.177), calls=%async_computation.5 | async-start | bytes 1310720 | tf_op jit(solution)/shard_map/all_to_all | solution.py:203
  436.0 24.0 %collective-permute-start.25 = (f32[2,2,40,1024]{3,2,1,0:T(8,128)}, f32[2,2,40,1024]{3,2,1,0:T(8,128)}, u32[]{:S(2)}, u32[]{:S(2)}) collective-permute-start(f32[2,2,40,1024]{3,2,1,0:T(8,128)} %bitcast_add_fusion.2), channel_id=1, source_target_pairs={{0,4},{1,5},{2,6},{3,7},{4,0},{5,1},{6,2},{7,3},{8,12},{9,13},{10,... | collective-permute-start | bytes 1966088 | tf_op jit(solution)/shard_map/ppermute | solution.py:50
  437.9 22.2 %collective-permute-start.24 = (f32[2,2,40,1024]{3,2,1,0:T(8,128)}, f32[2,2,40,1024]{3,2,1,0:T(8,128)}, u32[]{:S(2)}, u32[]{:S(2)}) collective-permute-start(f32[2,2,40,1024]{3,2,1,0:T(8,128)} %bitcast_add_fusion.3), channel_id=1, source_target_pairs={{0,2},{1,3},{2,0},{3,1},{4,6},{5,7},{6,4},{7,5},{8,10},{9,11},{10,... | collective-permute-start | bytes 1966088 | tf_op jit(solution)/shard_map/ppermute | solution.py:50
  441.3 13.7 %collective-permute-start.23 = (f32[2,2,2,16,256]{4,3,2,1,0:T(8,128)S(1)}, f32[2,2,2,16,256]{4,3,2,1,0:T(8,128)}, u32[]{:S(2)}, u32[]{:S(2)}) collective-permute-start(f32[2,2,2,16,256]{4,3,2,1,0:T(8,128)S(1)} %copy-done.17), channel_id=1, source_target_pairs={{0,8},{1,9},{2,10},{3,11},{4,12},{5,13},{6,14},{7,15},{8,0},{9,1},... | collective-permute-start | bytes 393224 | tf_op jit(solution)/shard_map/ppermute | solution.py:50
  442.7 12.4 %collective-permute-start.21 = (f32[2,2,2,16,256]{4,3,2,1,0:T(8,128)S(1)}, f32[2,2,2,16,256]{4,3,2,1,0:T(8,128)}, u32[]{:S(2)}, u32[]{:S(2)}) collective-permute-start(f32[2,2,2,16,256]{4,3,2,1,0:T(8,128)S(1)} %bitcast_add_fusion.11), channel_id=1, source_target_pairs={{0,8},{1,9},{2,10},{3,11},{4,12},{5,13},{6,14},{7,15},{8,0},{9,1},... | collective-permute-start | bytes 393224 | tf_op jit(solution)/shard_map/ppermute | solution.py:50
  466.6 24.6 %collective-permute-start.26 = (f32[2,80,1024]{2,1,0:T(8,128)}, f32[2,80,1024]{2,1,0:T(8,128)}, u32[]{:S(2)}, u32[]{:S(2)}) collective-permute-start(f32[2,80,1024]{2,1,0:T(8,128)} %fusion.8), channel_id=1, source_target_pairs={{0,8},{1,9},{2,10},{3,11},{4,12},{5,13},{6,14},{7,15},{8,0},{9,1},... | collective-permute-start | bytes 1966088 | tf_op jit(solution)/shard_map/ppermute | solution.py:50
  468.9 22.2 %all-to-all-start.6 = ((f32[32,16,128]{2,1,0:T(8,128)}), f32[32,16,128]{2,1,0:T(8,128)S(1)}, u32[]{:S(2)}, u32[]{:S(2)}) async-start(f32[32,16,128]{2,1,0:T(8,128)} %bitcast.408), calls=%async_computation.6 | async-start | bytes 524288 | tf_op jit(solution)/shard_map/all_to_all | solution.py:203
  475.5 17.0 %collective-permute-start.28 = (f32[2,2,16,256]{3,2,1,0:T(8,128)S(1)}, f32[2,2,16,256]{3,2,1,0:T(8,128)S(1)}, u32[]{:S(2)}, u32[]{:S(2)}) collective-permute-start(f32[2,2,16,256]{3,2,1,0:T(8,128)S(1)} %bitcast_add_fusion.14), channel_id=1, source_target_pairs={{0,16},{1,17},{2,18},{3,19},{4,20},{5,21},{6,22},{7,23},{8,24},{9,... | collective-permute-start | bytes 196616 | tf_op jit(solution)/shard_map/ppermute | solution.py:50
  478.3 14.2 %collective-permute-start.27 = (f32[2,2,16,256]{3,2,1,0:T(8,128)S(1)}, f32[2,2,16,256]{3,2,1,0:T(8,128)S(1)}, u32[]{:S(2)}, u32[]{:S(2)}) collective-permute-start(f32[2,2,16,256]{3,2,1,0:T(8,128)S(1)} %bitcast_add_fusion.12), channel_id=1, source_target_pairs={{0,16},{1,17},{2,18},{3,19},{4,20},{5,21},{6,22},{7,23},{8,24},{9,... | collective-permute-start | bytes 196616 | tf_op jit(solution)/shard_map/ppermute | solution.py:50
  492.5 17.7 %collective-permute-start.33 = (f32[80,1024]{1,0:T(8,128)S(1)}, f32[80,1024]{1,0:T(8,128)S(1)}, u32[]{:S(2)}, u32[]{:S(2)}) collective-permute-start(f32[80,1024]{1,0:T(8,128)S(1)} %dynamic-slice_bitcast_fusion), channel_id=1, source_target_pairs={{0,16},{1,17},{2,18},{3,19},{4,20},{5,21},{6,22},{7,23},{8,24},{9,... | collective-permute-start | bytes 983048 | tf_op jit(solution)/shard_map/ppermute | solution.py:50
  493.8 4.0 collective-permute-start.29
  495.4 4.2 collective-permute-start.31
  497.8 3.8 collective-permute-start.30
  499.6 3.8 collective-permute-start.32
  504.0 23.4 %copy-start.1 = (f32[2,16,512]{2,1,0:T(8,128)S(1)}, f32[2,16,512]{2,1,0:T(8,128)}, u32[]{:S(2)}) copy-start(f32[2,16,512]{2,1,0:T(8,128)} %param.26) | copy-start | bytes 196612
  (3 other events, 4.9 us)
Sparse Core Ops, SparseCore 0:
  11.4 125.9 all-gather.6
  144.3 92.7 all-gather.8
  239.9 76.1 all-gather.10

commit v5 on v4

--- a/solution.py
+++ b/solution.py
@@ -799,30 +799,32 @@
     sum_b = RowSum.of_parts(*parts, pairs)
     key_w = query_key[:, :, WIDTH:]
 
-    def attention_1(grad_film):
-        return attention_back(1, grad_film, attention_whole, key_w, probs, keys)
+    def attentions(grad_film_1, grad_film_0):
+        later = attention_back(1, grad_film_1, attention_whole, key_w, probs, keys)
+        return *later, *attention_back(0, grad_film_0, attention_whole, key_w, probs, keys)
 
     grad_film_0, grad_film_1 = grad_film_0.reshape(1, GATES), grad_film_1.reshape(1, GATES)
-    absorbed_1, query_1, row_1, mixed_1 = beside([sum_b, sum_1], attention_1, grad_film_1)
-
-    def attention_and_frames(grad_film, grad_pre):
-        attention = attention_back(0, grad_film, attention_whole, key_w, probs, keys)
-        return *attention, *layer_back_frames(frame_whole_0, grad_pre, grad_frames, live, 1)
-
-    absorbed_0, query_0, row_0, mixed_0, grad_frames, step_sum_0 = beside(
-        [sum_b, sum_1], attention_and_frames, grad_film_0, grad_pre_0
+    absorbed_1, query_1, row_1, mixed_1, absorbed_0, query_0, row_0, mixed_0 = beside(
+        [sum_b, sum_1], attentions, grad_film_1, grad_film_0
     )
     sum_d = RowSum([by_share(absorbed_0), by_share(absorbed_1)], pairs, far_first=True)
-    sum_d.step()
     query_parts = jnp.stack([query_0, query_1]).reshape(devices, -1)
     first_rows = jnp.concatenate(
         [part.reshape(-1) for part in (row_0, row_1, mixed_0, mixed_1, grad_film_0, grad_film_1)]
     )
-    query_cut, first_rows = beside([sum_d, sum_b], exchange, query_parts, to_all(first_rows, devices))
-    (query_cut,) = sum_d.step(jnp.sum(query_cut, axis=0))
+
+    def frames_and_rows(grad_pre, query_parts, first_rows):
+        came = exchange(query_parts, to_all(first_rows, devices))
+        return *layer_back_frames(frame_whole_0, grad_pre, grad_frames, live, 1), *came
+
+    grad_frames, step_sum_0, query_cut, first_rows = beside(
+        [sum_b, sum_1], frames_and_rows, grad_pre_0, query_parts, first_rows
+    )
+    sum_d.step()
+    query_cut = jnp.sum(query_cut, axis=0)
+    last_rows = jnp.concatenate([part.reshape(-1) for part in (step_sum_0, step_sum_1, query_cut)])
+    (last_rows,) = beside([sum_d, sum_b], exchange, to_all(last_rows, devices))
     sum_b.join()
-    last_rows = jnp.concatenate([part.reshape(-1) for part in (step_sum_0, step_sum_1, query_cut)])
-    (last_rows,) = beside([sum_b], exchange, to_all(last_rows, devices))
     (sum_d.state,) = sum_b.step(sum_d.state)
     while sum_d.at < len(pairs):
         sum_d.step()

time: 540 us -> 537 us (level)
  waiting for transfers between devices: 159 us -> 153 us
    all_to_all x6, waiting for transfers between devices: 50.8 us -> 44.4 us  [exchange(): lax.all_to_all(joined, AXIS, split_axis=0, concat_axis=0, tiled=True)]
  transfers between devices with their start and end apart: 44 -> 44, of which waited for: 20 -> 19; matrix products, arithmetic and copies ran while one was open for 14% -> 14% of each run, Pallas kernels for 34% -> 34%
where the time goes in v5:
time: 537 us; the launch traced here: 531 us
  Pallas kernels  187 us (35%)
  waiting for transfers between devices  153 us (28%)
  starting transfers between devices  67.6 us (13%)
  other arithmetic  50.3 us (9%)
  local copies, waits for them, and re-layouts  33 us (6%)
  between operations  16.8 us (3%)
  matrix products  12.2 us (2%)
  blocking collectives  11.5 us (2%)
    ppermute x34, waiting for transfers between devices, shift(): return lax.ppermute(block, AXIS, perm)  73.8 us
    all_to_all x6, waiting for transfers between devices, exchange(): lax.all_to_all(joined, AXIS, split_axis=0, concat_axis=0, tiled=True)  44.4 us
    pallas_call x2, Pallas kernels, layer_back_weights(): kernel_call(functools.partial(back_weights_kernel, dilation), (GATES // T...  43.1 us
    pallas_call x2, Pallas kernels, layer_gates(): kernel_call(functools.partial(gates_kernel, dilation), (3,), [fixed(count...  41.1 us
    ppermute x34, starting transfers between devices, shift(): return lax.ppermute(block, AXIS, perm)  40.8 us
    pallas_call x2, Pallas kernels, layer_back_frames(): kernel_call(functools.partial(back_frames_kernel, dilation), (2,), [fixed...  35.5 us
    pallas_call x2, Pallas kernels, layer_back_gates(): kernel_call(back_gates_kernel, (2,), [rows, rows, pl.BlockSpec((count //...  27.7 us
    all_to_all x1, waiting for transfers between devices, on_device(): keys = lax.all_to_all(sent, AXIS, split_axis=0, concat_axis=0, tiled=True)  25 us
  transfers between devices with their start and end apart: 44, of which 19 were waited for; matrix products, arithmetic and copies ran while one was open for 14% of the time, Pallas kernels for 34%

profile of v5, /device:TPU:0, one launch (start us, length us, event | category | flops | bytes accessed | tf_op | source)
XLA Modules:
  0.0 531.3 jit_solution(7784070661315288817)
XLA Ops:
  10.1 2.6 copy.95
  13.8 1.6 pad_maximum_fusion.1
  15.5 3.0 collective-permute-start
  18.5 2.6 collective-permute-start.1
  22.4 2.5 collective-permute-done
  25.0 8.4 %collective-permute-done.1 = f32[32,1024]{1,0:T(8,128)S(1)} collective-permute-done((f32[32,1024]{1,0:T(8,128)S(1)}, f32[32,1024]{1,0:T(8,128)S(1)}, u32[]{:S(2)}, u32[]{:S(2)}) %collective-permute-start.1) | collective-permute-done | bytes 131104 | tf_op jit(solution)/shard_map/ppermute | solution.py:50
  35.2 1.6 collective-permute-start.5
  36.8 7.4 %all-to-all-start = ((f32[32,32,512]{2,1,0:T(8,128)}), f32[32,32,512]{2,1,0:T(8,128)S(1)}, u32[]{:S(2)}, u32[]{:S(2)}) async-start(f32[32,32,512]{2,1,0:T(8,128)} %pad_maximum_fusion.1), calls=%async_computation | async-start | bytes 4194304 | tf_op jit(solution)/shard_map/all_to_all | solution.py:692
  45.5 1.8 collective-permute-start.6
  48.9 38.3 %collective-permute-done.6 = f32[2,4,16,1024]{3,2,0,1:T(8,128)S(1)} collective-permute-done((f32[2,4,16,1024]{3,2,0,1:T(8,128)S(1)}, f32[2,4,16,1024]{3,2,0,1:T(8,128)S(1)}, u32[]{:S(2)}, u32[]{:S(2)}) %collective-permute-start.6) | collective-permute-done | bytes 524320 | tf_op jit(solution)/shard_map/ppermute | solution.py:50
  90.6 3.2 collective-permute-done.7
  93.7 2.8 select_bitcast_fusion.1
  97.6 2.0 copy-done.3
  101.2 3.1 copy.103
  104.3 25.0 %all-to-all-done = f32[32,32,512]{2,1,0:T(8,128)S(1)} async-done(((f32[32,32,512]{2,1,0:T(8,128)}), f32[32,32,512]{2,1,0:T(8,128)S(1)}, u32[]{:S(2)}, u32[]{:S(2)}) %all-to-all-start) | async-done | bytes 2097184 | tf_op jit(solution)/shard_map/all_to_all | solution.py:692
  129.8 3.1 fusion
  133.9 2.8 convolution_multiply_fusion
  136.7 3.7 select_reduce_fusion
  140.9 2.1 bitcast_reduce_fusion
  146.0 3.3 all-to-all-start.1
  149.5 12.9 %all-to-all-done.1 = f32[32,16,128]{2,1,0:T(8,128)S(1)} async-done(((f32[32,16,128]{2,1,0:T(8,128)}), f32[32,16,128]{2,1,0:T(8,128)S(1)}, u32[]{:S(2)}, u32[]{:S(2)}) %all-to-all-start.1) | async-done | bytes 262176 | tf_op jit(solution)/shard_map/all_to_all | solution.py:203
  164.8 3.9 all-to-all-start.2
  168.7 8.3 %all-to-all-done.2 = f32[32,8,128]{2,1,0:T(8,128)S(1)} async-done(((f32[32,8,128]{2,1,0:T(8,128)}), f32[32,8,128]{2,1,0:T(8,128)S(1)}, u32[]{:S(2)}, u32[]{:S(2)}) %all-to-all-start.2) | async-done | bytes 131104 | tf_op jit(solution)/shard_map/all_to_all | solution.py:203
  179.0 2.6 all-to-all-start.3
  183.0 8.7 %all-to-all-done.3 = f32[32,8,128]{2,1,0:T(8,128)S(1)} async-done(((f32[32,8,128]{2,1,0:T(8,128)}), f32[32,8,128]{2,1,0:T(8,128)S(1)}, u32[]{:S(2)}, u32[]{:S(2)}) %all-to-all-start.3) | async-done | bytes 131104 | tf_op jit(solution)/shard_map/all_to_all | solution.py:203
  193.3 3.5 all-to-all-start.4
  196.9 21.2 %shard_map.282 = (f32[1024,512]{1,0:T(8,128)}, f32[1024,512]{1,0:T(8,128)}) custom-call(f32[1024,512]{1,0:T(8,128)} %bitcast.356, f32[1024,512]{1,0:T(8,128)} %bitcast.350, f32[32,80,1024]{2,1,0:T(8,128)} %bitcast.332, f32[32,80,1024]{2,1,0:T(8,128)} %bitcast.333, f32[1,512]{1,0:T(1,128)S(1)} %bitcast.316, f32[1024,1]{1,0:T(8,128)S(1)} %fusion.18.live), custom_call_target="tpu_custom_call" | custom-call | flops 2147483648 | bytes 16777216 | tf_op jit(solution)/shard_map/pallas_call | solution.py:459
  219.8 7.8 %shard_map.283 = (f32[1024,512]{1,0:T(8,128)}, f32[1024,512]{1,0:T(8,128)}) custom-call(f32[1024,512]{1,0:T(8,128)} %get-tuple-element.190.tanh, f32[1024,512]{1,0:T(8,128)} %get-tuple-element.191.sig, f32[2,512]{1,0:T(2,128)S(1)} %reshape_squeeze.8.film, f32[32,80,1024]{2,1,0:T(8,128)} %bitcast.334, f32[1024,512]{1,0:T(8,128)} %bitcast.357, ...), custom_call_target="tpu_custom_call" | custom-call | flops 536870912 | bytes 16777216 | tf_op jit(solution)/shard_map/pallas_call | solution.py:489
  227.6 9.5 %all-gather.9.cloned.1.call-done = f32[2560,1024]{1,0:T(8,128)} async-done(((f32[80,1024]{1,0:T(8,128)}), f32[2560,1024]{1,0:T(8,128)}) %all-gather.9.cloned.1.call-update) | async-done | bytes 10485776 | tf_op jit(solution)/shard_map/all_gather | solution.py:729
  237.1 19.9 %shard_map.284 = (f32[1024,512]{1,0:T(8,128)}, f32[1024,512]{1,0:T(8,128)}) custom-call(f32[1024,512]{1,0:T(8,128)} %get-tuple-element.195.frames, f32[1024,512]{1,0:T(8,128)} %bitcast.351, f32[32,80,1024]{2,1,0:T(8,128)} %bitcast.337, f32[32,80,1024]{2,1,0:T(8,128)} %bitcast.338, f32[1,512]{1,0:T(1,128)S(1)} %bitcast.318, f32[1024,1]{1,0:T(8,128)S(1)} %fusion.18.live), custom_call_target="tpu_custom_call" | custom-call | flops 2147483648 | bytes 16777216 | tf_op jit(solution)/shard_map/pallas_call | solution.py:459
  257.0 13.9 %shard_map.285 = (bf16[1024,1024]{1,0:T(8,128)(2,1)}, bf16[1024,1024]{1,0:T(8,128)(2,1)}, f32[2,512]{1,0:T(2,128)S(1)}, f32[512,1024]{1,0:T(8,128)}) custom-call(f32[1024,512]{1,0:T(8,128)} %bitcast.363, f32[1024,512]{1,0:T(8,128)} %bitcast.365, f32[1024,1]{1,0:T(8,128)S(1)} %fusion.18.live, f32[1024,512]{1,0:T(8,128)} %get-tuple-element.208.tanh, ...), custom_call_target="tpu_custom_call" | custom-call | flops 1073741824 | bytes 16777216 | tf_op jit(solution)/shard_map/pallas_call | solution.py:539
  270.9 21.5 %shard_map.286 = (f32[16,40,1024]{2,1,0:T(8,128)}, f32[16,40,1024]{2,1,0:T(8,128)}, f32[16,40,1024]{2,1,0:T(8,128)}, f32[16,40,1024]{2,1,0:T(8,128)}) custom-call(s32[1]{0:T(128)} %bitcast.core, f32[1024,512]{1,0:T(8,128)} %get-tuple-element.195.frames, f32[1024,512]{1,0:T(8,128)} %bitcast.352, f32[1,512]{1,0:T(1,128)S(1)} %bitcast.319, ...), custom_call_target="tpu_custom_call" | custom-call | flops 2147483648 | bytes 16777216 | tf_op jit(solution)/shard_map/pallas_call | solution.py:595
  292.9 8.0 %shard_map.287 = (f32[1024,512]{1,0:T(8,128)}, f32[1024,512]{1,0:T(8,128)}) custom-call(f32[1024,512]{1,0:T(8,128)} %get-tuple-element.208.tanh, f32[1024,512]{1,0:T(8,128)} %get-tuple-element.209.sig, f32[2,512]{1,0:T(2,128)S(1)} %reshape_squeeze.9.film, f32[32,80,1024]{2,1,0:T(8,128)} %bitcast.340, f32[1024,512]{1,0:T(8,128)} %get-tuple-element.195.frames, ...), custom_call_target="tpu_custom_call" | custom-call | flops 536870912 | bytes 16777216 | tf_op jit(solution)/shard_map/pallas_call | solution.py:489
  301.6 2.8 add_bitcast_fusion.3
  304.4 2.7 add_bitcast_fusion.2
  309.7 18.1 %shard_map.288 = (f32[1024,512]{1,0:T(8,128)}, f32[1,512]{1,0:T(1,128)S(1)}) custom-call(bf16[1024,1024]{1,0:T(8,128)(2,1)} %get-tuple-element.227.pre_high, bf16[1024,1024]{1,0:T(8,128)(2,1)} %get-tuple-element.228.pre_low, f32[32,80,1024]{2,1,0:T(8,128)} %bitcast.341, f32[1024,512]{1,0:T(8,128)} %bitcast.364, f32[1024,1]{1,0:T(8,128)S(1)} %fusion.18.live), custom_call_target="tpu_custom_call" | custom-call | flops 1610612736 | bytes 16777216 | tf_op jit(solution)/shard_map/pallas_call | solution.py:636
  327.7 13.8 %shard_map.289 = (bf16[1024,1024]{1,0:T(8,128)(2,1)}, bf16[1024,1024]{1,0:T(8,128)(2,1)}, f32[2,512]{1,0:T(2,128)S(1)}, f32[512,1024]{1,0:T(8,128)}) custom-call(f32[1024,512]{1,0:T(8,128)} %get-tuple-element.298.grad_frames, f32[1024,512]{1,0:T(8,128)} %bitcast.366, f32[1024,1]{1,0:T(8,128)S(1)} %fusion.18.live, f32[1024,512]{1,0:T(8,128)} %get-tuple-element.190.tanh, ...), custom_call_target="tpu_custom_call" | custom-call | flops 1073741824 | bytes 16777216 | tf_op jit(solution)/shard_map/pallas_call | solution.py:539
  343.0 1.6 bitcast_add_fusion.6
  346.2 21.6 %shard_map.290 = (f32[16,40,1024]{2,1,0:T(8,128)}, f32[16,40,1024]{2,1,0:T(8,128)}, f32[16,40,1024]{2,1,0:T(8,128)}, f32[16,40,1024]{2,1,0:T(8,128)}) custom-call(s32[1]{0:T(128)} %bitcast.core, f32[1024,512]{1,0:T(8,128)} %bitcast.358, f32[1024,512]{1,0:T(8,128)} %bitcast.353, f32[1,512]{1,0:T(1,128)S(1)} %bitcast.317, f32[1024,1]{1,0:T(8,128)S(1)} %fusion.18.live, ...), custom_call_target="tpu_custom_call" | custom-call | flops 2147483648 | bytes 16777216 | tf_op jit(solution)/shard_map/pallas_call | solution.py:595
  368.4 1.7 fusion.16
  370.1 1.7 fusion.17
  373.4 7.7 %shard_map.292 = (f32[512,256]{1,0:T(8,128)S(1)}, f32[32,512]{1,0:T(8,128)S(1)}, f32[1,512]{1,0:T(1,128)S(1)}, f32[1,512]{1,0:T(1,128)S(1)}) custom-call(f32[1,1024]{1,0:T(1,128)S(1)} %bitcast.321, f32[32,2,2,16,1024]{4,3,2,1,0:T(8,128)} %bitcast.342, f32[32,2,2,16,1024]{4,3,2,1,0:T(8,128)} %bitcast.343, f32[2,512,512]{2,1,0:T(8,128)} %slice.134.key_w, ...), custom_call_target="tpu_custom_call" | custom-call | flops 335544320 | bytes 16777216 | tf_op jit(solution)/shard_map/pallas_call | solution.py:281
  381.1 7.8 %shard_map.291 = (f32[512,256]{1,0:T(8,128)S(1)}, f32[32,512]{1,0:T(8,128)S(1)}, f32[1,512]{1,0:T(1,128)S(1)}, f32[1,512]{1,0:T(1,128)S(1)}) custom-call(f32[1,1024]{1,0:T(1,128)S(1)} %bitcast.320, f32[32,2,2,16,1024]{4,3,2,1,0:T(8,128)} %bitcast.344, f32[32,2,2,16,1024]{4,3,2,1,0:T(8,128)} %bitcast.345, f32[2,512,512]{2,1,0:T(8,128)} %slice.134.key_w, ...), custom_call_target="tpu_custom_call" | custom-call | flops 335544320 | bytes 16777216 | tf_op jit(solution)/shard_map/pallas_call | solution.py:281
  389.9 3.3 add_bitcast_fusion.1
  393.2 2.6 add_bitcast_fusion
  400.7 2.9 all-to-all-start.5
  405.5 2.8 collective-permute-start.19
  408.9 17.4 %shard_map.293 = (f32[1024,512]{1,0:T(8,128)}, f32[1,512]{1,0:T(1,128)S(1)}) custom-call(bf16[1024,1024]{1,0:T(8,128)(2,1)} %get-tuple-element.296.pre_high, bf16[1024,1024]{1,0:T(8,128)(2,1)} %get-tuple-element.297.pre_low, f32[32,80,1024]{2,1,0:T(8,128)} %bitcast.336, f32[1024,512]{1,0:T(8,128)} %get-tuple-element.298.grad_frames, f32[1024,1]{1,0:T(8,128)S(1)} %fusion.18.live), custom_call_target="tpu_custom_call" | custom-call | flops 1610612736 | bytes 16777216 | tf_op jit(solution)/shard_map/pallas_call | solution.py:636
  428.4 6.5 %all-to-all-done.5 = f32[32,40,128]{2,1,0:T(8,128)S(1)} async-done(((f32[32,40,128]{2,1,0:T(8,128)}), f32[32,40,128]{2,1,0:T(8,128)S(1)}, u32[]{:S(2)}, u32[]{:S(2)}) %all-to-all-start.5) | async-done | bytes 655392 | tf_op jit(solution)/shard_map/all_to_all | solution.py:203
  436.0 2.6 bitcast_add_fusion.2
  438.6 2.6 bitcast_add_fusion.3
  444.5 3.1 all-to-all-start.6
  451.4 1.9 collective-permute-start.23
  454.2 8.0 %all-to-all-done.6 = f32[32,16,128]{2,1,0:T(8,128)S(1)} async-done(((f32[32,16,128]{2,1,0:T(8,128)}), f32[32,16,128]{2,1,0:T(8,128)S(1)}, u32[]{:S(2)}, u32[]{:S(2)}) %all-to-all-start.6) | async-done | bytes 262176 | tf_op jit(solution)/shard_map/all_to_all | solution.py:203
  462.3 1.9 fusion.14
  464.3 1.7 fusion.15
  471.7 1.9 collective-permute-start.29
  474.3 9.2 %collective-permute-done.26 = f32[2,2,16,256]{3,2,1,0:T(8,128)S(1)} collective-permute-done((f32[2,2,16,256]{3,2,1,0:T(8,128)S(1)}, f32[2,2,16,256]{3,2,1,0:T(8,128)S(1)}, u32[]{:S(2)}, u32[]{:S(2)}) %collective-permute-start.26) | collective-permute-done | bytes 65568 | tf_op jit(solution)/shard_map/ppermute | solution.py:50
  492.3 3.4 collective-permute-start.33
  496.4 3.5 shard_map.294
  499.9 7.0 %collective-permute-done.33 = f32[80,1024]{1,0:T(8,128)S(1)} collective-permute-done((f32[80,1024]{1,0:T(8,128)S(1)}, f32[80,1024]{1,0:T(8,128)S(1)}, u32[]{:S(2)}, u32[]{:S(2)}) %collective-permute-start.33) | collective-permute-done | bytes 327712 | tf_op jit(solution)/shard_map/ppermute | solution.py:50
  507.7 2.6 shard_map.295
  510.3 11.5 %all_to_all.40.squares = f32[32,8,128]{2,1,0:T(8,128)} all-to-all(f32[32,8,128]{2,1,0:T(8,128)} %shard_map.295), channel_id=1, replica_groups=mesh['items'=32] {'items'}, dimensions={0} | all-to-all | bytes 262144 | tf_op jit(solution)/shard_map/all_to_all | solution.py:850
  521.8 2.4 shard_map.296
  (261 shorter events, 73.4 us)
Async XLA Ops:
  7.2 137.4 %copy-start = (f32[2,16,512]{2,1,0:T(8,128)S(1)}, f32[2,16,512]{2,1,0:T(8,128)}, u32[]{:S(2)}) copy-start(f32[2,16,512]{2,1,0:T(8,128)} %param.26) | copy-start | bytes 196612
  7.2 136.9 %all-gather.7.cloned.1.call-start = ((), (), s32[]{:S(2)}) async-start(), calls=%async_computation.8 | async-start | bytes 10813440 | tf_op jit(solution)/shard_map/all_gather | solution.py:680
  10.0 3.4 copy-start.26
  10.0 3.8 copy-start.20
  10.0 3.8 copy-start.25
  15.5 9.5 %collective-permute-start = (f32[32,1024]{1,0:T(8,128)S(1)}, f32[32,1024]{1,0:T(8,128)S(1)}, u32[]{:S(2)}, u32[]{:S(2)}) collective-permute-start(f32[32,1024]{1,0:T(8,128)S(1)} %bitcast.403), channel_id=1, source_target_pairs={{0,8},{1,9},{2,10},{3,11},{4,12},{5,13},{6,14},{7,15},{8,16},{9,17... | collective-permute-start | bytes 393224 | tf_op jit(solution)/shard_map/ppermute | solution.py:50
  18.5 14.9 %collective-permute-start.1 = (f32[32,1024]{1,0:T(8,128)S(1)}, f32[32,1024]{1,0:T(8,128)S(1)}, u32[]{:S(2)}, u32[]{:S(2)}) collective-permute-start(f32[32,1024]{1,0:T(8,128)S(1)} %bitcast.404), channel_id=1, source_target_pairs={{0,16},{1,17},{2,18},{3,19},{4,20},{5,21},{6,22},{7,23},{8,24},{9,... | collective-permute-start | bytes 393224 | tf_op jit(solution)/shard_map/ppermute | solution.py:50
  21.1 12.6 %collective-permute-start.2 = (f32[32,1024]{1,0:T(8,128)S(1)}, f32[32,1024]{1,0:T(8,128)S(1)}, u32[]{:S(2)}, u32[]{:S(2)}) collective-permute-start(f32[32,1024]{1,0:T(8,128)S(1)} %bitcast.405), channel_id=1, source_target_pairs={{0,24},{1,25},{2,26},{3,27},{4,28},{5,29},{6,30},{7,31},{8,0},{9,1... | collective-permute-start | bytes 393224 | tf_op jit(solution)/shard_map/ppermute | solution.py:50
  33.8 10.6 %collective-permute-start.3 = (f32[4,16,1024]{2,1,0:T(8,128)S(1)}, f32[4,16,1024]{2,1,0:T(8,128)}, u32[]{:S(2)}, u32[]{:S(2)}) collective-permute-start(f32[4,16,1024]{2,1,0:T(8,128)S(1)} %get-tuple-element.367), channel_id=1, source_target_pairs={{0,2},{1,3},{2,0},{3,1},{4,6},{5,7},{6,4},{7,5},{8,10},{9,11},{10,... | collective-permute-start | bytes 786440 | tf_op jit(solution)/shard_map/ppermute | solution.py:50
  35.2 9.1 %collective-permute-start.5 = (f32[4,16,1024]{2,1,0:T(8,128)S(1)}, f32[4,16,1024]{2,1,0:T(8,128)}, u32[]{:S(2)}, u32[]{:S(2)}) collective-permute-start(f32[4,16,1024]{2,1,0:T(8,128)S(1)} %get-tuple-element.368), channel_id=1, source_target_pairs={{0,4},{1,5},{2,6},{3,7},{4,0},{5,1},{6,2},{7,3},{8,12},{9,13},{10,... | collective-permute-start | bytes 786440 | tf_op jit(solution)/shard_map/ppermute | solution.py:50
  36.8 92.5 %all-to-all-start = ((f32[32,32,512]{2,1,0:T(8,128)}), f32[32,32,512]{2,1,0:T(8,128)S(1)}, u32[]{:S(2)}, u32[]{:S(2)}) async-start(f32[32,32,512]{2,1,0:T(8,128)} %pad_maximum_fusion.1), calls=%async_computation | async-start | bytes 4194304 | tf_op jit(solution)/shard_map/all_to_all | solution.py:692
  44.2 192.9 %all-gather.9.cloned.1.call-start = ((), (), s32[]{:S(2)}) async-start(), calls=%async_computation.9 | async-start | bytes 10813440 | tf_op jit(solution)/shard_map/all_gather | solution.py:729
  45.5 41.8 %collective-permute-start.6 = (f32[2,4,16,1024]{3,2,0,1:T(8,128)S(1)}, f32[2,4,16,1024]{3,2,0,1:T(8,128)S(1)}, u32[]{:S(2)}, u32[]{:S(2)}) collective-permute-start(f32[2,4,16,1024]{3,2,0,1:T(8,128)S(1)} %pad_maximum_fusion.4), channel_id=1, source_target_pairs={{0,2},{1,3},{2,0},{3,1},{4,6},{5,7},{6,4},{7,5},{8,10},{9,11},{10,... | collective-permute-start | bytes 1572872 | tf_op jit(solution)/shard_map/ppermute | solution.py:50
  47.4 40.1 %collective-permute-start.4 = (f32[2,4,16,1024]{3,2,1,0:T(8,128)S(1)}, f32[2,4,16,1024]{3,2,1,0:T(8,128)S(1)}, u32[]{:S(2)}, u32[]{:S(2)}) collective-permute-start(f32[2,4,16,1024]{3,2,1,0:T(8,128)S(1)} %pad_maximum_fusion.3), channel_id=1, source_target_pairs={{0,4},{1,5},{2,6},{3,7},{4,0},{5,1},{6,2},{7,3},{8,12},{9,13},{10,... | collective-permute-start | bytes 1572872 | tf_op jit(solution)/shard_map/ppermute | solution.py:50
  89.2 4.5 collective-permute-start.7
  129.3 13.7 %copy-start.2 = (f32[32,32,512]{2,1,0:T(8,128)}, f32[32,32,512]{2,1,0:T(8,128)S(1)}, u32[]{:S(2)}) copy-start(f32[32,32,512]{2,1,0:T(8,128)S(1)} %all-to-all-done) | copy-start | bytes 6291460
  144.1 5.3 copy-start.18
  144.6 18.6 %copy-start.21 = (f32[32,16]{1,0:T(8,128)}, f32[32,16]{1,0:T(8,128)S(1)}, u32[]{:S(2)}) copy-start(f32[32,16]{1,0:T(8,128)S(1)} %fusion.34.embeds) | copy-start | bytes 6148
  146.0 16.4 %all-to-all-start.1 = ((f32[32,16,128]{2,1,0:T(8,128)}), f32[32,16,128]{2,1,0:T(8,128)S(1)}, u32[]{:S(2)}, u32[]{:S(2)}) async-start(f32[32,16,128]{2,1,0:T(8,128)} %bitcast.159), calls=%async_computation.1 | async-start | bytes 524288 | tf_op jit(solution)/shard_map/all_to_all | solution.py:203
  149.4 19.4 %copy-start.19 = (f32[2,16,512]{2,1,0:T(8,128)S(1)}, f32[2,16,512]{2,1,0:T(8,128)}, u32[]{:S(2)}) copy-start(f32[2,16,512]{2,1,0:T(8,128)} %param.34) | copy-start | bytes 196612
  164.0 17.6 %copy-start.11 = (f32[2,16,1024]{2,1,0:T(8,128)S(1)}, f32[2,16,1024]{2,1,0:T(8,128)}, u32[]{:S(2)}) copy-start(f32[2,16,1024]{2,1,0:T(8,128)} %param.35) | copy-start | bytes 393220
  164.8 12.2 %all-to-all-start.2 = ((f32[32,8,128]{2,1,0:T(8,128)}), f32[32,8,128]{2,1,0:T(8,128)S(1)}, u32[]{:S(2)}, u32[]{:S(2)}) async-start(f32[32,8,128]{2,1,0:T(8,128)} %copy.112), calls=%async_computation.2 | async-start | bytes 262144 | tf_op jit(solution)/shard_map/all_to_all | solution.py:203
  179.0 12.7 %all-to-all-start.3 = ((f32[32,8,128]{2,1,0:T(8,128)}), f32[32,8,128]{2,1,0:T(8,128)S(1)}, u32[]{:S(2)}, u32[]{:S(2)}) async-start(f32[32,8,128]{2,1,0:T(8,128)} %copy.116), calls=%async_computation.3 | async-start | bytes 262144 | tf_op jit(solution)/shard_map/all_to_all | solution.py:203
  193.3 24.8 %all-to-all-start.4 = ((f32[32,16,128]{2,1,0:T(8,128)}), f32[32,16,128]{2,1,0:T(8,128)S(1)}, u32[]{:S(2)}, u32[]{:S(2)}) async-start(f32[32,16,128]{2,1,0:T(8,128)} %reshape.326), calls=%async_computation.4 | async-start | bytes 524288 | tf_op jit(solution)/shard_map/all_to_all | solution.py:203
  196.8 176.5 %all-gather.11.cloned.1.call-start = ((), (), s32[]{:S(2)}) async-start(), calls=%async_computation.10 | async-start | bytes 8650752 | tf_op jit(solution)/shard_map/all_gather | solution.py:763
  292.4 8.5 %collective-permute-start.8 = (f32[2,2,2,2,40,1024]{5,4,3,2,1,0:T(8,128)}, f32[2,2,2,2,40,1024]{5,4,3,2,1,0:T(8,128)}, u32[]{:S(2)}, u32[]{:S(2)}) collective-permute-start(f32[2,2,2,2,40,1024]{5,4,3,2,1,0:T(8,128)} %bitcast.418), channel_id=1, source_target_pairs={{0,1},{1,0},{2,3},{3,2},{4,5},{5,4},{6,7},{7,6},{8,9},{9,8},{10,11... | collective-permute-start | bytes 7864328 | tf_op jit(solution)/shard_map/ppermute | solution.py:50
  292.7 8.9 %collective-permute-start.9 = (f32[2,2,2,2,40,1024]{5,4,3,2,1,0:T(8,128)}, f32[2,2,2,2,40,1024]{5,4,3,2,1,0:T(8,128)}, u32[]{:S(2)}, u32[]{:S(2)}) collective-permute-start(f32[2,2,2,2,40,1024]{5,4,3,2,1,0:T(8,128)} %bitcast.417), channel_id=1, source_target_pairs={{0,1},{1,0},{2,3},{3,2},{4,5},{5,4},{6,7},{7,6},{8,9},{9,8},{10,11... | collective-permute-start | bytes 7864328 | tf_op jit(solution)/shard_map/ppermute | solution.py:50
  292.9 8.6 %copy-start.7 = (f32[16,40,1024]{2,1,0:T(8,128)S(1)}, f32[16,40,1024]{2,1,0:T(8,128)}, u32[]{:S(2)}) copy-start(f32[16,40,1024]{2,1,0:T(8,128)} %get-tuple-element.217) | copy-start | bytes 7864324
  300.9 3.4 copy-start.8
  307.1 34.5 %collective-permute-start.11 = (f32[2,2,2,40,1024]{4,3,2,1,0:T(8,128)}, f32[2,2,2,40,1024]{4,3,2,1,0:T(8,128)}, u32[]{:S(2)}, u32[]{:S(2)}) collective-permute-start(f32[2,2,2,40,1024]{4,3,2,1,0:T(8,128)} %add_bitcast_fusion.2), channel_id=1, source_target_pairs={{0,2},{1,3},{2,0},{3,1},{4,6},{5,7},{6,4},{7,5},{8,10},{9,11},{10,... | collective-permute-start | bytes 3932168 | tf_op jit(solution)/shard_map/ppermute | solution.py:50
  308.2 33.3 %collective-permute-start.10 = (f32[2,2,2,40,1024]{4,3,2,1,0:T(8,128)}, f32[2,2,2,40,1024]{4,3,2,1,0:T(8,128)}, u32[]{:S(2)}, u32[]{:S(2)}) collective-permute-start(f32[2,2,2,40,1024]{4,3,2,1,0:T(8,128)} %add_bitcast_fusion.3), channel_id=1, source_target_pairs={{0,4},{1,5},{2,6},{3,7},{4,0},{5,1},{6,2},{7,3},{8,12},{9,13},{10,... | collective-permute-start | bytes 3932168 | tf_op jit(solution)/shard_map/ppermute | solution.py:50
  344.6 23.2 %collective-permute-start.13 = (f32[2,2,40,1024]{3,2,1,0:T(8,128)S(1)}, f32[2,2,40,1024]{3,2,1,0:T(8,128)S(1)}, u32[]{:S(2)}, u32[]{:S(2)}) collective-permute-start(f32[2,2,40,1024]{3,2,1,0:T(8,128)S(1)} %bitcast_add_fusion.6), channel_id=1, source_target_pairs={{0,4},{1,5},{2,6},{3,7},{4,0},{5,1},{6,2},{7,3},{8,12},{9,13},{10,... | collective-permute-start | bytes 1966088 | tf_op jit(solution)/shard_map/ppermute | solution.py:50
  345.2 22.6 %collective-permute-start.12 = (f32[2,2,40,1024]{3,2,1,0:T(8,128)S(1)}, f32[2,2,40,1024]{3,2,1,0:T(8,128)S(1)}, u32[]{:S(2)}, u32[]{:S(2)}) collective-permute-start(f32[2,2,40,1024]{3,2,1,0:T(8,128)S(1)} %bitcast_add_fusion.7), channel_id=1, source_target_pairs={{0,2},{1,3},{2,0},{3,1},{4,6},{5,7},{6,4},{7,5},{8,10},{9,11},{10,... | collective-permute-start | bytes 1966088 | tf_op jit(solution)/shard_map/ppermute | solution.py:50
  367.8 21.9 %collective-permute-start.14 = (f32[2,2,2,2,40,1024]{5,4,3,2,1,0:T(8,128)}, f32[2,2,2,2,40,1024]{5,4,3,2,1,0:T(8,128)}, u32[]{:S(2)}, u32[]{:S(2)}) collective-permute-start(f32[2,2,2,2,40,1024]{5,4,3,2,1,0:T(8,128)} %bitcast.416), channel_id=1, source_target_pairs={{0,1},{1,0},{2,3},{3,2},{4,5},{5,4},{6,7},{7,6},{8,9},{9,8},{10,11... | collective-permute-start | bytes 7864328 | tf_op jit(solution)/shard_map/ppermute | solution.py:50
  367.9 21.8 %collective-permute-start.15 = (f32[2,2,2,2,40,1024]{5,4,3,2,1,0:T(8,128)}, f32[2,2,2,2,40,1024]{5,4,3,2,1,0:T(8,128)}, u32[]{:S(2)}, u32[]{:S(2)}) collective-permute-start(f32[2,2,2,2,40,1024]{5,4,3,2,1,0:T(8,128)} %bitcast.415), channel_id=1, source_target_pairs={{0,1},{1,0},{2,3},{3,2},{4,5},{5,4},{6,7},{7,6},{8,9},{9,8},{10,11... | collective-permute-start | bytes 7864328 | tf_op jit(solution)/shard_map/ppermute | solution.py:50
  372.7 17.0 %collective-permute-start.16 = (f32[2,80,1024]{2,1,0:T(8,128)}, f32[2,80,1024]{2,1,0:T(8,128)}, u32[]{:S(2)}, u32[]{:S(2)}) collective-permute-start(f32[2,80,1024]{2,1,0:T(8,128)} %fusion.13), channel_id=1, source_target_pairs={{0,8},{1,9},{2,10},{3,11},{4,12},{5,13},{6,14},{7,15},{8,0},{9,1},... | collective-permute-start | bytes 1966088 | tf_op jit(solution)/shard_map/ppermute | solution.py:50
  389.8 3.4 copy-start.6
  397.0 3.7 copy-start.9
  397.0 39.0 %collective-permute-start.18 = (f32[2,2,2,40,1024]{4,3,2,1,0:T(8,128)}, f32[2,2,2,40,1024]{4,3,2,1,0:T(8,128)}, u32[]{:S(2)}, u32[]{:S(2)}) collective-permute-start(f32[2,2,2,40,1024]{4,3,2,1,0:T(8,128)} %add_bitcast_fusion), channel_id=1, source_target_pairs={{0,2},{1,3},{2,0},{3,1},{4,6},{5,7},{6,4},{7,5},{8,10},{9,11},{10,... | collective-permute-start | bytes 3932168 | tf_op jit(solution)/shard_map/ppermute | solution.py:50
  398.1 37.9 %collective-permute-start.17 = (f32[2,2,2,40,1024]{4,3,2,1,0:T(8,128)}, f32[2,2,2,40,1024]{4,3,2,1,0:T(8,128)}, u32[]{:S(2)}, u32[]{:S(2)}) collective-permute-start(f32[2,2,2,40,1024]{4,3,2,1,0:T(8,128)} %add_bitcast_fusion.1), channel_id=1, source_target_pairs={{0,4},{1,5},{2,6},{3,7},{4,0},{5,1},{6,2},{7,3},{8,12},{9,13},{10,... | collective-permute-start | bytes 3932168 | tf_op jit(solution)/shard_map/ppermute | solution.py:50
  400.7 34.3 %all-to-all-start.5 = ((f32[32,40,128]{2,1,0:T(8,128)}), f32[32,40,128]{2,1,0:T(8,128)S(1)}, u32[]{:S(2)}, u32[]{:S(2)}) async-start(f32[32,40,128]{2,1,0:T(8,128)} %bitcast.173), calls=%async_computation.5 | async-start | bytes 1310720 | tf_op jit(solution)/shard_map/all_to_all | solution.py:203
  405.5 30.5 %collective-permute-start.19 = (f32[80,1024]{1,0:T(8,128)S(1)}, f32[80,1024]{1,0:T(8,128)S(1)}, u32[]{:S(2)}, u32[]{:S(2)}) collective-permute-start(f32[80,1024]{1,0:T(8,128)S(1)} %dynamic-slice_bitcast_fusion.1), channel_id=1, source_target_pairs={{0,16},{1,17},{2,18},{3,19},{4,20},{5,21},{6,22},{7,23},{8,24},{9,... | collective-permute-start | bytes 983048 | tf_op jit(solution)/shard_map/ppermute | solution.py:50
  408.3 18.1 %collective-permute-start.22 = (f32[2,2,2,2,16,256]{5,4,3,2,1,0:T(8,128)S(1)}, f32[2,2,2,2,16,256]{5,4,3,2,1,0:T(8,128)S(1)}, u32[]{:S(2)}, u32[]{:S(2)}) collective-permute-start(f32[2,2,2,2,16,256]{5,4,3,2,1,0:T(8,128)S(1)} %dynamic-slice_bitcast_fusion.2), channel_id=1, source_target_pairs={{0,1},{1,0},{2,3},{3,2},{4,5},{5,4},{6,7},{7,6},{8,9},{9,8},{10,11... | collective-permute-start | bytes 786440 | tf_op jit(solution)/shard_map/ppermute | solution.py:50
  408.4 18.0 %collective-permute-start.20 = (f32[2,2,2,2,16,256]{5,4,3,2,1,0:T(8,128)S(1)}, f32[2,2,2,2,16,256]{5,4,3,2,1,0:T(8,128)S(1)}, u32[]{:S(2)}, u32[]{:S(2)}) collective-permute-start(f32[2,2,2,2,16,256]{5,4,3,2,1,0:T(8,128)S(1)} %dynamic-slice_bitcast_fusion.3), channel_id=1, source_target_pairs={{0,1},{1,0},{2,3},{3,2},{4,5},{5,4},{6,7},{7,6},{8,9},{9,8},{10,11... | collective-permute-start | bytes 786440 | tf_op jit(solution)/shard_map/ppermute | solution.py:50
  436.0 5.2 copy-start.14
  438.6 14.9 %copy-start.10 = (f32[2,80,1024]{2,1,0:T(8,128)S(1)}, f32[2,80,1024]{2,1,0:T(8,128)}, u32[]{:S(2)}) copy-start(f32[2,80,1024]{2,1,0:T(8,128)} %copy-done.9) | copy-start | bytes 1966084
  441.2 12.2 %copy-start.15 = (f32[80,1024]{1,0:T(8,128)S(1)}, f32[80,1024]{1,0:T(8,128)}, u32[]{:S(2)}) copy-start(f32[80,1024]{1,0:T(8,128)} %copy-done.14) | copy-start | bytes 983044
  441.3 21.0 %collective-permute-start.25 = (f32[2,2,40,1024]{3,2,1,0:T(8,128)}, f32[2,2,40,1024]{3,2,1,0:T(8,128)}, u32[]{:S(2)}, u32[]{:S(2)}) collective-permute-start(f32[2,2,40,1024]{3,2,1,0:T(8,128)} %bitcast_add_fusion.2), channel_id=1, source_target_pairs={{0,4},{1,5},{2,6},{3,7},{4,0},{5,1},{6,2},{7,3},{8,12},{9,13},{10,... | collective-permute-start | bytes 1966088 | tf_op jit(solution)/shard_map/ppermute | solution.py:50
  442.7 19.6 %collective-permute-start.24 = (f32[2,2,40,1024]{3,2,1,0:T(8,128)}, f32[2,2,40,1024]{3,2,1,0:T(8,128)S(1)}, u32[]{:S(2)}, u32[]{:S(2)}) collective-permute-start(f32[2,2,40,1024]{3,2,1,0:T(8,128)} %bitcast_add_fusion.3), channel_id=1, source_target_pairs={{0,2},{1,3},{2,0},{3,1},{4,6},{5,7},{6,4},{7,5},{8,10},{9,11},{10,... | collective-permute-start | bytes 1966088 | tf_op jit(solution)/shard_map/ppermute | solution.py:50
  444.5 17.7 %all-to-all-start.6 = ((f32[32,16,128]{2,1,0:T(8,128)}), f32[32,16,128]{2,1,0:T(8,128)S(1)}, u32[]{:S(2)}, u32[]{:S(2)}) async-start(f32[32,16,128]{2,1,0:T(8,128)} %bitcast.177), calls=%async_computation.6 | async-start | bytes 524288 | tf_op jit(solution)/shard_map/all_to_all | solution.py:203
  451.4 10.9 %collective-permute-start.23 = (f32[2,2,2,16,256]{4,3,2,1,0:T(8,128)S(1)}, f32[2,2,2,16,256]{4,3,2,1,0:T(8,128)S(1)}, u32[]{:S(2)}, u32[]{:S(2)}) collective-permute-start(f32[2,2,2,16,256]{4,3,2,1,0:T(8,128)S(1)} %bitcast_add_fusion.10), channel_id=1, source_target_pairs={{0,8},{1,9},{2,10},{3,11},{4,12},{5,13},{6,14},{7,15},{8,0},{9,1},... | collective-permute-start | bytes 393224 | tf_op jit(solution)/shard_map/ppermute | solution.py:50
  453.3 9.0 %collective-permute-start.21 = (f32[2,2,2,16,256]{4,3,2,1,0:T(8,128)}, f32[2,2,2,16,256]{4,3,2,1,0:T(8,128)S(1)}, u32[]{:S(2)}, u32[]{:S(2)}) collective-permute-start(f32[2,2,2,16,256]{4,3,2,1,0:T(8,128)} %bitcast_add_fusion.11), channel_id=1, source_target_pairs={{0,8},{1,9},{2,10},{3,11},{4,12},{5,13},{6,14},{7,15},{8,0},{9,1},... | collective-permute-start | bytes 393224 | tf_op jit(solution)/shard_map/ppermute | solution.py:50
  462.3 3.7 copy-start.22
  462.3 3.7 copy-start.23
  466.0 4.8 copy-start.12
  466.1 26.1 %collective-permute-start.32 = (f32[2,80,1024]{2,1,0:T(8,128)S(1)}, f32[2,80,1024]{2,1,0:T(8,128)S(1)}, u32[]{:S(2)}, u32[]{:S(2)}) collective-permute-start(f32[2,80,1024]{2,1,0:T(8,128)S(1)} %fusion.8), channel_id=1, source_target_pairs={{0,8},{1,9},{2,10},{3,11},{4,12},{5,13},{6,14},{7,15},{8,0},{9,1},... | collective-permute-start | bytes 1966088 | tf_op jit(solution)/shard_map/ppermute | solution.py:50
  469.7 13.8 %collective-permute-start.26 = (f32[2,2,16,256]{3,2,1,0:T(8,128)S(1)}, f32[2,2,16,256]{3,2,1,0:T(8,128)S(1)}, u32[]{:S(2)}, u32[]{:S(2)}) collective-permute-start(f32[2,2,16,256]{3,2,1,0:T(8,128)S(1)} %add_bitcast_fusion.5), channel_id=1, source_target_pairs={{0,16},{1,17},{2,18},{3,19},{4,20},{5,21},{6,22},{7,23},{8,24},{9,... | collective-permute-start | bytes 196616 | tf_op jit(solution)/shard_map/ppermute | solution.py:50
  471.7 14.2 %collective-permute-start.29 = (f32[2,2,16,256]{3,2,1,0:T(8,128)S(1)}, f32[2,2,16,256]{3,2,1,0:T(8,128)S(1)}, u32[]{:S(2)}, u32[]{:S(2)}) collective-permute-start(f32[2,2,16,256]{3,2,1,0:T(8,128)S(1)} %add_bitcast_fusion.4), channel_id=1, source_target_pairs={{0,16},{1,17},{2,18},{3,19},{4,20},{5,21},{6,22},{7,23},{8,24},{9,... | collective-permute-start | bytes 196616 | tf_op jit(solution)/shard_map/ppermute | solution.py:50
  484.4 4.0 collective-permute-start.27
  486.8 4.0 collective-permute-start.30
  488.4 3.8 collective-permute-start.28
  490.8 5.0 collective-permute-start.31
  492.3 14.6 %collective-permute-start.33 = (f32[80,1024]{1,0:T(8,128)S(1)}, f32[80,1024]{1,0:T(8,128)S(1)}, u32[]{:S(2)}, u32[]{:S(2)}) collective-permute-start(f32[80,1024]{1,0:T(8,128)S(1)} %dynamic-slice_bitcast_fusion), channel_id=1, source_target_pairs={{0,16},{1,17},{2,18},{3,19},{4,20},{5,21},{6,22},{7,23},{8,24},{9,... | collective-permute-start | bytes 983048 | tf_op jit(solution)/shard_map/ppermute | solution.py:50
  496.4 27.8 %copy-start.1 = (f32[2,16,512]{2,1,0:T(8,128)S(1)}, f32[2,16,512]{2,1,0:T(8,128)}, u32[]{:S(2)}) copy-start(f32[2,16,512]{2,1,0:T(8,128)} %param.26) | copy-start | bytes 196612
  (9 other events, 17.1 us)
Sparse Core Ops, SparseCore 0:
  11.4 125.9 all-gather.6
  144.3 92.7 all-gather.8
  239.9 76.1 all-gather.10
